TPU v7x, 32 devices: a whole 2x2x4 slice. The times are simulated.
32 devices in a mesh: lat: 4 (over y, x), lev: 8 (over z, core).
Axes of the slice: x: 2, y: 2, z: 4, core: 2. Of those that a mesh axis runs over, the one named last changes fastest.
Arguments:
- grid_gradient: float32 [64, 640, 1280], P('lev', 'lat'), may hold values from -0.4375 to 0.4375
- legendre: bfloat16 [640, 640, 320], P('lat', 'lev'), may hold values from -0.15625 to 0.15625
- assign: int32 [640], replicated, may hold values from 0 to 639, as said below
Outputs:
- coeff_gradient: bfloat16 [640, 640, 128], P('lat', 'lev')
Inputs may be any that keep to these rules, and one draw needn't show every extreme that they name: `assign`: each wavenumber appears once; slots 2q and 2q + 1 hold two wavenumbers that sum to 639.
All inputs are finite; a program needn't handle non-finite values.
Results may differ from a plain program's by a relative error of at most 0.0059.
Values may be sent and summed in bfloat16 or wider, within the bound.
No kernel may reach another device: no remote copies, remote signals or barrier semaphores. Data moves between devices by JAX's collectives and lax.ppermute only.
A program may use at most 128 MiB of HBM per device.

v0:
```python
import math

import jax
import jax.numpy as jnp
from jax import lax
from jax.sharding import PartitionSpec as P


def split_halves(arrived, half):
    north = arrived[..., :half].astype(jnp.float32)
    south = arrived[..., ::-1][..., :half].astype(jnp.float32)
    return ((north + south).astype(jnp.bfloat16), (north - south).astype(jnp.bfloat16))


def per_device(grid_gradient, legendre, assign):
    fl_dev, rows, nlon = grid_gradient.shape
    modes = nlon // 2
    slots_dev, deg_dev, half = legendre.shape
    lat_id = lax.axis_index("lat")
    lev_id = lax.axis_index("lev")
    longitudes = jnp.arange(nlon, dtype=jnp.int32)
    phase = longitudes[:, None] * assign[None, :] % nlon
    angle = phase.astype(jnp.float32) * (2.0 * math.pi / nlon)
    weight = jnp.where(assign == 0, 1.0, 2.0).astype(jnp.float32)
    table = jnp.stack([jnp.cos(angle) * weight, -jnp.sin(angle) * weight], axis=1)
    spec = jnp.einsum(
        "lcs,frl->sfcr",
        table,
        grid_gradient,
        precision=lax.Precision.HIGHEST,
        preferred_element_type=jnp.float32,
    ).astype(jnp.bfloat16)
    arrived = lax.all_to_all(spec, "lat", split_axis=0, concat_axis=3, tiled=True)
    mine = lax.dynamic_slice(assign, (lat_id * slots_dev,), (slots_dev,))
    paired = legendre.reshape(slots_dev, deg_dev // 2, 2, half)
    piece = lax.all_gather(arrived, "lev", axis=1, tiled=True)
    even, odd = split_halves(piece, half)
    from_even = jnp.einsum(
        "str,sfcr->stcf", paired[:, :, 0], even, preferred_element_type=jnp.float32
    )
    from_odd = jnp.einsum(
        "str,sfcr->stcf", paired[:, :, 1], odd, preferred_element_type=jnp.float32
    )
    both = jnp.stack([from_even, from_odd], axis=2)
    columns = both.reshape(slots_dev, deg_dev, 2, piece.shape[1])
    degrees = lev_id * deg_dev + jnp.arange(deg_dev, dtype=jnp.int32)
    valid = degrees[None, :] < (modes - mine)[:, None]
    result = jnp.where(valid[:, :, None, None], columns, 0.0).astype(jnp.bfloat16)
    return result.reshape(slots_dev, deg_dev, result.shape[2] * result.shape[3])


def solution(mesh):
    in_specs = (P("lev", "lat", None), P("lat", "lev", None), P())
    out_specs = P("lat", "lev", None)
    return jax.shard_map(
        per_device, mesh=mesh, in_specs=in_specs, out_specs=out_specs, check_vma=False
    )
```

profile of v0, /device:TPU:0, one launch (start us, length us, event | category | flops | bytes accessed | tf_op | source)
XLA Modules:
  0.0 492.4 jit_solution(12443085402093244559)
XLA Ops:
  6.5 0.0 all-gather.2.cloned.1.call-start
  6.5 0.0 copy-start
  6.5 0.8 compare_select_fusion
  7.4 14.3 %cosine_multiply_fusion = (f32[1280,1,640]{2,0,1:T(8,128)S(1)}, f32[1280,1,640]{2,0,1:T(8,128)S(1)}) fusion(f32[640]{0:T(1024)S(1)} %compare_select_fusion, s32[640]{0:T(1024)} %param.5), kind=kLoop, calls=%fused_computation.22 | loop fusion | flops 9830400 | bytes 6558720 | tf_op jit(solution)/shard_map/mul | solution.py:25
  21.7 0.0 copy-done
  21.7 28.2 %convert_bitcast_fusion = bf16[640,8,2,160]{0,3,1,2:T(8,128)(2,1)S(1)} fusion(f32[8,160,1280]{2,1,0:T(8,128)S(1)} %copy-done, f32[1280,1,640]{2,0,1:T(8,128)S(1)} %get-tuple-element.8, f32[1280,1,640]{2,0,1:T(8,128)S(1)} %get-tuple-element.7), kind=kOutput, calls=%fused_computation.20 | convolution fusion | flops 25169100800 | bytes 16384000 | tf_op jit(solution)/shard_map/lcs,frl->sfcr/dot_general | solution.py:26
  49.9 6.5 %copy.18 = bf16[640,8,2,160]{3,1,2,0:T(8,128)(2,1)} copy(bf16[640,8,2,160]{0,3,1,2:T(8,128)(2,1)S(1)} %convert_bitcast_fusion) | data formatting | bytes 6553600 | tf_op jit(solution)/shard_map/convert_element_type | solution.py:32
  56.4 64.5 %all_to_all.18 = bf16[640,8,2,160]{3,1,2,0:T(8,128)(2,1)S(1)} all-to-all(bf16[640,8,2,160]{3,1,2,0:T(8,128)(2,1)} %copy.18), channel_id=1, replica_groups=mesh['lat'=4,'lev'=8] {'lat'}, dimensions={0} | all-to-all | bytes 6553600 | tf_op jit(solution)/shard_map/all_to_all | solution.py:33
  120.9 9.0 %copy.19 = bf16[160,8,2,4,160]{4,3,1,2,0:T(4,128)(2,1)} copy(bf16[160,8,2,4,160]{4,1,2,0,3:T(8,128)(2,1)S(1)} %bitcast.48) | data formatting | bytes 6553600 | tf_op jit(solution)/shard_map/all_to_all | solution.py:33
  129.9 8.2 %all_to_all.16 = bf16[160,8,2,640]{3,1,2,0:T(8,128)(2,1)} reshape(bf16[160,8,2,4,160]{4,3,1,2,0:T(4,128)(2,1)} %copy.19) | data formatting | bytes 6553600 | tf_op jit(solution)/shard_map/all_to_all | solution.py:33
  138.1 0.0 all-gather.2.cloned.1.call-update
  138.2 11.1 %copy.20 = bf16[160,80,320]{2,0,1:T(8,128)(2,1)} copy(bf16[160,80,320]{2,1,0:T(8,128)(2,1)} %param.4) | data formatting | bytes 16384000 | tf_op args[1]
  149.2 0.8 dynamic-slice_subtract_fusion
  150.0 0.1 broadcast_compare_fusion
  150.1 10.5 %fusion.26 = (bf16[160,40,1,320]{3,0,2,1:T(8,128)(2,1)}, bf16[160,40,1,320]{3,0,2,1:T(8,128)(2,1)}) fusion(bf16[160,40,2,320]{3,0,2,1:T(8,128)(2,1)} %bitcast.47), kind=kLoop, calls=%fused_computation.34 | loop fusion | bytes 16384000 | tf_op jit(solution)/shard_map/slice | solution.py:39
  160.6 206.0 %all-gather.2.cloned.1.call-done = bf16[160,64,2,640]{3,1,2,0:T(8,128)(2,1)} async-done(((bf16[160,8,2,640]{3,1,2,0:T(8,128)(2,1)}), bf16[160,64,2,640]{3,1,2,0:T(8,128)(2,1)}) %all-gather.2.cloned.1.call-update) | async-done | bytes 26214416 | tf_op jit(solution)/shard_map/all_gather | solution.py:36
  366.6 16.8 %slice.21 = bf16[160,64,2,320]{3,1,2,0:T(8,128)(2,1)} slice(bf16[160,64,2,640]{3,1,2,0:T(8,128)(2,1)} %all-gather.2.cloned.1.call-done), slice={[0:160], [0:64], [0:2], [320:640]} | slice | bytes 26214400 | tf_op jit(solution)/shard_map/slice | solution.py:11
  383.4 0.0 slice-start
  383.4 38.2 %reverse.1 = bf16[160,64,2,384]{3,1,2,0:T(8,128)(2,1)} reverse(bf16[160,64,2,384]{3,1,2,0:T(8,128)(2,1)} %bitcast.46), dimensions={3} | reverse | bytes 31457280
  421.5 0.0 slice-start.1
  421.5 17.5 %fusion.17 = bf16[160,40,1,2,64]{4,1,3,0,2:T(8,128)(2,1)S(1)} fusion(bf16[160,40,1,320]{3,0,2,1:T(8,128)(2,1)} %get-tuple-element.5, bf16[160,64,2,640]{3,1,2,0:T(8,128)(2,1)} %all-gather.2.cloned.1.call-done, bf16[160,64,2,384]{3,1,2,0:T(8,128)(2,1)} %reverse.1), kind=kOutput, calls=%fused_computation.27 | convolution fusion | flops 550502400 | bytes 38010880 | tf_op jit(solution)/shard_map/str,sfcr->stcf/dot_general | solution.py:38
  439.1 0.0 slice-done
  439.1 0.0 slice-done.1
  439.1 17.1 %fusion.20 = bf16[160,40,1,2,64]{4,1,3,0,2:T(8,128)(2,1)} fusion(bf16[160,40,1,320]{3,0,2,1:T(8,128)(2,1)S(1)} %bitcast.51, bf16[160,64,2,640]{3,1,2,0:T(8,128)(2,1)} %all-gather.2.cloned.1.call-done, bf16[160,64,2,384]{3,1,2,0:T(8,128)(2,1)} %reverse.1), kind=kOutput, calls=%fused_computation.28 | convolution fusion | flops 550502400 | bytes 37191680 | tf_op jit(solution)/shard_map/str,sfcr->stcf/dot_general | solution.py:41
  456.2 6.1 %pad_maximum_fusion = bf16[160,40,2,2,64]{4,1,3,0,2:T(8,128)(2,1)} fusion(bf16[160,40,1,2,64]{4,1,3,0,2:T(8,128)(2,1)} %fusion.20, bf16[160,40,1,2,64]{4,1,3,0,2:T(8,128)(2,1)S(1)} %fusion.17), kind=kLoop, calls=%fused_computation.8 | loop fusion | flops 1638400 | bytes 6553600 | tf_op jit(solution)/shard_map/stack | solution.py:44
  462.3 10.4 %copy.23 = bf16[160,40,2,2,64]{0,4,3,2,1:T(8,128)(2,1)} copy(bf16[160,40,2,2,64]{4,1,3,0,2:T(8,128)(2,1)} %pad_maximum_fusion) | data formatting | bytes 6553600 | tf_op jit(solution)/shard_map/stack | solution.py:44
  472.7 8.0 %copy.24 = bf16[160,80,128]{2,1,0:T(8,128)(2,1)S(1)} copy(bf16[160,80,128]{0,2,1:T(8,128)(2,1)} %bitcast.49) | data formatting | bytes 6553600 | tf_op jit(solution)/shard_map/reshape | solution.py:45
  480.8 4.6 select_convert_fusion
  (2 shorter events, 0.0 us)
Async XLA Ops:
  6.5 360.0 %all-gather.2.cloned.1.call-start = ((), (), s32[]{:S(2)}) async-start(), calls=%async_computation.1 | async-start | bytes 29491200 | tf_op jit(solution)/shard_map/all_gather | solution.py:36
  6.5 15.2 %copy-start = (f32[8,160,1280]{2,1,0:T(8,128)S(1)}, f32[8,160,1280]{2,1,0:T(8,128)}, u32[]{:S(2)}) copy-start(f32[8,160,1280]{2,1,0:T(8,128)} %param.3) | copy-start | bytes 19660804
  383.4 55.7 %slice-start = ((s8[4915200]{0:T(1024)(128)(4,1)}), s8[720896]{0:T(1024)(128)(4,1)S(1)}, s32[]{:S(2)}) async-start(s8[4915200]{0:T(1024)(128)(4,1)} %bitcast.50), calls=%async_computation.2 | async-start | bytes 1441792
  421.5 17.5 %slice-start.1 = ((s8[4915200]{0:T(1024)(128)(4,1)}), s8[4194304]{0:T(1024)(128)(4,1)S(1)}, s32[]{:S(2)}) async-start(s8[4915200]{0:T(1024)(128)(4,1)} %bitcast.50), calls=%async_computation.3 | async-start | bytes 8388608
Sparse Core Ops, SparseCore 0:
  138.3 228.2 all-gather.1
where the time goes:
time: 500 us; the launch traced here: 492 us
  waiting for transfers between devices  206 us (41%)
  local copies, waits for them, and re-layouts  119 us (24%)
  blocking collectives  64.5 us (13%)
  matrix products  62.8 us (13%)
  other arithmetic  26.8 us (5%)
  between operations  13.7 us (3%)
    all_gather x1, waiting for transfers between devices, per_device(): piece = lax.all_gather(arrived, 'lev', axis=1, tiled=True)  206 us
    all_to_all x1, blocking collectives, per_device(): lax.all_to_all(spec, 'lat', split_axis=0, concat_axis=3, tiled=True)  64.5 us
    unnamed x8, local copies, waits for them, and re-layouts  49.2 us
    dot_general x1, matrix products, per_device(): jnp.einsum('lcs,frl->sfcr', table, grid_gradient, precision=lax.Precision...  28.2 us
    dot_general x1, matrix products, per_device(): jnp.einsum('str,sfcr->stcf', paired[:, :, 0], even, preferred_element_typ...  17.5 us
    all_to_all x2, local copies, waits for them, and re-layouts, per_device(): lax.all_to_all(spec, 'lat', split_axis=0, concat_axis=3, tiled=True)  17.2 us
    dot_general x1, matrix products, per_device(): jnp.einsum('str,sfcr->stcf', paired[:, :, 1], odd, preferred_element_type...  17.1 us
    slice x1, local copies, waits for them, and re-layouts, split_halves(): south = arrived[..., ::-1][..., :half].astype(jnp.float32)  16.8 us
  transfers between devices with their start and end apart: 1, of which 1 were waited for; matrix products, arithmetic and copies ran while one was open for 5% of the time, Pallas kernels for 0%

commit v1 on v0

v1 whole, which is shorter than its diff:
```python
import functools
import math

import jax
import jax.numpy as jnp
from jax import lax
from jax.experimental import pallas as pl
from jax.experimental.pallas import tpu as pltpu
from jax.sharding import PartitionSpec as P

LANES = 128
VMEM_LIMIT = 48 * 1024 * 1024


def dot_nt(a, b):
    return lax.dot_general(a, b, (((1,), (1,)), ((), ())), preferred_element_type=jnp.float32)


def params():
    return pltpu.CompilerParams(vmem_limit_bytes=VMEM_LIMIT)


def hi_lo(x):
    hi = x.astype(jnp.bfloat16)
    return hi, (x - hi.astype(jnp.float32)).astype(jnp.bfloat16)


def fold_kernel(order_ref, grid_ref, out_ref):
    half = out_ref.shape[2]
    near, far = grid_ref[0, :, :half], grid_ref[0, :, half:]
    for parity, folded in enumerate((near + far, near - far)):
        for part, term in enumerate(hi_lo(folded)):
            moved = jnp.dot(order_ref[...], term, preferred_element_type=jnp.float32)
            out_ref[2 * parity + part] = moved.astype(jnp.bfloat16)


def fold_grid(grid, order):
    fields, rows, nlon = grid.shape
    half = nlon // 2
    return pl.pallas_call(
        fold_kernel,
        grid=(fields,),
        in_specs=[
            pl.BlockSpec((rows, rows), lambda f: (0, 0)),
            pl.BlockSpec((1, rows, nlon), lambda f: (f, 0, 0)),
        ],
        out_specs=pl.BlockSpec((4, None, rows, half), lambda f: (0, f, 0, 0)),
        out_shape=jax.ShapeDtypeStruct((4, fields, rows, half), jnp.bfloat16),
        compiler_params=params(),
        cost_estimate=pl.CostEstimate(
            flops=8 * fields * rows * rows * half, bytes_accessed=8 * fields * rows * nlon, transcendentals=0
        ),
        name="fold",
    )(order, grid)


def zonal_kernel(start, base_ref, step_ref, first_ref, grid_ref, out_ref, table_ref):
    groups, _, _, pairs, _ = out_ref.shape
    count = groups * pairs
    steps = step_ref.shape[3]

    @pl.when(pl.program_id(0) == 0)
    def _():
        for parity in range(2):
            cos0 = base_ref[parity, 0, start : start + count]
            sin0 = base_ref[parity, 1, start : start + count]
            for b in range(steps):
                cos1 = step_ref[parity, 0, start : start + count, b : b + 1]
                sin1 = step_ref[parity, 1, start : start + count, b : b + 1]
                both = (cos0 * cos1 - sin0 * sin1, -(sin0 * cos1 + cos0 * sin1))
                for c, table in enumerate(both):
                    for part, term in enumerate(hi_lo(table)):
                        table_ref[parity, part, c * count : (c + 1) * count, b * LANES : (b + 1) * LANES] = term

    found = []
    for parity in range(2):
        hi, lo = table_ref[parity, 0], table_ref[parity, 1]
        found.append(
            dot_nt(hi, grid_ref[2 * parity])
            + (dot_nt(lo, grid_ref[2 * parity]) + dot_nt(hi, grid_ref[2 * parity + 1]))
        )
    first = first_ref[start : start + count] > 0.5
    for c in range(2):
        even, odd = found[0][c * count : (c + 1) * count], found[1][c * count : (c + 1) * count]
        low = jnp.where(first, even, odd).astype(jnp.bfloat16)
        high = jnp.where(first, odd, even).astype(jnp.bfloat16)
        for g in range(groups):
            out_ref[g, 0, c] = low[g * pairs : (g + 1) * pairs]
            out_ref[g, 1, c] = high[g * pairs : (g + 1) * pairs]


def zonal(base, step, first, folded, groups, start, pairs):
    columns, half = folded.shape[1:]
    block = columns // 5 if columns % (5 * LANES) == 0 else columns
    count = groups * pairs
    return pl.pallas_call(
        functools.partial(zonal_kernel, start),
        grid=(columns // block,),
        in_specs=[
            pl.BlockSpec(base.shape, lambda n: (0, 0, 0, 0)),
            pl.BlockSpec(step.shape, lambda n: (0, 0, 0, 0)),
            pl.BlockSpec(first.shape, lambda n: (0, 0)),
            pl.BlockSpec((4, block, half), lambda n: (0, n, 0)),
        ],
        out_specs=pl.BlockSpec((groups, 2, 2, pairs, block), lambda n: (0, 0, 0, 0, n)),
        out_shape=jax.ShapeDtypeStruct((groups, 2, 2, pairs, columns), jnp.bfloat16),
        scratch_shapes=[pltpu.VMEM((2, 2, 2 * count, half), jnp.bfloat16)],
        compiler_params=params(),
        cost_estimate=pl.CostEstimate(
            flops=24 * count * columns * half, bytes_accessed=8 * columns * half, transcendentals=0
        ),
        name="zonal",
    )(base, step, first, folded)


def halves_kernel(fields, wide, in_ref, low_ref, high_ref, work_ref):
    groups, _, _, pairs, columns = in_ref.shape
    rows = columns // fields
    for which, out_ref in enumerate((low_ref, high_ref)):
        for c in range(2):
            parts = [in_ref[g, which, c].astype(jnp.float32) for g in range(groups)]
            sums = [parts[g] + parts[groups - 1 - g] for g in range(groups // 2)]
            gaps = [parts[g] - parts[groups - 1 - g] for g in range(groups // 2)]
            for f in range(fields):
                at = slice(f * rows, (f + 1) * rows)
                even = jnp.concatenate([x[:, at] for x in sums], axis=1)
                odd = jnp.concatenate([x[:, at] for x in gaps], axis=1)
                whole = jnp.concatenate([even[:, :wide], odd[:, :wide], even[:, wide:], odd[:, wide:]], axis=1)
                work_ref[:, c * fields + f, :] = whole
        out_ref[...] = work_ref[...].astype(jnp.bfloat16)


def halves(arrived, fields, wide):
    groups, _, _, pairs, columns = arrived.shape
    length = groups * columns // fields
    shape = jax.ShapeDtypeStruct((pairs, 2 * fields, length), jnp.bfloat16)
    return pl.pallas_call(
        functools.partial(halves_kernel, fields, wide),
        out_shape=(shape, shape),
        in_specs=[pl.BlockSpec(memory_space=pltpu.VMEM)],
        out_specs=(pl.BlockSpec(memory_space=pltpu.VMEM),) * 2,
        scratch_shapes=[pltpu.VMEM((pairs, 2 * fields, length), jnp.float32)],
        compiler_params=params(),
        cost_estimate=pl.CostEstimate(
            flops=pairs * 4 * fields * length, bytes_accessed=16 * pairs * fields * length, transcendentals=0
        ),
        name="halves",
    )(arrived)


def contract(table, mine, other, index, wide, order):
    chips, _, lines, length = mine.shape
    spec = jnp.concatenate(
        [ref[d, index] for d in range(chips) for ref in (mine, other)], axis=0
    )
    half = length // 2
    count = spec.shape[0]
    degrees = table.shape[0]
    even_row = lax.rem(lax.broadcasted_iota(jnp.int32, (degrees, 1), 0), 2) == 0
    main = dot_nt(table[:, :wide], jnp.concatenate([spec[:, :wide], spec[:, wide : 2 * wide]], axis=0))
    total = jnp.where(even_row, main[:, :count], main[:, count:])
    if half > wide:
        rest = table[:, wide:].astype(jnp.float32)
        rest = jnp.concatenate([jnp.where(even_row, rest, 0.0), jnp.where(even_row, 0.0, rest)], axis=1)
        total = total + dot_nt(rest.astype(jnp.bfloat16), spec[:, 2 * wide :])
    return jnp.dot(total.astype(jnp.bfloat16), order, preferred_element_type=jnp.float32)


def keep_valid(values, first_degree, wave, modes):
    degrees = first_degree + lax.broadcasted_iota(jnp.int32, (values.shape[0], 1), 0)
    return jnp.where(degrees < modes - wave, values, 0.0).astype(jnp.bfloat16)


def column_order(lev_id, chips, lines):
    fields = lines // 2
    count = 2 * chips * lines
    row = lax.broadcasted_iota(jnp.int32, (count, count), 0)
    column = lax.broadcasted_iota(jnp.int32, (count, count), 1)
    chip = lax.rem(row // (2 * lines) + lev_id // 2, chips)
    core = lax.rem(row // lines + lev_id, 2)
    c = lax.rem(row // fields, 2)
    target = c * (count // 2) + (2 * chip + core) * fields + lax.rem(row, fields)
    return jnp.where(column == target, 1.0, 0.0).astype(jnp.bfloat16)


def high_kernel(start, modes, wide, info_ref, waves_ref, order_ref, table_ref, given_ref, mine_ref, other_ref, own_ref, back_ref):
    pairs, degrees, _ = own_ref.shape
    block = pl.program_id(0)
    lev = info_ref[0]
    order = order_ref[...]

    def body(i, _):
        q = start + block * pairs + i
        swapped = waves_ref[2 * q] > waves_ref[2 * q + 1]
        slot = 2 * i + jnp.where(swapped, 0, 1)
        wave = jnp.maximum(waves_ref[2 * q], waves_ref[2 * q + 1])
        both = jnp.concatenate([table_ref[slot], given_ref[i]], axis=0)
        values = contract(both, mine_ref, other_ref, i, wide, order)
        own_ref[i] = keep_valid(values[:degrees], lev * degrees, wave, modes)
        back_ref[i] = keep_valid(values[degrees:], (lev - 2) * degrees, wave, modes)
        return 0

    lax.fori_loop(0, pairs, body, 0, unroll=2 if pairs % 2 == 0 else 1)


def low_kernel(start, modes, wide, info_ref, waves_ref, order_ref, table_ref, mine_ref, other_ref, own_ref, back_ref, *out_refs):
    out_ref = out_refs[-1]
    pairs, degrees, _ = own_ref.shape
    block = pl.program_id(0)
    lev = info_ref[0]
    order = order_ref[...]
    lowest = lev < 2

    def body(i, _):
        q = start + block * pairs + i
        swapped = waves_ref[2 * q] > waves_ref[2 * q + 1]
        slot = 2 * i + jnp.where(swapped, 1, 0)
        wave = jnp.minimum(waves_ref[2 * q], waves_ref[2 * q + 1])
        values = contract(table_ref[slot], mine_ref, other_ref, i, wide, order)
        out_ref[slot] = keep_valid(values, lev * degrees, wave, modes)
        out_ref[2 * i + jnp.where(swapped, 0, 1)] = jnp.where(lowest, back_ref[i], own_ref[i])
        return 0

    lax.fori_loop(0, pairs, body, 0, unroll=2 if pairs % 2 == 0 else 1)


def legendre_specs(start, block, degrees, half, mine, count):
    chips, _, lines, length = mine.shape
    smem = pl.BlockSpec(memory_space=pltpu.SMEM)
    offset = start // block
    piece = pl.BlockSpec((chips, block, lines, length), lambda i: (0, i, 0, 0))
    return [smem, smem, pl.BlockSpec((count, count), lambda i: (0, 0)),
            pl.BlockSpec((2 * block, degrees, half), lambda i: (offset + i, 0, 0))], piece


def block_pairs(start, pairs):
    for size in (8, 4, 2):
        if start % size == 0 and pairs % size == 0:
            return size
    return pairs if start % pairs == 0 else 1


def high_slots(start, modes, wide, info, waves, order, table, given, mine, other):
    pairs, degrees, half = given.shape
    count = order.shape[0]
    block = block_pairs(start, pairs)
    shared, piece = legendre_specs(start, block, degrees, half, mine, count)
    result = pl.BlockSpec((block, degrees, count), lambda i: (i, 0, 0))
    shape = jax.ShapeDtypeStruct((pairs, degrees, count), jnp.bfloat16)
    return pl.pallas_call(
        functools.partial(high_kernel, start, modes, wide),
        grid=(pairs // block,),
        in_specs=shared + [pl.BlockSpec((block, degrees, half), lambda i: (i, 0, 0)), piece, piece],
        out_specs=(result, result),
        out_shape=(shape, shape),
        compiler_params=params(),
        cost_estimate=pl.CostEstimate(
            flops=8 * pairs * degrees * half * count, bytes_accessed=pairs * count * half * 8, transcendentals=0
        ),
        name="high_slots",
    )(info, waves, order, table, given, mine, other)


def low_slots(start, modes, wide, info, waves, order, table, mine, other, own, back, out):
    pairs, degrees, count = own.shape
    slots, _, half = table.shape
    block = block_pairs(start, pairs)
    offset = start // block
    shared, piece = legendre_specs(start, block, degrees, half, mine, count)
    given = pl.BlockSpec((block, degrees, count), lambda i: (i, 0, 0))
    operands = [info, waves, order, table, mine, other, own, back]
    in_specs = shared + [piece, piece, given, given]
    aliases = {}
    if out is not None:
        aliases = {len(operands): 0}
        operands.append(out)
        in_specs.append(pl.BlockSpec(memory_space=pl.ANY))
    return pl.pallas_call(
        functools.partial(low_kernel, start, modes, wide),
        grid=(pairs // block,),
        in_specs=in_specs,
        out_specs=pl.BlockSpec((2 * block, degrees, count), lambda i: (offset + i, 0, 0)),
        out_shape=jax.ShapeDtypeStruct((slots, degrees, count), jnp.bfloat16),
        input_output_aliases=aliases,
        compiler_params=params(),
        cost_estimate=pl.CostEstimate(
            flops=4 * pairs * degrees * half * count, bytes_accessed=pairs * count * half * 8, transcendentals=0
        ),
        name="low_slots",
    )(*operands)


def on_cores(chip_pairs):
    return [(2 * a + core, 2 * b + core) for a, b in chip_pairs for core in range(2)]


def spread(own, z, chips, down_from, up_to):
    down, up = {0: own}, {0: own}
    for d in range(1, chips):
        pairs = [(t + 1, t) for t in range(down_from, chips - d)]
        down[d] = lax.ppermute(down[d - 1], "lev", on_cores(pairs)) if pairs else None
        pairs = [(t - 1, t) for t in range(d, up_to + 1)]
        up[d] = lax.ppermute(up[d - 1], "lev", on_cores(pairs)) if pairs else None
    blocks = [own]
    for d in range(1, chips):
        above, below = down[d], up[chips - d]
        if above is None or below is None:
            blocks.append(below if above is None else above)
        else:
            blocks.append(jnp.where(z + d < chips, above, below))
    blocks = [jnp.zeros_like(own) if b is None else b for b in blocks]
    return jnp.stack(blocks)


def chunk_sizes(pairs):
    if pairs % 16:
        return [pairs]
    if pairs % 80 == 0:
        return [pairs // 5, 2 * pairs // 5, 2 * pairs // 5]
    return [pairs]


def per_device(grid_gradient, legendre, assign):
    fields, rows, nlon = grid_gradient.shape
    modes = nlon // 2
    slots, degrees, half = legendre.shape
    groups = lax.axis_size("lat")
    chips = lax.axis_size("lev") // 2
    lat_id = lax.axis_index("lat")
    lev_id = lax.axis_index("lev")
    z = lev_id // 2
    pairs = slots // 2
    wide = half // 256 * 256 if half >= 256 else half
    lines = 2 * fields
    assign = assign.astype(jnp.int32)

    chunks, start = [], 0
    for size in chunk_sizes(pairs):
        chunks.append((start, size))
        start += size

    by_group = assign.reshape(groups, pairs, 2)
    listed = jnp.concatenate([by_group[:, s : s + n].reshape(groups * n, 2) for s, n in chunks])
    swapped = listed[:, 0] % 2 == 1
    even_wave = jnp.where(swapped, listed[:, 1], listed[:, 0])
    odd_wave = jnp.where(swapped, listed[:, 0], listed[:, 1])
    both = jnp.stack([even_wave, odd_wave])
    first = (even_wave < odd_wave).astype(jnp.float32)[:, None]
    weight = jnp.where(both == 0, 1.0, 2.0).astype(jnp.float32)[:, :, None]
    turn = 2.0 * math.pi / nlon

    def cos_sin(places, scale):
        angle = (both[:, :, None] * places % nlon).astype(jnp.float32) * turn
        return jnp.stack([jnp.cos(angle) * scale, jnp.sin(angle) * scale], axis=1)

    base = cos_sin(jnp.arange(LANES, dtype=jnp.int32), weight)
    step = cos_sin(jnp.arange(0, modes, LANES, dtype=jnp.int32), 1.0)

    here = jnp.arange(rows, dtype=jnp.int32)
    wanted = jnp.where(lat_id >= groups // 2, rows - 1 - here, here)
    row_order = (here[None, :] == wanted[:, None]).astype(jnp.bfloat16)
    folded = fold_grid(grid_gradient, row_order).reshape(4, fields * rows, modes)

    waves = lax.dynamic_slice(assign, (lat_id * slots,), (slots,))
    info = jnp.stack([lev_id])
    order = column_order(lev_id, chips, lines)
    in_pairs = legendre.reshape(pairs, 2, degrees, half)
    second_high = (waves[0::2] < waves[1::2])[:, None, None]
    high_table = jnp.where(second_high, in_pairs[:, 1], in_pairs[:, 0])
    swap = [(i, i ^ 1) for i in range(2 * chips)]

    out = None
    for s, n in chunks:
        given = lax.ppermute(high_table[s : s + n], "lev", on_cores([(0, 1)]))
        spec = zonal(base, step, first, folded, groups, groups * s, n)
        arrived = lax.all_to_all(spec, "lat", split_axis=0, concat_axis=0, tiled=True)
        low, high = halves(arrived, fields, wide)
        high_mine = spread(high, z, chips, 1, max(chips // 2 - 1, 1))
        low_mine = spread(low, z, chips, 0, chips - 1)
        high_other = lax.ppermute(high_mine, "lev", swap)
        own, back = high_slots(s, modes, wide, info, waves, order, legendre, given, high_mine, high_other)
        back = lax.ppermute(back, "lev", on_cores([(1, 0)]))
        low_other = lax.ppermute(low_mine, "lev", swap)
        out = low_slots(s, modes, wide, info, waves, order, legendre, low_mine, low_other, own, back, out)
    return out


def solution(mesh):
    in_specs = (P("lev", "lat", None), P("lat", "lev", None), P())
    out_specs = P("lat", "lev", None)
    return jax.shard_map(
        per_device, mesh=mesh, in_specs=in_specs, out_specs=out_specs, check_vma=False
    )
```

time: 500 us -> 370 us (0.74); the launches traced: 492 us -> 368 us
  starting transfers between devices: 0.01 us -> 122 us
  local copies, waits for them, and re-layouts: 119 us -> 12.3 us
  Pallas kernels: 0 us -> 97.3 us
  waiting for transfers between devices: 206 us -> 116 us
  blocking collectives: 64.5 us -> 0 us
  matrix products: 62.8 us -> 0 us
  between operations: 13.7 us -> 0.81 us
  other arithmetic: 26.8 us -> 20.5 us
    all_gather x1 -> x0, waiting for transfers between devices: 206 us -> none  [per_device(): piece = lax.all_gather(arrived, 'lev', axis=1, tiled=True)]
    ppermute x0 -> x39, waiting for transfers between devices: none -> 114 us  [the longest x3 42.8 us: per_device(): given = lax.ppermute(high_table[s:s + n], 'lev', on_cores([(0, 1)]))]
    ppermute x0 -> x39, starting transfers between devices: none -> 109 us  [the longest x3 46 us: per_device(): given = lax.ppermute(high_table[s:s + n], 'lev', on_cores([(0, 1)]))]
    pallas_call x0 -> x13, Pallas kernels: none -> 97.3 us  [the longest x3 28.4 us: low_slots(): pl.pallas_call(functools.partial(low_kernel, start, modes, wide), grid=(p...]
    all_to_all x1 -> x0, blocking collectives: 64.5 us -> none  [per_device(): lax.all_to_all(spec, 'lat', split_axis=0, concat_axis=3, tiled=True)]
    dot_general x3 -> x0, matrix products: 62.8 us -> none  [the longest x1 28.2 us: per_device(): jnp.einsum('lcs,frl->sfcr', table, grid_gradient, precision=lax.Precision...]
    unnamed x8 -> x46, local copies, waits for them, and re-layouts: 49.2 us -> 3.08 us
    slice x2 -> x7, local copies, waits for them, and re-layouts: 27.3 us -> 7.32 us  [the longest x2 6.72 us: per_device(): given = lax.ppermute(high_table[s:s + n], 'lev', on_cores([(0, 1)]))]
  transfers between devices with their start and end apart: 1 -> 42, of which waited for: 1 -> 13; matrix products, arithmetic and copies ran while one was open for 5% -> 7% of each run, Pallas kernels for 0% -> 19%
where the time goes in v1:
time: 370 us; the launch traced here: 368 us
  starting transfers between devices  122 us (33%)
  waiting for transfers between devices  116 us (31%)
  Pallas kernels  97.3 us (26%)
  other arithmetic  20.5 us (6%)
  local copies, waits for them, and re-layouts  12.3 us (3%)
    ppermute x3, starting transfers between devices, per_device(): given = lax.ppermute(high_table[s:s + n], 'lev', on_cores([(0, 1)]))  46 us
    ppermute x3, waiting for transfers between devices, per_device(): given = lax.ppermute(high_table[s:s + n], 'lev', on_cores([(0, 1)]))  42.8 us
    ppermute x15, waiting for transfers between devices, spread(): lax.ppermute(down[d - 1], 'lev', on_cores(pairs))  41.8 us
    ppermute x12, starting transfers between devices, spread(): up[d] = lax.ppermute(up[d - 1], 'lev', on_cores(pairs)) if pairs else None  40.1 us
    pallas_call x3, Pallas kernels, low_slots(): pl.pallas_call(functools.partial(low_kernel, start, modes, wide), grid=(p...  28.4 us
    pallas_call x3, Pallas kernels, high_slots(): pl.pallas_call(functools.partial(high_kernel, start, modes, wide), grid=(...  28.3 us
    ppermute x12, waiting for transfers between devices, spread(): up[d] = lax.ppermute(up[d - 1], 'lev', on_cores(pairs)) if pairs else None  26.4 us
    pallas_call x3, Pallas kernels, zonal(): pl.pallas_call(functools.partial(zonal_kernel, start), grid=(columns // b...  22.9 us
  transfers between devices with their start and end apart: 42, of which 13 were waited for; matrix products, arithmetic and copies ran while one was open for 7% of the time, Pallas kernels for 19%

profile of v1, /device:TPU:0, one launch (start us, length us, event | category | flops | bytes accessed | tf_op | source)
XLA Modules:
  0.0 368.4 jit_solution(14895885480483931524)
XLA Ops:
  2.3 1.4 cosine_multiply_fusion
  3.8 9.2 %fold.1 = bf16[4,8,160,640]{3,2,1,0:T(8,128)(2,1)} custom-call(bf16[160,160]{1,0:T(8,128)(2,1)S(1)} %fusion.9.order_ref, f32[8,160,1280]{2,1,0:T(8,128)} %grid_ref.1), custom_call_target="tpu_custom_call" | custom-call | flops 1048576000 | bytes 13107200 | tf_op jit(solution)/shard_map/fold/pallas_call | solution.py:40
  13.0 7.3 %zonal.5 = bf16[4,2,2,16,1280]{4,3,2,1,0:T(8,128)(2,1)} custom-call(f32[2,2,320,128]{3,2,1,0:T(8,128)S(1)} %pad_maximum_fusion.6.base_ref, f32[2,2,320,5]{3,2,1,0:T(8,128)S(1)} %copy.25.step_ref, f32[320,1]{1,0:T(8,128)S(1)} %fusion.8.first_ref, bf16[4,1280,640]{2,1,0:T(8,128)(2,1)} %bitcast.57), custom_call_target="tpu_custom_call" | custom-call | flops 1258291200 | bytes 6553600 | tf_op jit(solution)/shard_map/zonal/pallas_call | solution.py:96
  20.3 5.2 %all-to-all-start.2 = ((bf16[4,2,2,16,1280]{4,3,2,1,0:T(8,128)(2,1)}), bf16[4,2,2,16,1280]{4,3,2,1,0:T(8,128)(2,1)S(1)}, u32[]{:S(2)}, u32[]{:S(2)}) async-start(bf16[4,2,2,16,1280]{4,3,2,1,0:T(8,128)(2,1)} %zonal.5), calls=%async_computation.2 | async-start | bytes 1310720 | tf_op jit(solution)/shard_map/all_to_all | solution.py:376
  25.5 7.8 %zonal.4 = bf16[4,2,2,32,1280]{4,3,2,1,0:T(8,128)(2,1)} custom-call(f32[2,2,320,128]{3,2,1,0:T(8,128)S(1)} %pad_maximum_fusion.6.base_ref, f32[2,2,320,5]{3,2,1,0:T(8,128)S(1)} %copy.25.step_ref, f32[320,1]{1,0:T(8,128)S(1)} %fusion.8.first_ref, bf16[4,1280,640]{2,1,0:T(8,128)(2,1)} %bitcast.58), custom_call_target="tpu_custom_call" | custom-call | flops 2516582400 | bytes 6553600 | tf_op jit(solution)/shard_map/zonal/pallas_call | solution.py:96
  33.3 1.6 all-to-all-done.2.in_ref
  35.0 3.5 all-to-all-start.1
  39.6 6.8 %fusion = bf16[80,80,320]{2,1,0:T(8,128)(2,1)} fusion(bf16[80,2,80,320]{3,2,1,0:T(8,128)(2,1)} %bitcast.56, pred[80]{0:T(512)(128)(4,1)S(1)} %lt.54), kind=kLoop, calls=%fused_computation.1 | loop fusion | flops 2048000 | bytes 12288080 | tf_op jit(solution)/shard_map/jit(_where)/select_n | solution.py:369
  46.4 2.3 slice.60
  48.7 4.4 %collective-permute-start.33 = (bf16[16,80,320]{2,1,0:T(8,128)(2,1)}, bf16[16,80,320]{2,1,0:T(8,128)(2,1)}, u32[]{:S(2)}, u32[]{:S(2)}) collective-permute-start(bf16[16,80,320]{2,1,0:T(8,128)(2,1)} %slice.60), channel_id=1, source_target_pairs={{0,2},{1,3},{8,10},{9,11},{16,18},{17,19},{24,26},{25,27}} | collective-permute-start | bytes 2457608 | tf_op jit(solution)/shard_map/ppermute | solution.py:374
  53.1 7.8 %zonal.3 = bf16[4,2,2,32,1280]{4,3,2,1,0:T(8,128)(2,1)} custom-call(f32[2,2,320,128]{3,2,1,0:T(8,128)S(1)} %pad_maximum_fusion.6.base_ref, f32[2,2,320,5]{3,2,1,0:T(8,128)S(1)} %copy.25.step_ref, f32[320,1]{1,0:T(8,128)S(1)} %fusion.8.first_ref, bf16[4,1280,640]{2,1,0:T(8,128)(2,1)} %bitcast.59), custom_call_target="tpu_custom_call" | custom-call | flops 2516582400 | bytes 6553600 | tf_op jit(solution)/shard_map/zonal/pallas_call | solution.py:96
  60.9 4.1 %all-to-all-start = ((bf16[4,2,2,32,1280]{4,3,2,1,0:T(8,128)(2,1)}), bf16[4,2,2,32,1280]{4,3,2,1,0:T(8,128)(2,1)S(1)}, u32[]{:S(2)}, u32[]{:S(2)}) async-start(bf16[4,2,2,32,1280]{4,3,2,1,0:T(8,128)(2,1)} %zonal.3), calls=%async_computation | async-start | bytes 2621440 | tf_op jit(solution)/shard_map/all_to_all | solution.py:376
  65.1 1.9 halves.5
  69.7 3.7 %halves.4 = (bf16[32,16,640]{2,1,0:T(8,128)(2,1)S(1)}, bf16[32,16,640]{2,1,0:T(8,128)(2,1)}) custom-call(bf16[4,2,2,32,1280]{4,3,2,1,0:T(8,128)(2,1)S(1)} %all-to-all-done.1.in_ref), custom_call_target="tpu_custom_call" | custom-call | flops 655360 | bytes 2621440 | tf_op jit(solution)/shard_map/halves/pallas_call | solution.py:137
  73.4 3.5 collective-permute-start.14
  78.2 5.3 %collective-permute-start.36 = (bf16[16,16,640]{2,1,0:T(8,128)(2,1)S(1)}, bf16[16,16,640]{2,1,0:T(8,128)(2,1)}, u32[]{:S(2)}, u32[]{:S(2)}) collective-permute-start(bf16[16,16,640]{2,1,0:T(8,128)(2,1)S(1)} %get-tuple-element.26), channel_id=1, source_target_pairs={{0,2},{1,3},{8,10},{9,11},{16,18},{17,19},{24,26},{25,27}} | collective-permute-start | bytes 983048 | tf_op jit(solution)/shard_map/ppermute | solution.py:303
  87.6 13.0 %collective-permute-done.36 = bf16[16,16,640]{2,1,0:T(8,128)(2,1)} collective-permute-done((bf16[16,16,640]{2,1,0:T(8,128)(2,1)S(1)}, bf16[16,16,640]{2,1,0:T(8,128)(2,1)}, u32[]{:S(2)}, u32[]{:S(2)}) %collective-permute-start.36) | collective-permute-done | bytes 327712 | tf_op jit(solution)/shard_map/ppermute | solution.py:303
  100.6 5.3 %collective-permute-start.23 = (bf16[32,16,640]{2,1,0:T(8,128)(2,1)}, bf16[32,16,640]{2,1,0:T(8,128)(2,1)}, u32[]{:S(2)}, u32[]{:S(2)}) collective-permute-start(bf16[32,16,640]{2,1,0:T(8,128)(2,1)} %get-tuple-element.22), channel_id=1, source_target_pairs={{0,2},{1,3},{8,10},{9,11},{16,18},{17,19},{24,26},{25,27}} | collective-permute-start | bytes 1966088 | tf_op jit(solution)/shard_map/ppermute | solution.py:303
  106.8 1.5 collective-permute-start.21
  108.3 2.9 halves.3
  111.2 2.2 collective-permute-start.1
  115.5 5.1 %collective-permute-done.23 = bf16[32,16,640]{2,1,0:T(8,128)(2,1)} collective-permute-done((bf16[32,16,640]{2,1,0:T(8,128)(2,1)}, bf16[32,16,640]{2,1,0:T(8,128)(2,1)}, u32[]{:S(2)}, u32[]{:S(2)}) %collective-permute-start.23) | collective-permute-done | bytes 655392 | tf_op jit(solution)/shard_map/ppermute | solution.py:303
  120.6 1.5 collective-permute-start.15
  123.4 8.2 %collective-permute-done.1 = bf16[32,16,640]{2,1,0:T(8,128)(2,1)} collective-permute-done((bf16[32,16,640]{2,1,0:T(8,128)(2,1)S(1)}, bf16[32,16,640]{2,1,0:T(8,128)(2,1)}, u32[]{:S(2)}, u32[]{:S(2)}) %collective-permute-start.1) | collective-permute-done | bytes 655392 | tf_op jit(solution)/shard_map/ppermute | solution.py:303
  131.6 1.5 collective-permute-start.2
  134.4 4.5 %fusion.27 = (bf16[32,80,320]{2,1,0:T(8,128)(2,1)}, bf16[32,80,320]{2,1,0:T(8,128)(2,1)}) fusion(bf16[80,80,320]{2,1,0:T(8,128)(2,1)} %fusion), kind=kLoop, calls=%fused_computation.90 | loop fusion | bytes 6553600 | tf_op jit(solution)/shard_map/slice | solution.py:374
  141.2 16.6 %collective-permute-start.10 = (bf16[32,16,640]{2,1,0:T(8,128)(2,1)S(1)}, bf16[32,16,640]{2,1,0:T(8,128)(2,1)S(1)}, u32[]{:S(2)}, u32[]{:S(2)}) collective-permute-start(bf16[32,16,640]{2,1,0:T(8,128)(2,1)S(1)} %get-tuple-element.18), channel_id=1, source_target_pairs={{0,2},{1,3},{8,10},{9,11},{16,18},{17,19},{24,26},{25,27}} | collective-permute-start | bytes 1966088 | tf_op jit(solution)/shard_map/ppermute | solution.py:303
  163.7 2.0 pad_maximum_fusion.3.mine_ref
  165.7 11.1 %collective-permute-done.30 = bf16[16,16,640]{2,1,0:T(8,128)(2,1)S(1)} collective-permute-done((bf16[16,16,640]{2,1,0:T(8,128)(2,1)S(1)}, bf16[16,16,640]{2,1,0:T(8,128)(2,1)S(1)}, u32[]{:S(2)}, u32[]{:S(2)}) %collective-permute-start.30) | collective-permute-done | bytes 327712 | tf_op jit(solution)/shard_map/ppermute | solution.py:301
  176.8 40.1 %collective-permute-start.20 = (bf16[32,80,320]{2,1,0:T(8,128)(2,1)S(1)}, bf16[32,80,320]{2,1,0:T(8,128)(2,1)S(1)}, u32[]{:S(2)}, u32[]{:S(2)}) collective-permute-start(bf16[32,80,320]{2,1,0:T(8,128)(2,1)S(1)} %copy-done.15), channel_id=1, source_target_pairs={{0,2},{1,3},{8,10},{9,11},{16,18},{17,19},{24,26},{25,27}} | collective-permute-start | bytes 4915208 | tf_op jit(solution)/shard_map/ppermute | solution.py:374
  216.9 1.4 collective-permute-start.7
  220.1 1.4 collective-permute-start.5
  224.6 13.5 %collective-permute-done.18 = bf16[32,16,640]{2,1,0:T(8,128)(2,1)S(1)} collective-permute-done((bf16[32,16,640]{2,1,0:T(8,128)(2,1)}, bf16[32,16,640]{2,1,0:T(8,128)(2,1)S(1)}, u32[]{:S(2)}, u32[]{:S(2)}) %collective-permute-start.18) | collective-permute-done | bytes 655392 | tf_op jit(solution)/shard_map/ppermute | solution.py:301
  239.5 12.7 %collective-permute-done.5 = bf16[32,16,640]{2,1,0:T(8,128)(2,1)S(1)} collective-permute-done((bf16[32,16,640]{2,1,0:T(8,128)(2,1)}, bf16[32,16,640]{2,1,0:T(8,128)(2,1)S(1)}, u32[]{:S(2)}, u32[]{:S(2)}) %collective-permute-start.5) | collective-permute-done | bytes 655392 | tf_op jit(solution)/shard_map/ppermute | solution.py:301
  252.7 3.8 %collective-permute-done.31 = bf16[16,16,640]{2,1,0:T(8,128)(2,1)S(1)} collective-permute-done((bf16[16,16,640]{2,1,0:T(8,128)(2,1)S(1)}, bf16[16,16,640]{2,1,0:T(8,128)(2,1)S(1)}, u32[]{:S(2)}, u32[]{:S(2)}) %collective-permute-start.31) | collective-permute-done | bytes 327712 | tf_op jit(solution)/shard_map/ppermute | solution.py:301
  256.9 3.1 collective-permute-done.20.given_ref
  260.0 39.7 %collective-permute-done.7.given_ref = bf16[32,80,320]{2,1,0:T(8,128)(2,1)S(1)} collective-permute-done((bf16[32,80,320]{2,1,0:T(8,128)(2,1)S(1)}, bf16[32,80,320]{2,1,0:T(8,128)(2,1)S(1)}, u32[]{:S(2)}, u32[]{:S(2)}) %collective-permute-start.7) | collective-permute-done | bytes 1638432 | tf_op jit(solution)/shard_map/ppermute | solution.py:374
  299.9 1.5 pad_maximum_fusion.4.mine_ref
  302.0 6.5 %high_slots.5 = (bf16[16,80,128]{2,1,0:T(8,128)(2,1)S(1)}, bf16[16,80,128]{2,1,0:T(8,128)(2,1)}) custom-call(s32[1]{0:T(128)} %bitcast.info_ref, s32[160]{0:T(256)S(1)} %dynamic_slice.3.waves_ref, bf16[128,128]{1,0:T(8,128)(2,1)S(1)} %select_convert_fusion.order_ref, bf16[160,80,320]{2,1,0:T(8,128)(2,1)} %table_ref.11, ...), custom_call_target="tpu_custom_call" | custom-call | flops 419430400 | bytes 5242880 | tf_op jit(solution)/shard_map/high_slots/pallas_call | solution.py:250
  309.3 1.4 collective-permute-start.38
  310.7 1.5 copy-done.3
  312.2 11.2 %high_slots.4 = (bf16[32,80,128]{2,1,0:T(8,128)(2,1)S(1)}, bf16[32,80,128]{2,1,0:T(8,128)(2,1)}) custom-call(s32[1]{0:T(128)} %bitcast.info_ref, s32[160]{0:T(256)S(1)} %dynamic_slice.3.waves_ref, bf16[128,128]{1,0:T(8,128)(2,1)S(1)} %select_convert_fusion.order_ref, bf16[160,80,320]{2,1,0:T(8,128)(2,1)} %table_ref.11, bf16[32,80,320]{2,1,0:T(8,128)(2,1)S(1)} %copy-done.3, ...), custom_call_target="tpu_custom_call" | custom-call | flops 838860800 | bytes 10485760 | tf_op jit(solution)/shard_map/high_slots/pallas_call | solution.py:250
  323.5 1.4 collective-permute-start.25
  324.9 10.6 %high_slots.3 = (bf16[32,80,128]{2,1,0:T(8,128)(2,1)S(1)}, bf16[32,80,128]{2,1,0:T(8,128)(2,1)S(1)}) custom-call(s32[1]{0:T(128)} %bitcast.info_ref, s32[160]{0:T(256)S(1)} %dynamic_slice.3.waves_ref, bf16[128,128]{1,0:T(8,128)(2,1)S(1)} %select_convert_fusion.order_ref, bf16[160,80,320]{2,1,0:T(8,128)(2,1)} %table_ref.11, ...), custom_call_target="tpu_custom_call" | custom-call | flops 838860800 | bytes 10485760 | tf_op jit(solution)/shard_map/high_slots/pallas_call | solution.py:250
  336.8 6.7 %low_slots.3.out_refs_0_ = bf16[160,80,128]{2,1,0:T(8,128)(2,1)} custom-call(s32[1]{0:T(128)} %bitcast.info_ref, s32[160]{0:T(256)S(1)} %dynamic_slice.3.waves_ref, bf16[128,128]{1,0:T(8,128)(2,1)S(1)} %select_convert_fusion.order_ref, bf16[160,80,320]{2,1,0:T(8,128)(2,1)} %table_ref.11, bf16[4,16,16,640]{3,2,1,0:T(8,128)(2,1)} %pad_maximum_fusion.4.mine_ref, ...), custom_call_target="tpu_custom_call" | custom-call | flops 209715200 | bytes 5242880 | tf_op jit(solution)/shard_map/low_slots/pallas_call | solution.py:278
  344.0 10.9 %low_slots.4.out_refs_0_ = bf16[160,80,128]{2,1,0:T(8,128)(2,1)} custom-call(s32[1]{0:T(128)} %bitcast.info_ref, s32[160]{0:T(256)S(1)} %dynamic_slice.3.waves_ref, bf16[128,128]{1,0:T(8,128)(2,1)S(1)} %select_convert_fusion.order_ref, bf16[160,80,320]{2,1,0:T(8,128)(2,1)} %table_ref.11, ...), custom_call_target="tpu_custom_call", output_to_operand_aliasing={{}: (8, {})} | custom-call | flops 419430400 | bytes 10485760 | tf_op jit(solution)/shard_map/low_slots/pallas_call | solution.py:278
  354.9 2.6 collective-permute-done.12.back_ref
  357.5 10.9 %low_slots.5 = bf16[160,80,128]{2,1,0:T(8,128)(2,1)} custom-call(s32[1]{0:T(128)} %bitcast.info_ref, s32[160]{0:T(256)S(1)} %dynamic_slice.3.waves_ref, bf16[128,128]{1,0:T(8,128)(2,1)S(1)} %select_convert_fusion.order_ref, bf16[160,80,320]{2,1,0:T(8,128)(2,1)} %table_ref.11, ...), custom_call_target="tpu_custom_call", output_to_operand_aliasing={{}: (8, {})} | custom-call | flops 419430400 | bytes 10485760 | tf_op jit(solution)/shard_map/low_slots/pallas_call | solution.py:278
  (141 shorter events, 35.1 us)
Async XLA Ops:
  20.3 14.6 %all-to-all-start.2 = ((bf16[4,2,2,16,1280]{4,3,2,1,0:T(8,128)(2,1)}), bf16[4,2,2,16,1280]{4,3,2,1,0:T(8,128)(2,1)S(1)}, u32[]{:S(2)}, u32[]{:S(2)}) async-start(bf16[4,2,2,16,1280]{4,3,2,1,0:T(8,128)(2,1)} %zonal.5), calls=%async_computation.2 | async-start | bytes 1310720 | tf_op jit(solution)/shard_map/all_to_all | solution.py:376
  35.0 26.0 %all-to-all-start.1 = ((bf16[4,2,2,32,1280]{4,3,2,1,0:T(8,128)(2,1)}), bf16[4,2,2,32,1280]{4,3,2,1,0:T(8,128)(2,1)S(1)}, u32[]{:S(2)}, u32[]{:S(2)}) async-start(bf16[4,2,2,32,1280]{4,3,2,1,0:T(8,128)(2,1)} %zonal.4), calls=%async_computation.1 | async-start | bytes 2621440 | tf_op jit(solution)/shard_map/all_to_all | solution.py:376
  48.7 29.5 %collective-permute-start.33 = (bf16[16,80,320]{2,1,0:T(8,128)(2,1)}, bf16[16,80,320]{2,1,0:T(8,128)(2,1)}, u32[]{:S(2)}, u32[]{:S(2)}) collective-permute-start(bf16[16,80,320]{2,1,0:T(8,128)(2,1)} %slice.60), channel_id=1, source_target_pairs={{0,2},{1,3},{8,10},{9,11},{16,18},{17,19},{24,26},{25,27}} | collective-permute-start | bytes 2457608 | tf_op jit(solution)/shard_map/ppermute | solution.py:374
  60.9 47.4 %all-to-all-start = ((bf16[4,2,2,32,1280]{4,3,2,1,0:T(8,128)(2,1)}), bf16[4,2,2,32,1280]{4,3,2,1,0:T(8,128)(2,1)S(1)}, u32[]{:S(2)}, u32[]{:S(2)}) async-start(bf16[4,2,2,32,1280]{4,3,2,1,0:T(8,128)(2,1)} %zonal.3), calls=%async_computation | async-start | bytes 2621440 | tf_op jit(solution)/shard_map/all_to_all | solution.py:376
  67.0 16.6 %collective-permute-start.27 = (bf16[16,16,640]{2,1,0:T(8,128)(2,1)S(1)}, bf16[16,16,640]{2,1,0:T(8,128)(2,1)S(1)}, u32[]{:S(2)}, u32[]{:S(2)}) collective-permute-start(bf16[16,16,640]{2,1,0:T(8,128)(2,1)S(1)} %get-tuple-element.25), channel_id=1, source_target_pairs={{0,2},{1,3},{2,4},{3,5},{4,6},{5,7},{8,10},{9,11},{10,12},{11,13},... | collective-permute-start | bytes 983048 | tf_op jit(solution)/shard_map/ppermute | solution.py:303
  68.3 15.9 %collective-permute-start.34 = (bf16[16,16,640]{2,1,0:T(8,128)(2,1)S(1)}, bf16[16,16,640]{2,1,0:T(8,128)(2,1)}, u32[]{:S(2)}, u32[]{:S(2)}) collective-permute-start(bf16[16,16,640]{2,1,0:T(8,128)(2,1)S(1)} %get-tuple-element.26), channel_id=1, source_target_pairs={{4,2},{5,3},{6,4},{7,5},{12,10},{13,11},{14,12},{15,13},{20,18},{2... | collective-permute-start | bytes 983048 | tf_op jit(solution)/shard_map/ppermute | solution.py:301
  73.4 65.5 %copy-start.4 = (bf16[32,16,640]{2,1,0:T(8,128)(2,1)}, bf16[32,16,640]{2,1,0:T(8,128)(2,1)S(1)}, u32[]{:S(2)}) copy-start(bf16[32,16,640]{2,1,0:T(8,128)(2,1)S(1)} %get-tuple-element.21) | copy-start | bytes 1966084
  73.4 40.0 %collective-permute-start.14 = (bf16[32,16,640]{2,1,0:T(8,128)(2,1)S(1)}, bf16[32,16,640]{2,1,0:T(8,128)(2,1)}, u32[]{:S(2)}, u32[]{:S(2)}) collective-permute-start(bf16[32,16,640]{2,1,0:T(8,128)(2,1)S(1)} %get-tuple-element.21), channel_id=1, source_target_pairs={{0,2},{1,3},{2,4},{3,5},{4,6},{5,7},{8,10},{9,11},{10,12},{11,13},... | collective-permute-start | bytes 1966088 | tf_op jit(solution)/shard_map/ppermute | solution.py:303
  76.9 9.4 %collective-permute-start.26 = (bf16[16,16,640]{2,1,0:T(8,128)(2,1)S(1)}, bf16[16,16,640]{2,1,0:T(8,128)(2,1)S(1)}, u32[]{:S(2)}, u32[]{:S(2)}) collective-permute-start(bf16[16,16,640]{2,1,0:T(8,128)(2,1)S(1)} %get-tuple-element.25), channel_id=1, source_target_pairs={{2,0},{3,1},{4,2},{5,3},{6,4},{7,5},{10,8},{11,9},{12,10},{13,11},... | collective-permute-start | bytes 983048 | tf_op jit(solution)/shard_map/ppermute | solution.py:301
  78.2 22.4 %collective-permute-start.36 = (bf16[16,16,640]{2,1,0:T(8,128)(2,1)S(1)}, bf16[16,16,640]{2,1,0:T(8,128)(2,1)}, u32[]{:S(2)}, u32[]{:S(2)}) collective-permute-start(bf16[16,16,640]{2,1,0:T(8,128)(2,1)S(1)} %get-tuple-element.26), channel_id=1, source_target_pairs={{0,2},{1,3},{8,10},{9,11},{16,18},{17,19},{24,26},{25,27}} | collective-permute-start | bytes 983048 | tf_op jit(solution)/shard_map/ppermute | solution.py:303
  83.5 22.5 %collective-permute-start.28 = (bf16[16,16,640]{2,1,0:T(8,128)(2,1)S(1)}, bf16[16,16,640]{2,1,0:T(8,128)(2,1)S(1)}, u32[]{:S(2)}, u32[]{:S(2)}) collective-permute-start(bf16[16,16,640]{2,1,0:T(8,128)(2,1)S(1)} %collective-permute-done.27), channel_id=1, source_target_pairs={{2,4},{3,5},{4,6},{5,7},{10,12},{11,13},{12,14},{13,15},{18,20},{1... | collective-permute-start | bytes 983048 | tf_op jit(solution)/shard_map/ppermute | solution.py:303
  84.2 26.9 %collective-permute-start.35 = (bf16[16,16,640]{2,1,0:T(8,128)(2,1)}, bf16[16,16,640]{2,1,0:T(8,128)(2,1)}, u32[]{:S(2)}, u32[]{:S(2)}) collective-permute-start(bf16[16,16,640]{2,1,0:T(8,128)(2,1)} %collective-permute-done.34), channel_id=1, source_target_pairs={{4,2},{5,3},{12,10},{13,11},{20,18},{21,19},{28,26},{29,27}} | collective-permute-start | bytes 983048 | tf_op jit(solution)/shard_map/ppermute | solution.py:301
  86.3 28.3 %collective-permute-start.13 = (bf16[32,16,640]{2,1,0:T(8,128)(2,1)S(1)}, bf16[32,16,640]{2,1,0:T(8,128)(2,1)}, u32[]{:S(2)}, u32[]{:S(2)}) collective-permute-start(bf16[32,16,640]{2,1,0:T(8,128)(2,1)S(1)} %get-tuple-element.21), channel_id=1, source_target_pairs={{2,0},{3,1},{4,2},{5,3},{6,4},{7,5},{10,8},{11,9},{12,10},{13,11},... | collective-permute-start | bytes 1966088 | tf_op jit(solution)/shard_map/ppermute | solution.py:301
  100.6 20.0 %collective-permute-start.23 = (bf16[32,16,640]{2,1,0:T(8,128)(2,1)}, bf16[32,16,640]{2,1,0:T(8,128)(2,1)}, u32[]{:S(2)}, u32[]{:S(2)}) collective-permute-start(bf16[32,16,640]{2,1,0:T(8,128)(2,1)} %get-tuple-element.22), channel_id=1, source_target_pairs={{0,2},{1,3},{8,10},{9,11},{16,18},{17,19},{24,26},{25,27}} | collective-permute-start | bytes 1966088 | tf_op jit(solution)/shard_map/ppermute | solution.py:303
  106.8 15.4 %collective-permute-start.21 = (bf16[32,16,640]{2,1,0:T(8,128)(2,1)}, bf16[32,16,640]{2,1,0:T(8,128)(2,1)}, u32[]{:S(2)}, u32[]{:S(2)}) collective-permute-start(bf16[32,16,640]{2,1,0:T(8,128)(2,1)} %get-tuple-element.22), channel_id=1, source_target_pairs={{4,2},{5,3},{6,4},{7,5},{12,10},{13,11},{14,12},{15,13},{20,18},{2... | collective-permute-start | bytes 1966088 | tf_op jit(solution)/shard_map/ppermute | solution.py:301
  111.2 20.5 %collective-permute-start.1 = (bf16[32,16,640]{2,1,0:T(8,128)(2,1)S(1)}, bf16[32,16,640]{2,1,0:T(8,128)(2,1)}, u32[]{:S(2)}, u32[]{:S(2)}) collective-permute-start(bf16[32,16,640]{2,1,0:T(8,128)(2,1)S(1)} %get-tuple-element.17), channel_id=1, source_target_pairs={{0,2},{1,3},{2,4},{3,5},{4,6},{5,7},{8,10},{9,11},{10,12},{11,13},... | collective-permute-start | bytes 1966088 | tf_op jit(solution)/shard_map/ppermute | solution.py:303
  113.3 19.8 %collective-permute-start = (bf16[32,16,640]{2,1,0:T(8,128)(2,1)S(1)}, bf16[32,16,640]{2,1,0:T(8,128)(2,1)}, u32[]{:S(2)}, u32[]{:S(2)}) collective-permute-start(bf16[32,16,640]{2,1,0:T(8,128)(2,1)S(1)} %get-tuple-element.17), channel_id=1, source_target_pairs={{2,0},{3,1},{4,2},{5,3},{6,4},{7,5},{10,8},{11,9},{12,10},{13,11},... | collective-permute-start | bytes 1966088 | tf_op jit(solution)/shard_map/ppermute | solution.py:301
  114.7 24.3 %collective-permute-start.8 = (bf16[32,16,640]{2,1,0:T(8,128)(2,1)S(1)}, bf16[32,16,640]{2,1,0:T(8,128)(2,1)S(1)}, u32[]{:S(2)}, u32[]{:S(2)}) collective-permute-start(bf16[32,16,640]{2,1,0:T(8,128)(2,1)S(1)} %get-tuple-element.18), channel_id=1, source_target_pairs={{4,2},{5,3},{6,4},{7,5},{12,10},{13,11},{14,12},{15,13},{20,18},{2... | collective-permute-start | bytes 1966088 | tf_op jit(solution)/shard_map/ppermute | solution.py:301
  120.6 20.5 %collective-permute-start.15 = (bf16[32,16,640]{2,1,0:T(8,128)(2,1)}, bf16[32,16,640]{2,1,0:T(8,128)(2,1)}, u32[]{:S(2)}, u32[]{:S(2)}) collective-permute-start(bf16[32,16,640]{2,1,0:T(8,128)(2,1)} %collective-permute-done.14), channel_id=1, source_target_pairs={{2,4},{3,5},{4,6},{5,7},{10,12},{11,13},{12,14},{13,15},{18,20},{1... | collective-permute-start | bytes 1966088 | tf_op jit(solution)/shard_map/ppermute | solution.py:303
  122.1 35.7 %collective-permute-start.17 = (bf16[32,16,640]{2,1,0:T(8,128)(2,1)}, bf16[32,16,640]{2,1,0:T(8,128)(2,1)}, u32[]{:S(2)}, u32[]{:S(2)}) collective-permute-start(bf16[32,16,640]{2,1,0:T(8,128)(2,1)} %collective-permute-done.13), channel_id=1, source_target_pairs={{2,0},{3,1},{4,2},{5,3},{10,8},{11,9},{12,10},{13,11},{18,16},{19,... | collective-permute-start | bytes 1966088 | tf_op jit(solution)/shard_map/ppermute | solution.py:301
  131.6 28.1 %collective-permute-start.2 = (bf16[32,16,640]{2,1,0:T(8,128)(2,1)}, bf16[32,16,640]{2,1,0:T(8,128)(2,1)}, u32[]{:S(2)}, u32[]{:S(2)}) collective-permute-start(bf16[32,16,640]{2,1,0:T(8,128)(2,1)} %collective-permute-done.1), channel_id=1, source_target_pairs={{2,4},{3,5},{4,6},{5,7},{10,12},{11,13},{12,14},{13,15},{18,20},{1... | collective-permute-start | bytes 1966088 | tf_op jit(solution)/shard_map/ppermute | solution.py:303
  133.1 27.9 %collective-permute-start.4 = (bf16[32,16,640]{2,1,0:T(8,128)(2,1)}, bf16[32,16,640]{2,1,0:T(8,128)(2,1)}, u32[]{:S(2)}, u32[]{:S(2)}) collective-permute-start(bf16[32,16,640]{2,1,0:T(8,128)(2,1)} %collective-permute-done), channel_id=1, source_target_pairs={{2,0},{3,1},{4,2},{5,3},{10,8},{11,9},{12,10},{13,11},{18,16},{19,... | collective-permute-start | bytes 1966088 | tf_op jit(solution)/shard_map/ppermute | solution.py:301
  138.9 24.0 %collective-permute-start.22 = (bf16[32,16,640]{2,1,0:T(8,128)(2,1)}, bf16[32,16,640]{2,1,0:T(8,128)(2,1)S(1)}, u32[]{:S(2)}, u32[]{:S(2)}) collective-permute-start(bf16[32,16,640]{2,1,0:T(8,128)(2,1)} %collective-permute-done.21), channel_id=1, source_target_pairs={{4,2},{5,3},{12,10},{13,11},{20,18},{21,19},{28,26},{29,27}} | collective-permute-start | bytes 1966088 | tf_op jit(solution)/shard_map/ppermute | solution.py:301
  141.2 75.7 %collective-permute-start.10 = (bf16[32,16,640]{2,1,0:T(8,128)(2,1)S(1)}, bf16[32,16,640]{2,1,0:T(8,128)(2,1)S(1)}, u32[]{:S(2)}, u32[]{:S(2)}) collective-permute-start(bf16[32,16,640]{2,1,0:T(8,128)(2,1)S(1)} %get-tuple-element.18), channel_id=1, source_target_pairs={{0,2},{1,3},{8,10},{9,11},{16,18},{17,19},{24,26},{25,27}} | collective-permute-start | bytes 1966088 | tf_op jit(solution)/shard_map/ppermute | solution.py:303
  157.8 60.5 %collective-permute-start.9 = (bf16[32,16,640]{2,1,0:T(8,128)(2,1)S(1)}, bf16[32,16,640]{2,1,0:T(8,128)(2,1)S(1)}, u32[]{:S(2)}, u32[]{:S(2)}) collective-permute-start(bf16[32,16,640]{2,1,0:T(8,128)(2,1)S(1)} %collective-permute-done.8), channel_id=1, source_target_pairs={{4,2},{5,3},{12,10},{13,11},{20,18},{21,19},{28,26},{29,27}} | collective-permute-start | bytes 1966088 | tf_op jit(solution)/shard_map/ppermute | solution.py:301
  159.7 17.0 %collective-permute-start.30 = (bf16[16,16,640]{2,1,0:T(8,128)(2,1)S(1)}, bf16[16,16,640]{2,1,0:T(8,128)(2,1)S(1)}, u32[]{:S(2)}, u32[]{:S(2)}) collective-permute-start(bf16[16,16,640]{2,1,0:T(8,128)(2,1)S(1)} %copy-done.19), channel_id=1, source_target_pairs={{2,0},{3,1},{4,2},{5,3},{10,8},{11,9},{12,10},{13,11},{18,16},{19,... | collective-permute-start | bytes 983048 | tf_op jit(solution)/shard_map/ppermute | solution.py:301
  161.0 59.0 %collective-permute-start.16 = (bf16[32,16,640]{2,1,0:T(8,128)(2,1)}, bf16[32,16,640]{2,1,0:T(8,128)(2,1)S(1)}, u32[]{:S(2)}, u32[]{:S(2)}) collective-permute-start(bf16[32,16,640]{2,1,0:T(8,128)(2,1)} %collective-permute-done.15), channel_id=1, source_target_pairs={{4,6},{5,7},{12,14},{13,15},{20,22},{21,23},{28,30},{29,31}} | collective-permute-start | bytes 1966088 | tf_op jit(solution)/shard_map/ppermute | solution.py:303
  162.9 59.8 %collective-permute-start.3 = (bf16[32,16,640]{2,1,0:T(8,128)(2,1)}, bf16[32,16,640]{2,1,0:T(8,128)(2,1)S(1)}, u32[]{:S(2)}, u32[]{:S(2)}) collective-permute-start(bf16[32,16,640]{2,1,0:T(8,128)(2,1)} %collective-permute-done.2), channel_id=1, source_target_pairs={{4,6},{5,7},{12,14},{13,15},{20,22},{21,23},{28,30},{29,31}} | collective-permute-start | bytes 1966088 | tf_op jit(solution)/shard_map/ppermute | solution.py:303
  163.6 53.2 %copy-start.14 = (bf16[32,80,320]{2,1,0:T(8,128)(2,1)S(1)}, bf16[32,80,320]{2,1,0:T(8,128)(2,1)}, u32[]{:S(2)}) copy-start(bf16[32,80,320]{2,1,0:T(8,128)(2,1)} %get-tuple-element.32) | copy-start | bytes 4915204
  176.8 83.3 %collective-permute-start.20 = (bf16[32,80,320]{2,1,0:T(8,128)(2,1)S(1)}, bf16[32,80,320]{2,1,0:T(8,128)(2,1)S(1)}, u32[]{:S(2)}, u32[]{:S(2)}) collective-permute-start(bf16[32,80,320]{2,1,0:T(8,128)(2,1)S(1)} %copy-done.15), channel_id=1, source_target_pairs={{0,2},{1,3},{8,10},{9,11},{16,18},{17,19},{24,26},{25,27}} | collective-permute-start | bytes 4915208 | tf_op jit(solution)/shard_map/ppermute | solution.py:374
  216.9 82.8 %collective-permute-start.7 = (bf16[32,80,320]{2,1,0:T(8,128)(2,1)S(1)}, bf16[32,80,320]{2,1,0:T(8,128)(2,1)S(1)}, u32[]{:S(2)}, u32[]{:S(2)}) collective-permute-start(bf16[32,80,320]{2,1,0:T(8,128)(2,1)S(1)} %copy-done.14), channel_id=1, source_target_pairs={{0,2},{1,3},{8,10},{9,11},{16,18},{17,19},{24,26},{25,27}} | collective-permute-start | bytes 4915208 | tf_op jit(solution)/shard_map/ppermute | solution.py:374
  218.3 19.8 %collective-permute-start.18 = (bf16[32,16,640]{2,1,0:T(8,128)(2,1)}, bf16[32,16,640]{2,1,0:T(8,128)(2,1)S(1)}, u32[]{:S(2)}, u32[]{:S(2)}) collective-permute-start(bf16[32,16,640]{2,1,0:T(8,128)(2,1)} %collective-permute-done.17), channel_id=1, source_target_pairs={{2,0},{3,1},{10,8},{11,9},{18,16},{19,17},{26,24},{27,25}} | collective-permute-start | bytes 1966088 | tf_op jit(solution)/shard_map/ppermute | solution.py:301
  220.1 32.1 %collective-permute-start.5 = (bf16[32,16,640]{2,1,0:T(8,128)(2,1)}, bf16[32,16,640]{2,1,0:T(8,128)(2,1)S(1)}, u32[]{:S(2)}, u32[]{:S(2)}) collective-permute-start(bf16[32,16,640]{2,1,0:T(8,128)(2,1)} %collective-permute-done.4), channel_id=1, source_target_pairs={{2,0},{3,1},{10,8},{11,9},{18,16},{19,17},{26,24},{27,25}} | collective-permute-start | bytes 1966088 | tf_op jit(solution)/shard_map/ppermute | solution.py:301
  222.7 15.5 %collective-permute-start.29 = (bf16[16,16,640]{2,1,0:T(8,128)(2,1)S(1)}, bf16[16,16,640]{2,1,0:T(8,128)(2,1)S(1)}, u32[]{:S(2)}, u32[]{:S(2)}) collective-permute-start(bf16[16,16,640]{2,1,0:T(8,128)(2,1)S(1)} %copy-done.22), channel_id=1, source_target_pairs={{4,6},{5,7},{12,14},{13,15},{20,22},{21,23},{28,30},{29,31}} | collective-permute-start | bytes 983048 | tf_op jit(solution)/shard_map/ppermute | solution.py:303
  238.1 71.1 %collective-permute-start.24 = (bf16[4,32,16,640]{3,2,1,0:T(8,128)(2,1)S(1)}, bf16[4,32,16,640]{3,2,1,0:T(8,128)(2,1)}, u32[]{:S(2)}, u32[]{:S(2)}) collective-permute-start(bf16[4,32,16,640]{3,2,1,0:T(8,128)(2,1)S(1)} %pad_maximum_fusion.3.mine_ref), channel_id=1, source_target_pairs={{0,1},{1,0},{2,3},{3,2},{4,5},{5,4},{6,7},{7,6},{8,9},{9,8},{10,11... | collective-permute-start | bytes 7864328 | tf_op jit(solution)/shard_map/ppermute | solution.py:380
  238.2 18.3 %collective-permute-start.31 = (bf16[16,16,640]{2,1,0:T(8,128)(2,1)S(1)}, bf16[16,16,640]{2,1,0:T(8,128)(2,1)S(1)}, u32[]{:S(2)}, u32[]{:S(2)}) collective-permute-start(bf16[16,16,640]{2,1,0:T(8,128)(2,1)S(1)} %collective-permute-done.30), channel_id=1, source_target_pairs={{2,0},{3,1},{10,8},{11,9},{18,16},{19,17},{26,24},{27,25}} | collective-permute-start | bytes 983048 | tf_op jit(solution)/shard_map/ppermute | solution.py:301
  252.2 71.3 %collective-permute-start.11 = (bf16[4,32,16,640]{3,2,1,0:T(8,128)(2,1)S(1)}, bf16[4,32,16,640]{3,2,1,0:T(8,128)(2,1)}, u32[]{:S(2)}, u32[]{:S(2)}) collective-permute-start(bf16[4,32,16,640]{3,2,1,0:T(8,128)(2,1)S(1)} %pad_maximum_fusion.1.mine_ref), channel_id=1, source_target_pairs={{0,1},{1,0},{2,3},{3,2},{4,5},{5,4},{6,7},{7,6},{8,9},{9,8},{10,11... | collective-permute-start | bytes 7864328 | tf_op jit(solution)/shard_map/ppermute | solution.py:380
  256.5 45.0 %collective-permute-start.37 = (bf16[4,16,16,640]{3,2,1,0:T(8,128)(2,1)S(1)}, bf16[4,16,16,640]{3,2,1,0:T(8,128)(2,1)S(1)}, u32[]{:S(2)}, u32[]{:S(2)}) collective-permute-start(bf16[4,16,16,640]{3,2,1,0:T(8,128)(2,1)S(1)} %pad_maximum_fusion.5.mine_ref), channel_id=1, source_target_pairs={{0,1},{1,0},{2,3},{3,2},{4,5},{5,4},{6,7},{7,6},{8,9},{9,8},{10,11... | collective-permute-start | bytes 3932168 | tf_op jit(solution)/shard_map/ppermute | solution.py:380
  256.5 43.3 %copy-start.20 = (bf16[16,16,640]{2,1,0:T(8,128)(2,1)S(1)}, bf16[16,16,640]{2,1,0:T(8,128)(2,1)}, u32[]{:S(2)}) copy-start(bf16[16,16,640]{2,1,0:T(8,128)(2,1)} %copy-done.18) | copy-start | bytes 983044
  256.5 43.4 %copy-start.17 = (bf16[16,16,640]{2,1,0:T(8,128)(2,1)S(1)}, bf16[16,16,640]{2,1,0:T(8,128)(2,1)}, u32[]{:S(2)}) copy-start(bf16[16,16,640]{2,1,0:T(8,128)(2,1)} %copy-done.16) | copy-start | bytes 983044
  256.9 43.0 %copy-start.9 = (bf16[16,16,640]{2,1,0:T(8,128)(2,1)S(1)}, bf16[16,16,640]{2,1,0:T(8,128)(2,1)}, u32[]{:S(2)}) copy-start(bf16[16,16,640]{2,1,0:T(8,128)(2,1)} %copy-done.8) | copy-start | bytes 983044
  260.0 41.4 %copy-start.2 = (bf16[32,80,320]{2,1,0:T(8,128)(2,1)}, bf16[32,80,320]{2,1,0:T(8,128)(2,1)S(1)}, u32[]{:S(2)}) copy-start(bf16[32,80,320]{2,1,0:T(8,128)(2,1)S(1)} %collective-permute-done.20.given_ref) | copy-start | bytes 4915204
  260.0 97.5 %collective-permute-start.6 = (bf16[4,32,16,640]{3,2,1,0:T(8,128)(2,1)S(1)}, bf16[4,32,16,640]{3,2,1,0:T(8,128)(2,1)}, u32[]{:S(2)}, u32[]{:S(2)}) collective-permute-start(bf16[4,32,16,640]{3,2,1,0:T(8,128)(2,1)S(1)} %pad_maximum_fusion.mine_ref), channel_id=1, source_target_pairs={{0,1},{1,0},{2,3},{3,2},{4,5},{5,4},{6,7},{7,6},{8,9},{9,8},{10,11... | collective-permute-start | bytes 7864328 | tf_op jit(solution)/shard_map/ppermute | solution.py:383
  299.7 44.3 %collective-permute-start.19 = (bf16[4,32,16,640]{3,2,1,0:T(8,128)(2,1)S(1)}, bf16[4,32,16,640]{3,2,1,0:T(8,128)(2,1)}, u32[]{:S(2)}, u32[]{:S(2)}) collective-permute-start(bf16[4,32,16,640]{3,2,1,0:T(8,128)(2,1)S(1)} %pad_maximum_fusion.2.mine_ref), channel_id=1, source_target_pairs={{0,1},{1,0},{2,3},{3,2},{4,5},{5,4},{6,7},{7,6},{8,9},{9,8},{10,11... | collective-permute-start | bytes 7864328 | tf_op jit(solution)/shard_map/ppermute | solution.py:383
  301.4 35.4 %collective-permute-start.32 = (bf16[4,16,16,640]{3,2,1,0:T(8,128)(2,1)}, bf16[4,16,16,640]{3,2,1,0:T(8,128)(2,1)}, u32[]{:S(2)}, u32[]{:S(2)}) collective-permute-start(bf16[4,16,16,640]{3,2,1,0:T(8,128)(2,1)} %pad_maximum_fusion.4.mine_ref), channel_id=1, source_target_pairs={{0,1},{1,0},{2,3},{3,2},{4,5},{5,4},{6,7},{7,6},{8,9},{9,8},{10,11... | collective-permute-start | bytes 3932168 | tf_op jit(solution)/shard_map/ppermute | solution.py:383
  309.3 26.3 %collective-permute-start.38 = (bf16[16,80,128]{2,1,0:T(8,128)(2,1)}, bf16[16,80,128]{2,1,0:T(8,128)(2,1)}, u32[]{:S(2)}, u32[]{:S(2)}) collective-permute-start(bf16[16,80,128]{2,1,0:T(8,128)(2,1)} %get-tuple-element.28), channel_id=1, source_target_pairs={{2,0},{3,1},{10,8},{11,9},{18,16},{19,17},{26,24},{27,25}} | collective-permute-start | bytes 983048 | tf_op jit(solution)/shard_map/ppermute | solution.py:382
  323.5 20.5 %collective-permute-start.25 = (bf16[32,80,128]{2,1,0:T(8,128)(2,1)}, bf16[32,80,128]{2,1,0:T(8,128)(2,1)S(1)}, u32[]{:S(2)}, u32[]{:S(2)}) collective-permute-start(bf16[32,80,128]{2,1,0:T(8,128)(2,1)} %get-tuple-element.24), channel_id=1, source_target_pairs={{2,0},{3,1},{10,8},{11,9},{18,16},{19,17},{26,24},{27,25}} | collective-permute-start | bytes 1966088 | tf_op jit(solution)/shard_map/ppermute | solution.py:382
  335.5 22.0 %collective-permute-start.12 = (bf16[32,80,128]{2,1,0:T(8,128)(2,1)S(1)}, bf16[32,80,128]{2,1,0:T(8,128)(2,1)S(1)}, u32[]{:S(2)}, u32[]{:S(2)}) collective-permute-start(bf16[32,80,128]{2,1,0:T(8,128)(2,1)S(1)} %get-tuple-element.20), channel_id=1, source_target_pairs={{2,0},{3,1},{10,8},{11,9},{18,16},{19,17},{26,24},{27,25}} | collective-permute-start | bytes 1966088 | tf_op jit(solution)/shard_map/ppermute | solution.py:382
  (17 other events, 280.3 us)

commit v2 on v1

v2 whole, which is shorter than its diff:
```python
import functools
import math

import jax
import jax.numpy as jnp
from jax import lax
from jax.experimental import pallas as pl
from jax.experimental.pallas import tpu as pltpu
from jax.sharding import PartitionSpec as P

LANES = 128
VMEM_LIMIT = 48 * 1024 * 1024
MARK = jax.ShapeDtypeStruct((8, LANES), jnp.float32)
MARK_SPEC = pl.BlockSpec((8, LANES), lambda *_: (0, 0))
ANY = pl.BlockSpec(memory_space=pl.ANY)
SMALL = pl.CostEstimate(flops=1000, bytes_accessed=1000, transcendentals=0)


def dot_nt(a, b):
    return lax.dot_general(a, b, (((1,), (1,)), ((), ())), preferred_element_type=jnp.float32)


def params():
    return pltpu.CompilerParams(vmem_limit_bytes=VMEM_LIMIT)


def hi_lo(x):
    hi = x.astype(jnp.bfloat16)
    return hi, (x - hi.astype(jnp.float32)).astype(jnp.bfloat16)


def build_table(start, count, base_ref, step_ref, table_ref):
    for parity in range(2):
        cos0 = base_ref[parity, 0, start : start + count]
        sin0 = base_ref[parity, 1, start : start + count]
        for b in range(step_ref.shape[3]):
            cos1 = step_ref[parity, 0, start : start + count, b : b + 1]
            sin1 = step_ref[parity, 1, start : start + count, b : b + 1]
            both = (cos0 * cos1 - sin0 * sin1, -(sin0 * cos1 + cos0 * sin1))
            for c, table in enumerate(both):
                for part, term in enumerate(hi_lo(table)):
                    at = (2 * part + c) * count
                    table_ref[parity, at : at + count, b * LANES : (b + 1) * LANES] = term


def transform(start, count, first_ref, table_ref, folded, out_ref):
    groups, _, _, pairs, _ = out_ref.shape
    found = []
    for parity in range(2):
        main = dot_nt(table_ref[parity], folded[2 * parity])
        found.append(
            main[: 2 * count] + (main[2 * count :] + dot_nt(table_ref[parity, : 2 * count], folded[2 * parity + 1]))
        )
    first = first_ref[start : start + count] > 0.5
    for c in range(2):
        even, odd = found[0][c * count : (c + 1) * count], found[1][c * count : (c + 1) * count]
        low = jnp.where(first, even, odd).astype(jnp.bfloat16)
        high = jnp.where(first, odd, even).astype(jnp.bfloat16)
        for g in range(groups):
            out_ref[g, 0, c] = low[g * pairs : (g + 1) * pairs]
            out_ref[g, 1, c] = high[g * pairs : (g + 1) * pairs]


def fold_kernel(start, count, group, base_ref, step_ref, first_ref, order_ref, *refs):
    fields, refs = refs[:group], refs[-7:]
    out_ref, folded_refs, mark_ref, table_ref = refs[0], refs[1:5], refs[5], refs[6]
    mark_ref[...] = jnp.zeros_like(mark_ref)
    rows, half = order_ref.shape[0], folded_refs[0].shape[1]

    @pl.when(pl.program_id(0) == 0)
    def _():
        build_table(start, count, base_ref, step_ref, table_ref)

    for f, grid_ref in enumerate(fields):
        near, far = grid_ref[0, :, :half], grid_ref[0, :, half:]
        for parity, folded in enumerate((near + far, near - far)):
            for part, term in enumerate(hi_lo(folded)):
                moved = jnp.dot(order_ref[...], term, preferred_element_type=jnp.float32)
                folded_refs[2 * parity + part][f * rows : (f + 1) * rows] = moved.astype(jnp.bfloat16)
    transform(start, count, first_ref, table_ref, [ref[...] for ref in folded_refs], out_ref)


def fold_and_zonal(base, step, first, order, grid, groups, start, pairs, after):
    fields, rows, nlon = grid.shape
    half = nlon // 2
    group = 4 if fields % 4 == 0 and 4 * rows % LANES == 0 else fields
    count = groups * pairs
    whole = [pl.BlockSpec(a.shape, lambda n, r=a.ndim: (0,) * r) for a in (base, step, first, order)]
    return pl.pallas_call(
        functools.partial(fold_kernel, start, count, group),
        grid=(fields // group,),
        in_specs=whole
        + [pl.BlockSpec((1, rows, nlon), lambda n, f=f: (n * group + f, 0, 0)) for f in range(group)]
        + [ANY] * len(after),
        out_specs=(
            pl.BlockSpec((groups, 2, 2, pairs, group * rows), lambda n: (0, 0, 0, 0, n)),
            *[pl.BlockSpec((group * rows, half), lambda n: (n, 0))] * 4,
            MARK_SPEC,
        ),
        out_shape=(
            jax.ShapeDtypeStruct((groups, 2, 2, pairs, fields * rows), jnp.bfloat16),
            *[jax.ShapeDtypeStruct((fields * rows, half), jnp.bfloat16)] * 4,
            MARK,
        ),
        scratch_shapes=[pltpu.VMEM((2, 4 * count, half), jnp.bfloat16)],
        compiler_params=params(),
        cost_estimate=SMALL,
        name="fold_and_zonal",
    )(base, step, first, order, *[grid] * group, *after)


def zonal_kernel(start, count, base_ref, step_ref, first_ref, *refs):
    folded, (out_ref, mark_ref, table_ref) = refs[:4], refs[-3:]
    mark_ref[...] = jnp.zeros_like(mark_ref)

    @pl.when(pl.program_id(0) == 0)
    def _():
        build_table(start, count, base_ref, step_ref, table_ref)

    transform(start, count, first_ref, table_ref, [ref[...] for ref in folded], out_ref)


def zonal(base, step, first, folded, groups, start, pairs, after):
    columns, half = folded[0].shape
    block = columns // 5 if columns % (5 * LANES) == 0 else columns
    count = groups * pairs
    whole = [pl.BlockSpec(a.shape, lambda n, r=a.ndim: (0,) * r) for a in (base, step, first)]
    return pl.pallas_call(
        functools.partial(zonal_kernel, start, count),
        grid=(columns // block,),
        in_specs=whole + [pl.BlockSpec((block, half), lambda n: (n, 0))] * 4 + [ANY] * len(after),
        out_specs=(pl.BlockSpec((groups, 2, 2, pairs, block), lambda n: (0, 0, 0, 0, n)), MARK_SPEC),
        out_shape=(jax.ShapeDtypeStruct((groups, 2, 2, pairs, columns), jnp.bfloat16), MARK),
        scratch_shapes=[pltpu.VMEM((2, 4 * count, half), jnp.bfloat16)],
        compiler_params=params(),
        cost_estimate=SMALL,
        name="zonal",
    )(base, step, first, *folded, *after)


def halves_kernel(fields, wide, in_ref, *refs):
    both_ref, again_ref, low_ref, mark_ref, work_ref = refs[-5:]
    mark_ref[...] = jnp.zeros_like(mark_ref)
    groups, _, _, pairs, columns = in_ref.shape
    rows = columns // fields
    for which in range(2):
        for c in range(2):
            parts = [in_ref[g, which, c].astype(jnp.float32) for g in range(groups)]
            sums = [parts[g] + parts[groups - 1 - g] for g in range(groups // 2)]
            gaps = [parts[g] - parts[groups - 1 - g] for g in range(groups // 2)]
            for f in range(fields):
                at = slice(f * rows, (f + 1) * rows)
                even = jnp.concatenate([x[:, at] for x in sums], axis=1)
                odd = jnp.concatenate([x[:, at] for x in gaps], axis=1)
                whole = jnp.concatenate([even[:, :wide], odd[:, :wide], even[:, wide:], odd[:, wide:]], axis=1)
                work_ref[:, c * fields + f, :] = whole
        found = work_ref[...].astype(jnp.bfloat16)
        both_ref[which] = found
        again_ref[which] = found
        if which == 0:
            low_ref[...] = found


def halves(arrived, fields, wide, after):
    groups, _, _, pairs, columns = arrived.shape
    shape = (pairs, 2 * fields, groups * columns // fields)
    return pl.pallas_call(
        functools.partial(halves_kernel, fields, wide),
        out_shape=(
            *[jax.ShapeDtypeStruct((2, *shape), jnp.bfloat16)] * 2,
            jax.ShapeDtypeStruct(shape, jnp.bfloat16),
            MARK,
        ),
        in_specs=[pl.BlockSpec(memory_space=pltpu.VMEM)] + [ANY] * len(after),
        out_specs=(pl.BlockSpec(memory_space=pltpu.VMEM),) * 4,
        scratch_shapes=[pltpu.VMEM(shape, jnp.float32)],
        compiler_params=params(),
        cost_estimate=SMALL,
        name="halves",
    )(arrived, *after)


def contract(table, mine, other, index, wide):
    chips, _, lines, length = mine.shape
    spec = jnp.concatenate(
        [ref[d, index] for d in range(chips) for ref in (mine, other)], axis=0
    )
    half = length // 2
    count = spec.shape[0]
    degrees = table.shape[0]
    even_row = lax.rem(lax.broadcasted_iota(jnp.int32, (degrees, 1), 0), 2) == 0
    main = dot_nt(table[:, :wide], jnp.concatenate([spec[:, :wide], spec[:, wide : 2 * wide]], axis=0))
    total = jnp.where(even_row, main[:, :count], main[:, count:])
    if half > wide:
        rest = table[:, wide:].astype(jnp.float32)
        rest = jnp.concatenate([jnp.where(even_row, rest, 0.0), jnp.where(even_row, 0.0, rest)], axis=1)
        total = total + dot_nt(rest.astype(jnp.bfloat16), spec[:, 2 * wide :])
    return total


def keep_valid(values, first_degree, wave, modes):
    degrees = first_degree + lax.broadcasted_iota(jnp.int32, (values.shape[0], 1), 0)
    return jnp.where(degrees < modes - wave, values, 0.0).astype(jnp.bfloat16)


def column_order(lev_id, sources, lines):
    chips = sources.shape[0]
    fields = lines // 2
    count = 2 * chips * lines
    row = jnp.arange(count, dtype=jnp.int32)
    chip = jnp.repeat(sources, 2 * lines)
    core = (row // lines + lev_id) % 2
    c = row // fields % 2
    target = c * (count // 2) + (2 * chip + core) * fields + row % fields
    return (row[None, :] == target[:, None]).astype(jnp.bfloat16)


def in_order(values, order):
    count, degrees, columns = values.shape
    moved = jnp.dot(values.reshape(count * degrees, columns), order, preferred_element_type=jnp.float32)
    return moved.astype(jnp.bfloat16).reshape(count, degrees, columns)


def high_kernel(start, modes, wide, info_ref, waves_ref, order_ref, table_ref, given_ref, mine_ref, other_ref, *refs):
    own_ref, back_ref, mark_ref, work_ref = refs[-4:]
    mark_ref[...] = jnp.zeros_like(mark_ref)
    pairs, degrees, _ = own_ref.shape
    block = pl.program_id(0)
    lev = info_ref[0]
    for i in range(pairs):
        q = start + block * pairs + i
        swapped = waves_ref[2 * q] > waves_ref[2 * q + 1]
        wave = jnp.maximum(waves_ref[2 * q], waves_ref[2 * q + 1])
        table = table_ref[2 * i + jnp.where(swapped, 0, 1)]
        both = jnp.concatenate([table, unpacked(given_ref[i], *table.shape)], axis=0)
        values = contract(both, mine_ref, other_ref, i, wide)
        work_ref[i] = keep_valid(values[:degrees], lev * degrees, wave, modes)
        work_ref[pairs + i] = keep_valid(values[degrees:], (lev - 2) * degrees, wave, modes)
    own_ref[...] = in_order(work_ref[:pairs], order_ref[...])
    back_ref[...] = in_order(work_ref[pairs:], order_ref[...])


def low_kernel(start, modes, wide, info_ref, waves_ref, order_ref, table_ref, mine_ref, other_ref, own_ref, back_ref, *refs):
    out_ref, mark_ref, work_ref = refs[-3:]
    mark_ref[...] = jnp.zeros_like(mark_ref)
    pairs, degrees, _ = own_ref.shape
    block = pl.program_id(0)
    lev = info_ref[0]
    for i in range(pairs):
        q = start + block * pairs + i
        swapped = waves_ref[2 * q] > waves_ref[2 * q + 1]
        wave = jnp.minimum(waves_ref[2 * q], waves_ref[2 * q + 1])
        table = table_ref[2 * i + jnp.where(swapped, 1, 0)]
        values = contract(table, mine_ref, other_ref, i, wide)
        work_ref[i] = keep_valid(values, lev * degrees, wave, modes)
    found = in_order(work_ref[...], order_ref[...])
    for i in range(pairs):
        q = start + block * pairs + i
        swapped = waves_ref[2 * q] > waves_ref[2 * q + 1]
        out_ref[2 * i + jnp.where(swapped, 1, 0)] = found[i]
        out_ref[2 * i + jnp.where(swapped, 0, 1)] = jnp.where(lev < 2, back_ref[i], own_ref[i])


def legendre_specs(start, block, degrees, half, mine, count):
    chips, _, lines, length = mine.shape
    smem = pl.BlockSpec(memory_space=pltpu.SMEM)
    offset = start // block
    piece = pl.BlockSpec((chips, block, lines, length), lambda i: (0, i, 0, 0))
    return [smem, smem, pl.BlockSpec((count, count), lambda i: (0, 0)),
            pl.BlockSpec((2 * block, degrees, half), lambda i: (offset + i, 0, 0))], piece


def block_pairs(start, pairs):
    for size in (8, 4, 2):
        if start % size == 0 and pairs % size == 0:
            return size
    return pairs if start % pairs == 0 else 1


def high_slots(start, modes, wide, info, waves, order, table, given, mine, other, after):
    _, degrees, half = table.shape
    pairs, *line = given.shape
    count = order.shape[0]
    block = block_pairs(start, pairs)
    shared, piece = legendre_specs(start, block, degrees, half, mine, count)
    result = pl.BlockSpec((block, degrees, count), lambda i: (i, 0, 0))
    shape = jax.ShapeDtypeStruct((pairs, degrees, count), jnp.bfloat16)
    return pl.pallas_call(
        functools.partial(high_kernel, start, modes, wide),
        grid=(pairs // block,),
        in_specs=shared + [pl.BlockSpec((block, *line), lambda i: (i, 0, 0)), piece, piece] + [ANY] * len(after),
        out_specs=(result, result, MARK_SPEC),
        out_shape=(shape, shape, MARK),
        scratch_shapes=[pltpu.VMEM((2 * block, degrees, count), jnp.bfloat16)],
        compiler_params=params(),
        cost_estimate=SMALL,
        name="high_slots",
    )(info, waves, order, table, given, mine, other, *after)


def low_slots(start, modes, wide, info, waves, order, table, mine, other, own, back, out, after):
    pairs, degrees, count = own.shape
    slots, _, half = table.shape
    block = block_pairs(start, pairs)
    offset = start // block
    shared, piece = legendre_specs(start, block, degrees, half, mine, count)
    given = pl.BlockSpec((block, degrees, count), lambda i: (i, 0, 0))
    operands = [info, waves, order, table, mine, other, own, back]
    in_specs = shared + [piece, piece, given, given]
    aliases = {}
    if out is not None:
        aliases = {len(operands): 0}
        operands.append(out)
        in_specs.append(ANY)
    operands += after
    in_specs += [ANY] * len(after)
    return pl.pallas_call(
        functools.partial(low_kernel, start, modes, wide),
        grid=(pairs // block,),
        in_specs=in_specs,
        out_specs=(pl.BlockSpec((2 * block, degrees, count), lambda i: (offset + i, 0, 0)), MARK_SPEC),
        out_shape=(jax.ShapeDtypeStruct((slots, degrees, count), jnp.bfloat16), MARK),
        input_output_aliases=aliases,
        scratch_shapes=[pltpu.VMEM((block, degrees, count), jnp.bfloat16)],
        compiler_params=params(),
        cost_estimate=SMALL,
        name="low_slots",
    )(*operands)


def give_kernel(start, waves_ref, table_ref, *refs):
    out_ref, mark_ref = refs[-2:]
    pairs, lines, _ = out_ref.shape
    degrees, half = table_ref.shape[1:]
    mark_ref[...] = jnp.zeros_like(mark_ref)
    for i in range(pairs):
        q = start + pl.program_id(0) * pairs + i
        table = table_ref[2 * i + jnp.where(waves_ref[2 * q] > waves_ref[2 * q + 1], 0, 1)]
        if lines == degrees:
            out_ref[i] = table
            continue
        whole = half // LANES
        for b in range(whole):
            out_ref[i, b * degrees : (b + 1) * degrees] = table[:, b * LANES : (b + 1) * LANES]
        rest = table[:, whole * LANES :]
        out_ref[i, whole * degrees :] = jnp.concatenate([rest[: degrees // 2], rest[degrees // 2 :]], axis=1)


def packs(degrees, half):
    return half % LANES == LANES // 2 and degrees % 16 == 0


def unpacked(block, degrees, half):
    if not packs(degrees, half):
        return block
    whole = half // LANES
    rest = block[whole * degrees :]
    rest = jnp.concatenate([rest[:, : LANES // 2], rest[:, LANES // 2 :]], axis=0)
    return jnp.concatenate([block[b * degrees : (b + 1) * degrees] for b in range(whole)] + [rest], axis=1)


def give(waves, table, start, pairs, after):
    _, degrees, half = table.shape
    block = block_pairs(start, pairs)
    offset = start // block
    line = (degrees * half // LANES, LANES) if packs(degrees, half) else (degrees, half)
    return pl.pallas_call(
        functools.partial(give_kernel, start),
        grid=(pairs // block,),
        in_specs=[
            pl.BlockSpec(memory_space=pltpu.SMEM),
            pl.BlockSpec((2 * block, degrees, half), lambda i: (offset + i, 0, 0)),
        ] + [ANY] * len(after),
        out_specs=(pl.BlockSpec((block, *line), lambda i: (i, 0, 0)), MARK_SPEC),
        out_shape=(jax.ShapeDtypeStruct((pairs, *line), jnp.bfloat16), MARK),
        compiler_params=params(),
        cost_estimate=SMALL,
        name="give",
    )(waves, table, *after)


def gate_kernel(*refs):
    pass


def gate(arrays, after):
    count = len(arrays)
    found = pl.pallas_call(
        gate_kernel,
        in_specs=[ANY] * (count + len(after)),
        out_specs=(ANY,) * (count + 1),
        out_shape=(*[jax.ShapeDtypeStruct(a.shape, a.dtype) for a in arrays], MARK),
        input_output_aliases={i: i for i in range(count)},
        compiler_params=params(),
        cost_estimate=SMALL,
        name="gate",
    )(*arrays, *after)
    return found[:count], found[count]


def on_cores(chip_pairs):
    return [(2 * a + core, 2 * b + core) for a, b in chip_pairs for core in range(2)]


def send(block, pairs):
    return lax.ppermute(block, "lev", on_cores(pairs))


class Links:
    def __init__(self):
        self.mark = ()

    def send(self, block, pairs, after=()):
        after = tuple(mark for mark in after if mark is not None)
        if self.mark or after:
            (block,), _ = gate([block], (*self.mark, *after))
        (there,), mark = gate([send(block, pairs)], ())
        self.mark = (mark,)
        return block, there, mark


INWARD = [(0, 1), (3, 2)]
CENTRE = [(1, 2), (2, 1)]
OUTWARD = [(1, 0), (2, 3)]
GIVE = [(0, 1)]
RETURN = [(1, 0)]


def chunk_sizes(pairs):
    if pairs % 80 == 0:
        return [pairs // 5, 2 * pairs // 5, 2 * pairs // 5]
    return [pairs]


def laid_out(sizes):
    found, start = [], 0
    for size in sizes:
        found.append((start, size))
        start += size
    return found


def given_parts(sizes):
    beside = [8 * max(3 * size // 32, min(size // 8, 2)) for size in sizes]
    return laid_out([sum(sizes) - sum(beside)] + beside)


def per_device(grid_gradient, legendre, assign):
    fields, rows, nlon = grid_gradient.shape
    modes = nlon // 2
    slots, degrees, half = legendre.shape
    groups = lax.axis_size("lat")
    chips = lax.axis_size("lev") // 2
    lat_id = lax.axis_index("lat")
    lev_id = lax.axis_index("lev")
    z = lev_id // 2
    pairs = slots // 2
    wide = half // 256 * 256 if half >= 256 else half
    lines = 2 * fields
    in_line = chips == 4
    sizes = chunk_sizes(pairs) if in_line else [pairs]
    chunks = laid_out(sizes)
    count = len(chunks)
    assign = assign.astype(jnp.int32)

    by_group = assign.reshape(groups, pairs, 2)
    listed = jnp.concatenate([by_group[:, s : s + n].reshape(groups * n, 2) for s, n in chunks])
    swapped = listed[:, 0] % 2 == 1
    even_wave = jnp.where(swapped, listed[:, 1], listed[:, 0])
    odd_wave = jnp.where(swapped, listed[:, 0], listed[:, 1])
    waves_of = jnp.stack([even_wave, odd_wave])
    first = (even_wave < odd_wave).astype(jnp.float32)[:, None]
    weight = jnp.where(waves_of == 0, 1.0, 2.0).astype(jnp.float32)[:, :, None]
    turn = 2.0 * math.pi / nlon

    def cos_sin(places, scale):
        angle = (waves_of[:, :, None] * places % nlon).astype(jnp.float32) * turn
        return jnp.stack([jnp.cos(angle) * scale, jnp.sin(angle) * scale], axis=1)

    base = cos_sin(jnp.arange(LANES, dtype=jnp.int32), weight)
    step = cos_sin(jnp.arange(0, modes, LANES, dtype=jnp.int32), 1.0)

    here = jnp.arange(rows, dtype=jnp.int32)
    wanted = jnp.where(lat_id >= groups // 2, rows - 1 - here, here)
    row_order = (here[None, :] == wanted[:, None]).astype(jnp.bfloat16)

    waves = lax.dynamic_slice(assign, (lat_id * slots,), (slots,))
    info = jnp.stack([lev_id])
    spec, zonal_mark = [None] * count, [None] * count
    state = {"mark": (), "out": None}

    def do_zonal(i):
        s, n = chunks[i]
        if i == 0:
            found, *state["folded"], mark = fold_and_zonal(
                base, step, first, row_order, grid_gradient, groups, groups * s, n, ()
            )
        else:
            found, mark = zonal(base, step, first, state["folded"], groups, groups * s, n, state["mark"])
        state["mark"] = (mark,)
        zonal_mark[i] = mark
        spec[i] = lax.all_to_all(found, "lat", split_axis=0, concat_axis=0, tiled=True)

    def do_halves(i):
        both, again, low, mark = halves(spec[i], fields, wide, state["mark"])
        state["mark"] = (mark,)
        return both, again, low, mark

    if not in_line:
        do_zonal(0)
        both, _, _, _ = do_halves(0)
        everyone = lax.all_gather(both, "lev", axis=0)
        order = column_order(0, jnp.arange(chips), lines)
        given = jnp.zeros((pairs, degrees, half), jnp.bfloat16)
        own, _, _ = high_slots(
            0, modes, wide, info, waves, order, legendre, given, everyone[0::2, 1], everyone[1::2, 1], ()
        )
        found, _ = low_slots(
            0, modes, wide, info, waves, order, legendre, everyone[0::2, 0], everyone[1::2, 0], own, own, None, ()
        )
        return found

    inner = (z == 1) | (z == 2)
    sources = jnp.array([[0, 1, 2, 3], [1, 0, 2, 3], [2, 3, 1, 0], [3, 2, 1, 0]], jnp.int32)[z]
    order = column_order(lev_id, sources, lines)
    swap = [(i, i ^ 1) for i in range(2 * chips)]
    parts = given_parts(sizes)
    gives = len(parts)
    ready, table, give_mark, table_mark = [[None] * gives for _ in range(4)]
    both, again, low, halves_mark, own, back, low_mark = [[None] * count for _ in range(7)]
    first_in, first_cross, first_out = [[None] * count for _ in range(3)]
    second_cross, second_out = [[None] * count for _ in range(2)]
    out_mark, out2_mark, out3_mark, back_mark = [[None] * count for _ in range(4)]
    inward, centre, outward = Links(), Links(), Links()

    def at(marks, i):
        return marks[i] if 0 <= i < len(marks) else None

    def do_give(i):
        if parts[i][1]:
            ready[i], mark = give(waves, legendre, *parts[i], state["mark"])
            state["mark"] = (mark,)
            give_mark[i] = mark

    def send_table(i):
        if ready[i] is not None:
            _, table[i], table_mark[i] = inward.send(ready[i], GIVE)

    def given_for(i):
        s, n = chunks[i]
        found = []
        for (start, size), block in zip(parts, table):
            low_end, high_end = max(s, start), min(s + n, start + size)
            if low_end < high_end:
                found.append(block[low_end - start : high_end - start])
        return jnp.concatenate(found)

    def send_in(i):
        again[i], first_in[i], _ = inward.send(again[i], INWARD)

    def send_cross(i):
        after = (at(out2_mark, i - 1), at(back_mark, i - 2), at(table_mark, i), at(zonal_mark, i + 1))
        both[i], first_cross[i], _ = centre.send(both[i], CENTRE, after)

    def send_out(i):
        low[i], first_out[i], out_mark[i] = outward.send(low[i], OUTWARD)

    def send_cross2(i):
        after = (at(out_mark, i), at(out3_mark, i - 1), at(low_mark, i - 2))
        if i == 0:
            after += (at(give_mark, 1),)
        else:
            after += (at(give_mark, i + 1), at(halves_mark, i + 1))
        first_in[i], second_cross[i], _ = centre.send(first_in[i], CENTRE, after)

    def send_out2(i):
        _, second_out[i], out2_mark[i] = outward.send(first_cross[i][0], OUTWARD)

    def send_out3(i):
        _, third, out3_mark[i] = outward.send(
            second_cross[i][0], OUTWARD, (at(low_mark, i - 2), at(table_mark, i + 1) if i == count - 1 else None)
        )
        pieces = [low[i]]
        for passed, came in ((first_in, first_out[i]), (first_cross, second_out[i]), (second_cross, third)):
            pieces.append(jnp.where(inner, passed[i][0], came))
        low[i] = jnp.stack(pieces)

    def do_high(i):
        mine = jnp.stack([passed[i][1] for passed in (both, first_in, first_cross, second_cross)])
        own[i], back[i], _ = high_slots(
            chunks[i][0], modes, wide, info, waves, order, legendre, given_for(i), mine,
            lax.ppermute(mine, "lev", swap), (),
        )

    def send_back(i):
        _, back[i], back_mark[i] = outward.send(back[i], RETURN)

    def do_low(i):
        state["out"], low_mark[i] = low_slots(
            chunks[i][0], modes, wide, info, waves, order, legendre, low[i], lax.ppermute(low[i], "lev", swap), own[i],
            back[i], state["out"], (),
        )

    do_zonal(0)
    do_give(0)
    send_table(0)
    if count > 1:
        do_zonal(1)
    both[0], again[0], low[0], halves_mark[0] = do_halves(0)
    send_in(0)
    send_cross(0)
    send_out(0)
    for i in range(count):
        do_give(i + 1)
        send_table(i + 1)
        if i + 1 < count:
            both[i + 1], again[i + 1], low[i + 1], halves_mark[i + 1] = do_halves(i + 1)
        if i + 2 < count:
            do_zonal(i + 2)
        send_out2(i)
        if i + 1 < count:
            send_in(i + 1)
        if i > 0:
            do_high(i - 1)
            send_back(i - 1)
            do_low(i - 1)
        send_cross2(i)
        if i + 1 < count:
            send_cross(i + 1)
        send_out3(i)
        if i + 1 < count:
            send_out(i + 1)
    do_high(count - 1)
    send_back(count - 1)
    do_low(count - 1)
    return state["out"]


def solution(mesh):
    in_specs = (P("lev", "lat", None), P("lat", "lev", None), P())
    out_specs = P("lat", "lev", None)
    return jax.shard_map(
        per_device, mesh=mesh, in_specs=in_specs, out_specs=out_specs, check_vma=False
    )
```

time: 370 us -> 295 us (0.80)
  starting transfers between devices: 122 us -> 73.3 us
  waiting for transfers between devices: 116 us -> 90.8 us
  Pallas kernels: 97.3 us -> 80.3 us
  local copies, waits for them, and re-layouts: 12.3 us -> 28.6 us
    ppermute x39 -> x31, starting transfers between devices: 109 us -> 60.6 us  [the longest x25 60.2 us: send(): return lax.ppermute(block, 'lev', on_cores(pairs))]
    ppermute x39 -> x31, waiting for transfers between devices: 114 us -> 90 us  [the longest x25 90 us: send(): return lax.ppermute(block, 'lev', on_cores(pairs))]
    pallas_call x3, Pallas kernels: 28.4 us -> 15.7 us  [low_slots(): pl.pallas_call(functools.partial(low_kernel, start, modes, wide), grid=(p...]
    pallas_call x3, Pallas kernels: 28.3 us -> 16.4 us  [high_slots(): pl.pallas_call(functools.partial(high_kernel, start, modes, wide), grid=(...]
    unnamed x46 -> x72, local copies, waits for them, and re-layouts: 3.08 us -> 12.2 us
    pallas_call x3, Pallas kernels: 8.43 us -> 15.5 us  [halves(): pl.pallas_call(functools.partial(halves_kernel, fields, wide), out_shape=...]
    slice x4 -> x14, local copies, waits for them, and re-layouts: 7.06 us -> 14.1 us  [the longest x12 13 us: do_high(): passed[i][1]]
    select_n x2 -> x1, other arithmetic: 6.81 us -> 0.01 us  [per_device(): weight = jnp.where(waves_of == 0, 1.0, 2.0).astype(jnp.float32)[:, :, None]]
  transfers between devices with their start and end apart: 42 -> 34, of which waited for: 13 -> 13; matrix products, arithmetic and copies ran while one was open for 7% -> 10% of each run, Pallas kernels for 19% -> 22%
where the time goes in v2:
time: 295 us; the launch traced here: 293 us
  waiting for transfers between devices  90.8 us (31%)
  Pallas kernels  80.3 us (27%)
  starting transfers between devices  73.3 us (25%)
  local copies, waits for them, and re-layouts  28.6 us (10%)
  other arithmetic  18.7 us (6%)
    ppermute x25, waiting for transfers between devices, send(): return lax.ppermute(block, 'lev', on_cores(pairs))  90 us
    ppermute x25, starting transfers between devices, send(): return lax.ppermute(block, 'lev', on_cores(pairs))  60.2 us
    pallas_call x3, Pallas kernels, high_slots(): pl.pallas_call(functools.partial(high_kernel, start, modes, wide), grid=(...  16.4 us
    pallas_call x3, Pallas kernels, low_slots(): pl.pallas_call(functools.partial(low_kernel, start, modes, wide), grid=(p...  15.7 us
    pallas_call x3, Pallas kernels, halves(): pl.pallas_call(functools.partial(halves_kernel, fields, wide), out_shape=...  15.5 us
    slice x12, local copies, waits for them, and re-layouts, do_high(): passed[i][1]  13 us
    all_to_all x3, starting transfers between devices, do_zonal(): lax.all_to_all(found, 'lat', split_axis=0, concat_axis=0, tiled=True)  12.8 us
    pallas_call x2, Pallas kernels, zonal(): pl.pallas_call(functools.partial(zonal_kernel, start, count), grid=(colum...  12.4 us
  transfers between devices with their start and end apart: 34, of which 13 were waited for; matrix products, arithmetic and copies ran while one was open for 10% of the time, Pallas kernels for 22%

profile of v2, /device:TPU:0, one launch (start us, length us, event | category | flops | bytes accessed | tf_op | source)
XLA Modules:
  0.0 292.8 jit_solution(187374380639635361)
XLA Ops:
  4.6 8.2 %fold_and_zonal.1 = (bf16[4,2,2,16,1280]{4,3,2,1,0:T(8,128)(2,1)S(1)}, bf16[1280,640]{1,0:T(8,128)(2,1)S(1)}, bf16[1280,640]{1,0:T(8,128)(2,1)S(1)}, bf16[1280,6...) custom-call(f32[2,2,320,128]{3,2,1,0:T(8,128)S(1)} %pad_maximum_fusion.8.base_ref, ...), custom_call_target="tpu_custom_call" | custom-call | flops 1000 | bytes 1000 | tf_op jit(solution)/shard_map/fold_and_zonal/pallas_call | solution.py:89
  13.7 3.0 %give.4 = (bf16[16,200,128]{2,1,0:T(8,128)(2,1)}, f32[8,128]{1,0:T(8,128)S(1)}) custom-call(s32[160]{0:T(256)S(1)} %dynamic_slice.6.waves_ref, bf16[160,80,320]{2,1,0:T(8,128)(2,1)} %table_ref.19, f32[8,128]{1,0:T(8,128)S(1)} %get-tuple-element.120.refs_0_), custom_call_target="tpu_custom_call" | custom-call | flops 1000 | bytes 1000 | tf_op jit(solution)/shard_map/give/pallas_call | solution.py:367
  16.7 5.8 %collective-permute-start = (bf16[16,200,128]{2,1,0:T(8,128)(2,1)}, bf16[16,200,128]{2,1,0:T(8,128)(2,1)}, u32[]{:S(2)}, u32[]{:S(2)}) collective-permute-start(bf16[16,200,128]{2,1,0:T(8,128)(2,1)} %get-tuple-element.135), channel_id=1, source_target_pairs={{0,2},{1,3},{8,10},{9,11},{16,18},{17,19},{24,26},{25,27}} | collective-permute-start | bytes 2457608 | tf_op jit(solution)/shard_map/ppermute | solution.py:406
  22.5 4.2 %all-to-all-start.1 = ((bf16[4,2,2,16,1280]{4,3,2,1,0:T(8,128)(2,1)}), bf16[4,2,2,16,1280]{4,3,2,1,0:T(8,128)(2,1)}, u32[]{:S(2)}, u32[]{:S(2)}) async-start(bf16[4,2,2,16,1280]{4,3,2,1,0:T(8,128)(2,1)} %copy-done.27), calls=%async_computation.1 | async-start | bytes 1310720 | tf_op jit(solution)/shard_map/all_to_all | solution.py:502
  28.1 6.2 %zonal.2 = (bf16[4,2,2,32,1280]{4,3,2,1,0:T(8,128)(2,1)S(1)}, f32[8,128]{1,0:T(8,128)S(1)}) custom-call(f32[2,2,320,128]{3,2,1,0:T(8,128)S(1)} %pad_maximum_fusion.8.base_ref, f32[2,2,320,5]{3,2,1,0:T(8,128)S(1)} %copy.72.step_ref, f32[320,1]{1,0:T(8,128)S(1)} %fusion.10.first_ref, bf16[1280,640]{1,0:T(8,128)(2,1)S(1)} %get-tuple-element.116.refs_0_, ...), custom_call_target="tpu_custom_call" | custom-call | flops 1000 | bytes 1000 | tf_op jit(solution)/shard_map/zonal/pallas_call | solution.py:128
  36.1 4.1 %halves.3 = (bf16[2,16,16,640]{3,2,1,0:T(8,128)(2,1)}, bf16[2,16,16,640]{3,2,1,0:T(8,128)(2,1)}, bf16[16,16,640]{2,1,0:T(8,128)(2,1)}, f32[8,128]{1,0:T(8,128)S(1)}) custom-call(bf16[4,2,2,16,1280]{4,3,2,1,0:T(8,128)(2,1)} %all-to-all-done.1.in_ref, f32[8,128]{1,0:T(8,128)S(1)} %get-tuple-element.124.refs_0_.refs_2_), custom_call_target="tpu_custom_call" | custom-call | flops 1000 | bytes 1000 | tf_op jit(solution)/shard_map/halves/pallas_call | solution.py:167
  40.3 4.3 %collective-permute-start.1 = (bf16[2,16,16,640]{3,2,1,0:T(8,128)(2,1)}, bf16[2,16,16,640]{3,2,1,0:T(8,128)(2,1)}, u32[]{:S(2)}, u32[]{:S(2)}) collective-permute-start(bf16[2,16,16,640]{3,2,1,0:T(8,128)(2,1)} %get-tuple-element.137), channel_id=1, source_target_pairs={{0,2},{1,3},{6,4},{7,5},{8,10},{9,11},{14,12},{15,13},{16,18},{17,... | collective-permute-start | bytes 1966088 | tf_op jit(solution)/shard_map/ppermute | solution.py:406
  44.6 1.5 collective-permute-start.4
  47.4 4.3 %all-to-all-start = ((bf16[4,2,2,32,1280]{4,3,2,1,0:T(8,128)(2,1)}), bf16[4,2,2,32,1280]{4,3,2,1,0:T(8,128)(2,1)}, u32[]{:S(2)}, u32[]{:S(2)}) async-start(bf16[4,2,2,32,1280]{4,3,2,1,0:T(8,128)(2,1)} %copy-done.24), calls=%async_computation | async-start | bytes 2621440 | tf_op jit(solution)/shard_map/all_to_all | solution.py:502
  51.8 2.4 give.5
  54.2 3.0 %collective-permute-done.1.refs_0_ = bf16[2,16,16,640]{3,2,1,0:T(8,128)(2,1)} collective-permute-done((bf16[2,16,16,640]{3,2,1,0:T(8,128)(2,1)}, bf16[2,16,16,640]{3,2,1,0:T(8,128)(2,1)}, u32[]{:S(2)}, u32[]{:S(2)}) %collective-permute-start.1) | collective-permute-done | bytes 655392 | tf_op jit(solution)/shard_map/ppermute | solution.py:406
  57.2 5.3 %collective-permute-start.2 = (bf16[16,200,128]{2,1,0:T(8,128)(2,1)}, bf16[16,200,128]{2,1,0:T(8,128)(2,1)}, u32[]{:S(2)}, u32[]{:S(2)}) collective-permute-start(bf16[16,200,128]{2,1,0:T(8,128)(2,1)} %get-tuple-element.139), channel_id=1, source_target_pairs={{0,2},{1,3},{8,10},{9,11},{16,18},{17,19},{24,26},{25,27}} | collective-permute-start | bytes 2457608 | tf_op jit(solution)/shard_map/ppermute | solution.py:406
  62.5 1.5 collective-permute-start.6
  64.0 2.0 fusion.31
  67.4 6.0 %halves.4 = (bf16[2,32,16,640]{3,2,1,0:T(8,128)(2,1)}, bf16[2,32,16,640]{3,2,1,0:T(8,128)(2,1)}, bf16[32,16,640]{2,1,0:T(8,128)(2,1)}, f32[8,128]{1,0:T(8,128)S(1)}) custom-call(bf16[4,2,2,32,1280]{4,3,2,1,0:T(8,128)(2,1)} %all-to-all-done.in_ref, f32[8,128]{1,0:T(8,128)S(1)} %get-tuple-element.126.refs_0_.refs_3_), custom_call_target="tpu_custom_call" | custom-call | flops 1000 | bytes 1000 | tf_op jit(solution)/shard_map/halves/pallas_call | solution.py:167
  74.8 6.2 %zonal.3 = (bf16[4,2,2,32,1280]{4,3,2,1,0:T(8,128)(2,1)S(1)}, f32[8,128]{1,0:T(8,128)S(1)}) custom-call(f32[2,2,320,128]{3,2,1,0:T(8,128)S(1)} %pad_maximum_fusion.8.base_ref, f32[2,2,320,5]{3,2,1,0:T(8,128)S(1)} %copy.72.step_ref, f32[320,1]{1,0:T(8,128)S(1)} %fusion.10.first_ref, bf16[1280,640]{1,0:T(8,128)(2,1)S(1)} %get-tuple-element.116.refs_0_, ...), custom_call_target="tpu_custom_call" | custom-call | flops 1000 | bytes 1000 | tf_op jit(solution)/shard_map/zonal/pallas_call | solution.py:128
  82.1 4.6 %collective-permute-start.3 = (bf16[2,32,16,640]{3,2,1,0:T(8,128)(2,1)}, bf16[2,32,16,640]{3,2,1,0:T(8,128)(2,1)S(1)}, u32[]{:S(2)}, u32[]{:S(2)}) collective-permute-start(bf16[2,32,16,640]{3,2,1,0:T(8,128)(2,1)} %get-tuple-element.141), channel_id=1, source_target_pairs={{0,2},{1,3},{6,4},{7,5},{8,10},{9,11},{14,12},{15,13},{16,18},{17,... | collective-permute-start | bytes 3932168 | tf_op jit(solution)/shard_map/ppermute | solution.py:406
  87.5 4.3 %all-to-all-start.2 = ((bf16[4,2,2,32,1280]{4,3,2,1,0:T(8,128)(2,1)}), bf16[4,2,2,32,1280]{4,3,2,1,0:T(8,128)(2,1)}, u32[]{:S(2)}, u32[]{:S(2)}) async-start(bf16[4,2,2,32,1280]{4,3,2,1,0:T(8,128)(2,1)} %copy-done.23), calls=%async_computation.2 | async-start | bytes 2621440 | tf_op jit(solution)/shard_map/all_to_all | solution.py:502
  91.8 1.9 fusion.32
  93.7 1.5 collective-permute-start.9
  95.1 8.5 %collective-permute-done.9.refs_0_ = bf16[16,16,640]{2,1,0:T(8,128)(2,1)S(1)} collective-permute-done((bf16[16,16,640]{2,1,0:T(8,128)(2,1)S(1)}, bf16[16,16,640]{2,1,0:T(8,128)(2,1)S(1)}, u32[]{:S(2)}, u32[]{:S(2)}) %collective-permute-start.9) | collective-permute-done | bytes 327712 | tf_op jit(solution)/shard_map/ppermute | solution.py:406
  105.7 1.8 slice.101
  107.5 2.7 give.6
  111.3 1.8 slice.102
  113.0 5.4 %halves.5 = (bf16[2,32,16,640]{3,2,1,0:T(8,128)(2,1)S(1)}, bf16[2,32,16,640]{3,2,1,0:T(8,128)(2,1)}, bf16[32,16,640]{2,1,0:T(8,128)(2,1)S(1)}, f32[8,128]{1,0:T(8,128)S(1)}) custom-call(bf16[4,2,2,32,1280]{4,3,2,1,0:T(8,128)(2,1)} %all-to-all-done.2.in_ref, f32[8,128]{1,0:T(8,128)S(1)} %get-tuple-element.130.refs_0_.refs_4_), custom_call_target="tpu_custom_call" | custom-call | flops 1000 | bytes 1000 | tf_op jit(solution)/shard_map/halves/pallas_call | solution.py:167
  118.4 2.9 pad_maximum_fusion.6.mine_ref
  121.4 1.8 collective-permute-start.11
  125.8 5.9 %collective-permute-start.16 = (bf16[24,200,128]{2,1,0:T(8,128)(2,1)S(1)}, bf16[24,200,128]{2,1,0:T(8,128)(2,1)S(1)}, u32[]{:S(2)}, u32[]{:S(2)}) collective-permute-start(bf16[24,200,128]{2,1,0:T(8,128)(2,1)S(1)} %get-tuple-element.179), channel_id=1, source_target_pairs={{0,2},{1,3},{8,10},{9,11},{16,18},{17,19},{24,26},{25,27}} | collective-permute-start | bytes 3686408 | tf_op jit(solution)/shard_map/ppermute | solution.py:406
  134.9 4.0 %high_slots.3 = (bf16[16,80,128]{2,1,0:T(8,128)(2,1)S(1)}, bf16[16,80,128]{2,1,0:T(8,128)(2,1)S(1)}, f32[8,128]{1,0:T(8,128)}) custom-call(s32[1]{0:T(128)} %bitcast.info_ref, s32[160]{0:T(256)S(1)} %dynamic_slice.6.waves_ref, bf16[128,128]{1,0:T(8,128)(2,1)S(1)} %fusion.13.order_ref, bf16[160,80,320]{2,1,0:T(8,128)(2,1)} %table_ref.19, ...), custom_call_target="tpu_custom_call" | custom-call | flops 1000 | bytes 1000 | tf_op jit(solution)/shard_map/high_slots/pallas_call | solution.py:288
  139.0 5.6 %collective-permute-done.13.refs_0_ = bf16[32,16,640]{2,1,0:T(8,128)(2,1)S(1)} collective-permute-done((bf16[32,16,640]{2,1,0:T(8,128)(2,1)S(1)}, bf16[32,16,640]{2,1,0:T(8,128)(2,1)S(1)}, u32[]{:S(2)}, u32[]{:S(2)}) %collective-permute-start.13) | collective-permute-done | bytes 655392 | tf_op jit(solution)/shard_map/ppermute | solution.py:406
  150.6 5.2 %collective-permute-done.14.refs_0_ = bf16[16,80,128]{2,1,0:T(8,128)(2,1)S(1)} collective-permute-done((bf16[16,80,128]{2,1,0:T(8,128)(2,1)S(1)}, bf16[16,80,128]{2,1,0:T(8,128)(2,1)S(1)}, u32[]{:S(2)}, u32[]{:S(2)}) %collective-permute-start.14) | collective-permute-done | bytes 327712 | tf_op jit(solution)/shard_map/ppermute | solution.py:406
  155.9 2.4 collective-permute-done.16.refs_0_
  159.3 6.5 %collective-permute-start.17 = (bf16[2,32,16,640]{3,2,1,0:T(8,128)(2,1)}, bf16[2,32,16,640]{3,2,1,0:T(8,128)(2,1)S(1)}, u32[]{:S(2)}, u32[]{:S(2)}) collective-permute-start(bf16[2,32,16,640]{3,2,1,0:T(8,128)(2,1)} %get-tuple-element.181), channel_id=1, source_target_pairs={{0,2},{1,3},{6,4},{7,5},{8,10},{9,11},{14,12},{15,13},{16,18},{17,... | collective-permute-start | bytes 3932168 | tf_op jit(solution)/shard_map/ppermute | solution.py:406
  167.9 16.6 %collective-permute-done.15.refs_0_ = bf16[32,16,640]{2,1,0:T(8,128)(2,1)S(1)} collective-permute-done((bf16[32,16,640]{2,1,0:T(8,128)(2,1)S(1)}, bf16[32,16,640]{2,1,0:T(8,128)(2,1)S(1)}, u32[]{:S(2)}, u32[]{:S(2)}) %collective-permute-start.15) | collective-permute-done | bytes 655392 | tf_op jit(solution)/shard_map/ppermute | solution.py:406
  185.9 3.8 %give.7 = (bf16[24,200,128]{2,1,0:T(8,128)(2,1)}, f32[8,128]{1,0:T(8,128)S(1)}) custom-call(s32[160]{0:T(256)S(1)} %dynamic_slice.6.waves_ref, bf16[160,80,320]{2,1,0:T(8,128)(2,1)} %table_ref.19, f32[8,128]{1,0:T(8,128)S(1)} %get-tuple-element.163.refs_5_.refs_0_), custom_call_target="tpu_custom_call" | custom-call | flops 1000 | bytes 1000 | tf_op jit(solution)/shard_map/give/pallas_call | solution.py:367
  189.8 3.5 %low_slots.3 = (bf16[160,80,128]{2,1,0:T(8,128)(2,1)}, f32[8,128]{1,0:T(8,128)S(1)}) custom-call(s32[1]{0:T(128)} %bitcast.info_ref, s32[160]{0:T(256)S(1)} %dynamic_slice.6.waves_ref, bf16[128,128]{1,0:T(8,128)(2,1)S(1)} %fusion.13.order_ref, bf16[160,80,320]{2,1,0:T(8,128)(2,1)} %table_ref.19, bf16[4,16,16,640]{3,2,1,0:T(8,128)(2,1)S(1)} %pad_maximum_fusion.7.mine_ref, ...), custom_call_target="tpu_custom_call" | custom-call | flops 1000 | bytes 1000 | tf_op jit(solution)/shard_map/low_slots/pallas_call | solution.py:317
  194.6 4.3 %collective-permute-start.25 = (bf16[24,200,128]{2,1,0:T(8,128)(2,1)}, bf16[24,200,128]{2,1,0:T(8,128)(2,1)S(1)}, u32[]{:S(2)}, u32[]{:S(2)}) collective-permute-start(bf16[24,200,128]{2,1,0:T(8,128)(2,1)} %get-tuple-element.209), channel_id=1, source_target_pairs={{0,2},{1,3},{8,10},{9,11},{16,18},{17,19},{24,26},{25,27}} | collective-permute-start | bytes 3686408 | tf_op jit(solution)/shard_map/ppermute | solution.py:406
  199.0 3.5 %collective-permute-done.19.refs_0_ = bf16[32,16,640]{2,1,0:T(8,128)(2,1)S(1)} collective-permute-done((bf16[32,16,640]{2,1,0:T(8,128)(2,1)S(1)}, bf16[32,16,640]{2,1,0:T(8,128)(2,1)S(1)}, u32[]{:S(2)}, u32[]{:S(2)}) %collective-permute-start.19) | collective-permute-done | bytes 655392 | tf_op jit(solution)/shard_map/ppermute | solution.py:406
  211.5 10.7 %collective-permute-done.21.refs_0_ = bf16[32,16,640]{2,1,0:T(8,128)(2,1)S(1)} collective-permute-done((bf16[32,16,640]{2,1,0:T(8,128)(2,1)S(1)}, bf16[32,16,640]{2,1,0:T(8,128)(2,1)S(1)}, u32[]{:S(2)}, u32[]{:S(2)}) %collective-permute-start.21) | collective-permute-done | bytes 655392 | tf_op jit(solution)/shard_map/ppermute | solution.py:406
  222.2 6.2 %high_slots.4 = (bf16[32,80,128]{2,1,0:T(8,128)(2,1)S(1)}, bf16[32,80,128]{2,1,0:T(8,128)(2,1)S(1)}, f32[8,128]{1,0:T(8,128)}) custom-call(s32[1]{0:T(128)} %bitcast.info_ref, s32[160]{0:T(256)S(1)} %dynamic_slice.6.waves_ref, bf16[128,128]{1,0:T(8,128)(2,1)S(1)} %fusion.13.order_ref, bf16[160,80,320]{2,1,0:T(8,128)(2,1)} %table_ref.19, ...), custom_call_target="tpu_custom_call" | custom-call | flops 1000 | bytes 1000 | tf_op jit(solution)/shard_map/high_slots/pallas_call | solution.py:288
  230.9 1.5 pad_maximum_fusion.3.mine_ref
  233.5 11.0 %collective-permute-done.24.refs_0_ = bf16[32,80,128]{2,1,0:T(8,128)(2,1)S(1)} collective-permute-done((bf16[32,80,128]{2,1,0:T(8,128)(2,1)S(1)}, bf16[32,80,128]{2,1,0:T(8,128)(2,1)S(1)}, u32[]{:S(2)}, u32[]{:S(2)}) %collective-permute-start.24) | collective-permute-done | bytes 655392 | tf_op jit(solution)/shard_map/ppermute | solution.py:406
  244.5 1.6 collective-permute-start.26
  249.3 10.4 %collective-permute-done.26.refs_0_ = bf16[32,16,640]{2,1,0:T(8,128)(2,1)S(1)} collective-permute-done((bf16[32,16,640]{2,1,0:T(8,128)(2,1)S(1)}, bf16[32,16,640]{2,1,0:T(8,128)(2,1)S(1)}, u32[]{:S(2)}, u32[]{:S(2)}) %collective-permute-start.26) | collective-permute-done | bytes 655392 | tf_op jit(solution)/shard_map/ppermute | solution.py:406
  261.5 6.2 %high_slots.5 = (bf16[32,80,128]{2,1,0:T(8,128)(2,1)S(1)}, bf16[32,80,128]{2,1,0:T(8,128)(2,1)S(1)}, f32[8,128]{1,0:T(8,128)}) custom-call(s32[1]{0:T(128)} %bitcast.info_ref, s32[160]{0:T(256)S(1)} %dynamic_slice.6.waves_ref, bf16[128,128]{1,0:T(8,128)(2,1)S(1)} %fusion.13.order_ref, bf16[160,80,320]{2,1,0:T(8,128)(2,1)} %table_ref.19, ...), custom_call_target="tpu_custom_call" | custom-call | flops 1000 | bytes 1000 | tf_op jit(solution)/shard_map/high_slots/pallas_call | solution.py:288
  269.0 6.1 %low_slots.4 = (bf16[160,80,128]{2,1,0:T(8,128)(2,1)}, f32[8,128]{1,0:T(8,128)}) custom-call(s32[1]{0:T(128)} %bitcast.info_ref, s32[160]{0:T(256)S(1)} %dynamic_slice.6.waves_ref, bf16[128,128]{1,0:T(8,128)(2,1)S(1)} %fusion.13.order_ref, bf16[160,80,320]{2,1,0:T(8,128)(2,1)} %table_ref.19, ...), custom_call_target="tpu_custom_call", output_to_operand_aliasing={{0}: (8, {})} | custom-call | flops 1000 | bytes 1000 | tf_op jit(solution)/shard_map/low_slots/pallas_call | solution.py:317
  275.1 11.6 %collective-permute-done.29.refs_0_ = bf16[32,80,128]{2,1,0:T(8,128)(2,1)S(1)} collective-permute-done((bf16[32,80,128]{2,1,0:T(8,128)(2,1)S(1)}, bf16[32,80,128]{2,1,0:T(8,128)(2,1)S(1)}, u32[]{:S(2)}, u32[]{:S(2)}) %collective-permute-start.29) | collective-permute-done | bytes 655392 | tf_op jit(solution)/shard_map/ppermute | solution.py:406
  286.7 6.1 %low_slots.5 = (bf16[160,80,128]{2,1,0:T(8,128)(2,1)}, f32[8,128]{1,0:T(8,128)}) custom-call(s32[1]{0:T(128)} %bitcast.info_ref, s32[160]{0:T(256)S(1)} %dynamic_slice.6.waves_ref, bf16[128,128]{1,0:T(8,128)(2,1)S(1)} %fusion.13.order_ref, bf16[160,80,320]{2,1,0:T(8,128)(2,1)} %table_ref.19, ...), custom_call_target="tpu_custom_call", output_to_operand_aliasing={{0}: (8, {})} | custom-call | flops 1000 | bytes 1000 | tf_op jit(solution)/shard_map/low_slots/pallas_call | solution.py:317
  (210 shorter events, 53.7 us)
Async XLA Ops:
  13.7 3.0 %copy-start.2 = (bf16[1280,640]{1,0:T(8,128)(2,1)}, bf16[1280,640]{1,0:T(8,128)(2,1)S(1)}, u32[]{:S(2)}) copy-start(bf16[1280,640]{1,0:T(8,128)(2,1)S(1)} %get-tuple-element.117.refs_1_) | copy-start | bytes 4915204
  16.7 23.6 %collective-permute-start = (bf16[16,200,128]{2,1,0:T(8,128)(2,1)}, bf16[16,200,128]{2,1,0:T(8,128)(2,1)}, u32[]{:S(2)}, u32[]{:S(2)}) collective-permute-start(bf16[16,200,128]{2,1,0:T(8,128)(2,1)} %get-tuple-element.135), channel_id=1, source_target_pairs={{0,2},{1,3},{8,10},{9,11},{16,18},{17,19},{24,26},{25,27}} | collective-permute-start | bytes 2457608 | tf_op jit(solution)/shard_map/ppermute | solution.py:406
  22.5 13.6 %all-to-all-start.1 = ((bf16[4,2,2,16,1280]{4,3,2,1,0:T(8,128)(2,1)}), bf16[4,2,2,16,1280]{4,3,2,1,0:T(8,128)(2,1)}, u32[]{:S(2)}, u32[]{:S(2)}) async-start(bf16[4,2,2,16,1280]{4,3,2,1,0:T(8,128)(2,1)} %copy-done.27), calls=%async_computation.1 | async-start | bytes 1310720 | tf_op jit(solution)/shard_map/all_to_all | solution.py:502
  40.3 16.9 %collective-permute-start.1 = (bf16[2,16,16,640]{3,2,1,0:T(8,128)(2,1)}, bf16[2,16,16,640]{3,2,1,0:T(8,128)(2,1)}, u32[]{:S(2)}, u32[]{:S(2)}) collective-permute-start(bf16[2,16,16,640]{3,2,1,0:T(8,128)(2,1)} %get-tuple-element.137), channel_id=1, source_target_pairs={{0,2},{1,3},{6,4},{7,5},{8,10},{9,11},{14,12},{15,13},{16,18},{17,... | collective-permute-start | bytes 1966088 | tf_op jit(solution)/shard_map/ppermute | solution.py:406
  44.6 17.9 %collective-permute-start.4 = (bf16[2,16,16,640]{3,2,1,0:T(8,128)(2,1)}, bf16[2,16,16,640]{3,2,1,0:T(8,128)(2,1)}, u32[]{:S(2)}, u32[]{:S(2)}) collective-permute-start(bf16[2,16,16,640]{3,2,1,0:T(8,128)(2,1)} %get-tuple-element.146), channel_id=1, source_target_pairs={{2,4},{3,5},{4,2},{5,3},{10,12},{11,13},{12,10},{13,11},{18,20},{1... | collective-permute-start | bytes 1966088 | tf_op jit(solution)/shard_map/ppermute | solution.py:406
  46.1 16.3 %collective-permute-start.5 = (bf16[16,16,640]{2,1,0:T(8,128)(2,1)}, bf16[16,16,640]{2,1,0:T(8,128)(2,1)S(1)}, u32[]{:S(2)}, u32[]{:S(2)}) collective-permute-start(bf16[16,16,640]{2,1,0:T(8,128)(2,1)} %get-tuple-element.148), channel_id=1, source_target_pairs={{2,0},{3,1},{4,6},{5,7},{10,8},{11,9},{12,14},{13,15},{18,16},{19,... | collective-permute-start | bytes 983048 | tf_op jit(solution)/shard_map/ppermute | solution.py:406
  47.4 19.9 %all-to-all-start = ((bf16[4,2,2,32,1280]{4,3,2,1,0:T(8,128)(2,1)}), bf16[4,2,2,32,1280]{4,3,2,1,0:T(8,128)(2,1)}, u32[]{:S(2)}, u32[]{:S(2)}) async-start(bf16[4,2,2,32,1280]{4,3,2,1,0:T(8,128)(2,1)} %copy-done.24), calls=%async_computation | async-start | bytes 2621440 | tf_op jit(solution)/shard_map/all_to_all | solution.py:502
  57.2 23.9 %collective-permute-start.2 = (bf16[16,200,128]{2,1,0:T(8,128)(2,1)}, bf16[16,200,128]{2,1,0:T(8,128)(2,1)}, u32[]{:S(2)}, u32[]{:S(2)}) collective-permute-start(bf16[16,200,128]{2,1,0:T(8,128)(2,1)} %get-tuple-element.139), channel_id=1, source_target_pairs={{0,2},{1,3},{8,10},{9,11},{16,18},{17,19},{24,26},{25,27}} | collective-permute-start | bytes 2457608 | tf_op jit(solution)/shard_map/ppermute | solution.py:406
  62.5 3.5 %copy-start.17 = (bf16[16,16,640]{2,1,0:T(8,128)(2,1)}, bf16[16,16,640]{2,1,0:T(8,128)(2,1)S(1)}, u32[]{:S(2)}) copy-start(bf16[16,16,640]{2,1,0:T(8,128)(2,1)S(1)} %get-tuple-element.188) | copy-start | bytes 983044
  62.5 18.5 %collective-permute-start.6 = (bf16[2,16,16,640]{3,2,1,0:T(8,128)(2,1)}, bf16[2,16,16,640]{3,2,1,0:T(8,128)(2,1)}, u32[]{:S(2)}, u32[]{:S(2)}) collective-permute-start(bf16[2,16,16,640]{3,2,1,0:T(8,128)(2,1)} %get-tuple-element.150), channel_id=1, source_target_pairs={{2,4},{3,5},{4,2},{5,3},{10,12},{11,13},{12,10},{13,11},{18,20},{1... | collective-permute-start | bytes 1966088 | tf_op jit(solution)/shard_map/ppermute | solution.py:406
  66.0 15.0 %collective-permute-start.7 = (bf16[16,16,640]{2,1,0:T(8,128)(2,1)}, bf16[16,16,640]{2,1,0:T(8,128)(2,1)S(1)}, u32[]{:S(2)}, u32[]{:S(2)}) collective-permute-start(bf16[16,16,640]{2,1,0:T(8,128)(2,1)} %get-tuple-element.153), channel_id=1, source_target_pairs={{2,0},{3,1},{4,6},{5,7},{10,8},{11,9},{12,14},{13,15},{18,16},{19,... | collective-permute-start | bytes 983048 | tf_op jit(solution)/shard_map/ppermute | solution.py:406
  82.1 39.2 %collective-permute-start.3 = (bf16[2,32,16,640]{3,2,1,0:T(8,128)(2,1)}, bf16[2,32,16,640]{3,2,1,0:T(8,128)(2,1)S(1)}, u32[]{:S(2)}, u32[]{:S(2)}) collective-permute-start(bf16[2,32,16,640]{3,2,1,0:T(8,128)(2,1)} %get-tuple-element.141), channel_id=1, source_target_pairs={{0,2},{1,3},{6,4},{7,5},{8,10},{9,11},{14,12},{15,13},{16,18},{17,... | collective-permute-start | bytes 3932168 | tf_op jit(solution)/shard_map/ppermute | solution.py:406
  86.7 34.6 %collective-permute-start.8 = (bf16[2,32,16,640]{3,2,1,0:T(8,128)(2,1)}, bf16[2,32,16,640]{3,2,1,0:T(8,128)(2,1)S(1)}, u32[]{:S(2)}, u32[]{:S(2)}) collective-permute-start(bf16[2,32,16,640]{3,2,1,0:T(8,128)(2,1)} %get-tuple-element.155), channel_id=1, source_target_pairs={{2,4},{3,5},{4,2},{5,3},{10,12},{11,13},{12,10},{13,11},{18,20},{1... | collective-permute-start | bytes 3932168 | tf_op jit(solution)/shard_map/ppermute | solution.py:406
  87.5 25.5 %all-to-all-start.2 = ((bf16[4,2,2,32,1280]{4,3,2,1,0:T(8,128)(2,1)}), bf16[4,2,2,32,1280]{4,3,2,1,0:T(8,128)(2,1)}, u32[]{:S(2)}, u32[]{:S(2)}) async-start(bf16[4,2,2,32,1280]{4,3,2,1,0:T(8,128)(2,1)} %copy-done.23), calls=%async_computation.2 | async-start | bytes 2621440 | tf_op jit(solution)/shard_map/all_to_all | solution.py:502
  93.7 10.0 %collective-permute-start.9 = (bf16[16,16,640]{2,1,0:T(8,128)(2,1)S(1)}, bf16[16,16,640]{2,1,0:T(8,128)(2,1)S(1)}, u32[]{:S(2)}, u32[]{:S(2)}) collective-permute-start(bf16[16,16,640]{2,1,0:T(8,128)(2,1)S(1)} %get-tuple-element.159), channel_id=1, source_target_pairs={{2,0},{3,1},{4,6},{5,7},{10,8},{11,9},{12,14},{13,15},{18,16},{19,... | collective-permute-start | bytes 983048 | tf_op jit(solution)/shard_map/ppermute | solution.py:406
  104.4 16.9 %collective-permute-start.10 = (bf16[32,16,640]{2,1,0:T(8,128)(2,1)}, bf16[32,16,640]{2,1,0:T(8,128)(2,1)}, u32[]{:S(2)}, u32[]{:S(2)}) collective-permute-start(bf16[32,16,640]{2,1,0:T(8,128)(2,1)} %get-tuple-element.161), channel_id=1, source_target_pairs={{2,0},{3,1},{4,6},{5,7},{10,8},{11,9},{12,14},{13,15},{18,16},{19,... | collective-permute-start | bytes 1966088 | tf_op jit(solution)/shard_map/ppermute | solution.py:406
  113.0 5.4 %copy-start.35 = (bf16[1,16,16,640]{3,2,1,0:T(8,128)(2,1)S(1)}, bf16[1,16,16,640]{3,2,1,0:T(8,128)(2,1)}, u32[]{:S(2)}) copy-start(bf16[1,16,16,640]{3,2,1,0:T(8,128)(2,1)} %slice.102) | copy-start | bytes 983044
  121.3 13.6 %collective-permute-start.12 = (bf16[4,16,16,640]{3,2,1,0:T(8,128)(2,1)}, bf16[4,16,16,640]{3,2,1,0:T(8,128)(2,1)}, u32[]{:S(2)}, u32[]{:S(2)}) collective-permute-start(bf16[4,16,16,640]{3,2,1,0:T(8,128)(2,1)} %pad_maximum_fusion.6.mine_ref), channel_id=1, source_target_pairs={{0,1},{1,0},{2,3},{3,2},{4,5},{5,4},{6,7},{7,6},{8,9},{9,8},{10,11... | collective-permute-start | bytes 3932168 | tf_op jit(solution)/shard_map/ppermute | solution.py:592
  121.4 24.6 %collective-permute-start.11 = (bf16[2,32,16,640]{3,2,1,0:T(8,128)(2,1)S(1)}, bf16[2,32,16,640]{3,2,1,0:T(8,128)(2,1)}, u32[]{:S(2)}, u32[]{:S(2)}) collective-permute-start(bf16[2,32,16,640]{3,2,1,0:T(8,128)(2,1)S(1)} %get-tuple-element.164), channel_id=1, source_target_pairs={{2,4},{3,5},{4,2},{5,3},{10,12},{11,13},{12,10},{13,11},{18,20},{1... | collective-permute-start | bytes 3932168 | tf_op jit(solution)/shard_map/ppermute | solution.py:406
  124.2 7.5 %copy-start.18 = (bf16[16,16,640]{2,1,0:T(8,128)(2,1)S(1)}, bf16[16,16,640]{2,1,0:T(8,128)(2,1)}, u32[]{:S(2)}) copy-start(bf16[16,16,640]{2,1,0:T(8,128)(2,1)} %copy-done.17) | copy-start | bytes 983044
  124.2 8.5 %copy-start.20 = (bf16[16,16,640]{2,1,0:T(8,128)(2,1)S(1)}, bf16[16,16,640]{2,1,0:T(8,128)(2,1)}, u32[]{:S(2)}) copy-start(bf16[16,16,640]{2,1,0:T(8,128)(2,1)} %copy-done.19) | copy-start | bytes 983044
  124.2 20.4 %collective-permute-start.13 = (bf16[32,16,640]{2,1,0:T(8,128)(2,1)S(1)}, bf16[32,16,640]{2,1,0:T(8,128)(2,1)S(1)}, u32[]{:S(2)}, u32[]{:S(2)}) collective-permute-start(bf16[32,16,640]{2,1,0:T(8,128)(2,1)S(1)} %get-tuple-element.169), channel_id=1, source_target_pairs={{2,0},{3,1},{4,6},{5,7},{10,8},{11,9},{12,14},{13,15},{18,16},{19,... | collective-permute-start | bytes 1966088 | tf_op jit(solution)/shard_map/ppermute | solution.py:406
  125.8 32.5 %collective-permute-start.16 = (bf16[24,200,128]{2,1,0:T(8,128)(2,1)S(1)}, bf16[24,200,128]{2,1,0:T(8,128)(2,1)S(1)}, u32[]{:S(2)}, u32[]{:S(2)}) collective-permute-start(bf16[24,200,128]{2,1,0:T(8,128)(2,1)S(1)} %get-tuple-element.179), channel_id=1, source_target_pairs={{0,2},{1,3},{8,10},{9,11},{16,18},{17,19},{24,26},{25,27}} | collective-permute-start | bytes 3686408 | tf_op jit(solution)/shard_map/ppermute | solution.py:406
  139.0 7.0 %copy-start.28 = (bf16[16,80,128]{2,1,0:T(8,128)(2,1)}, bf16[16,80,128]{2,1,0:T(8,128)(2,1)S(1)}, u32[]{:S(2)}) copy-start(bf16[16,80,128]{2,1,0:T(8,128)(2,1)S(1)} %get-tuple-element.191.own_ref) | copy-start | bytes 983044
  144.7 11.2 %collective-permute-start.14 = (bf16[16,80,128]{2,1,0:T(8,128)(2,1)S(1)}, bf16[16,80,128]{2,1,0:T(8,128)(2,1)S(1)}, u32[]{:S(2)}, u32[]{:S(2)}) collective-permute-start(bf16[16,80,128]{2,1,0:T(8,128)(2,1)S(1)} %get-tuple-element.171), channel_id=1, source_target_pairs={{2,0},{3,1},{10,8},{11,9},{18,16},{19,17},{26,24},{27,25}} | collective-permute-start | bytes 983048 | tf_op jit(solution)/shard_map/ppermute | solution.py:406
  147.8 74.4 %collective-permute-start.23 = (bf16[4,32,16,640]{3,2,1,0:T(8,128)(2,1)S(1)}, bf16[4,32,16,640]{3,2,1,0:T(8,128)(2,1)}, u32[]{:S(2)}, u32[]{:S(2)}) collective-permute-start(bf16[4,32,16,640]{3,2,1,0:T(8,128)(2,1)S(1)} %pad_maximum_fusion.mine_ref), channel_id=1, source_target_pairs={{0,1},{1,0},{2,3},{3,2},{4,5},{5,4},{6,7},{7,6},{8,9},{9,8},{10,11... | collective-permute-start | bytes 7864328 | tf_op jit(solution)/shard_map/ppermute | solution.py:592
  150.6 39.2 %collective-permute-start.20 = (bf16[4,16,16,640]{3,2,1,0:T(8,128)(2,1)S(1)}, bf16[4,16,16,640]{3,2,1,0:T(8,128)(2,1)S(1)}, u32[]{:S(2)}, u32[]{:S(2)}) collective-permute-start(bf16[4,16,16,640]{3,2,1,0:T(8,128)(2,1)S(1)} %pad_maximum_fusion.7.mine_ref), channel_id=1, source_target_pairs={{0,1},{1,0},{2,3},{3,2},{4,5},{5,4},{6,7},{7,6},{8,9},{9,8},{10,11... | collective-permute-start | bytes 3932168 | tf_op jit(solution)/shard_map/ppermute | solution.py:600
  155.9 11.2 %copy-start.8 = (bf16[2,32,16,640]{3,2,1,0:T(8,128)(2,1)S(1)}, bf16[2,32,16,640]{3,2,1,0:T(8,128)(2,1)}, u32[]{:S(2)}) copy-start(bf16[2,32,16,640]{3,2,1,0:T(8,128)(2,1)} %copy-done.7) | copy-start | bytes 3932164
  159.3 35.4 %collective-permute-start.17 = (bf16[2,32,16,640]{3,2,1,0:T(8,128)(2,1)}, bf16[2,32,16,640]{3,2,1,0:T(8,128)(2,1)S(1)}, u32[]{:S(2)}, u32[]{:S(2)}) collective-permute-start(bf16[2,32,16,640]{3,2,1,0:T(8,128)(2,1)} %get-tuple-element.181), channel_id=1, source_target_pairs={{0,2},{1,3},{6,4},{7,5},{8,10},{9,11},{14,12},{15,13},{16,18},{17,... | collective-permute-start | bytes 3932168 | tf_op jit(solution)/shard_map/ppermute | solution.py:406
  165.8 18.7 %collective-permute-start.15 = (bf16[32,16,640]{2,1,0:T(8,128)(2,1)S(1)}, bf16[32,16,640]{2,1,0:T(8,128)(2,1)S(1)}, u32[]{:S(2)}, u32[]{:S(2)}) collective-permute-start(bf16[32,16,640]{2,1,0:T(8,128)(2,1)S(1)} %get-tuple-element.173), channel_id=1, source_target_pairs={{2,0},{3,1},{4,6},{5,7},{10,8},{11,9},{12,14},{13,15},{18,16},{19,... | collective-permute-start | bytes 1966088 | tf_op jit(solution)/shard_map/ppermute | solution.py:406
  167.1 22.7 %copy-start.9 = (bf16[2,32,16,640]{3,2,1,0:T(8,128)(2,1)}, bf16[2,32,16,640]{3,2,1,0:T(8,128)(2,1)S(1)}, u32[]{:S(2)}) copy-start(bf16[2,32,16,640]{3,2,1,0:T(8,128)(2,1)S(1)} %get-tuple-element.185) | copy-start | bytes 3932164
  167.1 35.4 %collective-permute-start.18 = (bf16[2,32,16,640]{3,2,1,0:T(8,128)(2,1)S(1)}, bf16[2,32,16,640]{3,2,1,0:T(8,128)(2,1)S(1)}, u32[]{:S(2)}, u32[]{:S(2)}) collective-permute-start(bf16[2,32,16,640]{3,2,1,0:T(8,128)(2,1)S(1)} %get-tuple-element.185), channel_id=1, source_target_pairs={{2,4},{3,5},{4,2},{5,3},{10,12},{11,13},{12,10},{13,11},{18,20},{1... | collective-permute-start | bytes 3932168 | tf_op jit(solution)/shard_map/ppermute | solution.py:406
  184.5 5.3 %copy-start.15 = (bf16[32,16,640]{2,1,0:T(8,128)(2,1)}, bf16[32,16,640]{2,1,0:T(8,128)(2,1)S(1)}, u32[]{:S(2)}) copy-start(bf16[32,16,640]{2,1,0:T(8,128)(2,1)S(1)} %get-tuple-element.221) | copy-start | bytes 1966084
  184.5 5.3 %copy-start.29 = (bf16[16,80,128]{2,1,0:T(8,128)(2,1)S(1)}, bf16[16,80,128]{2,1,0:T(8,128)(2,1)}, u32[]{:S(2)}) copy-start(bf16[16,80,128]{2,1,0:T(8,128)(2,1)} %copy-done.28) | copy-start | bytes 983044
  184.5 18.0 %collective-permute-start.19 = (bf16[32,16,640]{2,1,0:T(8,128)(2,1)S(1)}, bf16[32,16,640]{2,1,0:T(8,128)(2,1)S(1)}, u32[]{:S(2)}, u32[]{:S(2)}) collective-permute-start(bf16[32,16,640]{2,1,0:T(8,128)(2,1)S(1)} %get-tuple-element.175), channel_id=1, source_target_pairs={{2,0},{3,1},{4,6},{5,7},{10,8},{11,9},{12,14},{13,15},{18,16},{19,... | collective-permute-start | bytes 1966088 | tf_op jit(solution)/shard_map/ppermute | solution.py:406
  194.6 38.7 %collective-permute-start.25 = (bf16[24,200,128]{2,1,0:T(8,128)(2,1)}, bf16[24,200,128]{2,1,0:T(8,128)(2,1)S(1)}, u32[]{:S(2)}, u32[]{:S(2)}) collective-permute-start(bf16[24,200,128]{2,1,0:T(8,128)(2,1)} %get-tuple-element.209), channel_id=1, source_target_pairs={{0,2},{1,3},{8,10},{9,11},{16,18},{17,19},{24,26},{25,27}} | collective-permute-start | bytes 3686408 | tf_op jit(solution)/shard_map/ppermute | solution.py:406
  203.4 30.0 %collective-permute-start.22 = (bf16[2,32,16,640]{3,2,1,0:T(8,128)(2,1)S(1)}, bf16[2,32,16,640]{3,2,1,0:T(8,128)(2,1)S(1)}, u32[]{:S(2)}, u32[]{:S(2)}) collective-permute-start(bf16[2,32,16,640]{3,2,1,0:T(8,128)(2,1)S(1)} %get-tuple-element.195), channel_id=1, source_target_pairs={{2,4},{3,5},{4,2},{5,3},{10,12},{11,13},{12,10},{13,11},{18,20},{1... | collective-permute-start | bytes 3932168 | tf_op jit(solution)/shard_map/ppermute | solution.py:406
  205.1 17.1 %collective-permute-start.21 = (bf16[32,16,640]{2,1,0:T(8,128)(2,1)S(1)}, bf16[32,16,640]{2,1,0:T(8,128)(2,1)S(1)}, u32[]{:S(2)}, u32[]{:S(2)}) collective-permute-start(bf16[32,16,640]{2,1,0:T(8,128)(2,1)S(1)} %get-tuple-element.198), channel_id=1, source_target_pairs={{2,0},{3,1},{4,6},{5,7},{10,8},{11,9},{12,14},{13,15},{18,16},{19,... | collective-permute-start | bytes 1966088 | tf_op jit(solution)/shard_map/ppermute | solution.py:406
  222.2 7.5 %copy-start.16 = (bf16[32,16,640]{2,1,0:T(8,128)(2,1)S(1)}, bf16[32,16,640]{2,1,0:T(8,128)(2,1)}, u32[]{:S(2)}) copy-start(bf16[32,16,640]{2,1,0:T(8,128)(2,1)} %copy-done.15) | copy-start | bytes 1966084
  228.4 16.0 %collective-permute-start.24 = (bf16[32,80,128]{2,1,0:T(8,128)(2,1)S(1)}, bf16[32,80,128]{2,1,0:T(8,128)(2,1)S(1)}, u32[]{:S(2)}, u32[]{:S(2)}) collective-permute-start(bf16[32,80,128]{2,1,0:T(8,128)(2,1)S(1)} %get-tuple-element.205), channel_id=1, source_target_pairs={{2,0},{3,1},{10,8},{11,9},{18,16},{19,17},{26,24},{27,25}} | collective-permute-start | bytes 1966088 | tf_op jit(solution)/shard_map/ppermute | solution.py:406
  232.3 36.6 %collective-permute-start.30 = (bf16[4,32,16,640]{3,2,1,0:T(8,128)(2,1)S(1)}, bf16[4,32,16,640]{3,2,1,0:T(8,128)(2,1)}, u32[]{:S(2)}, u32[]{:S(2)}) collective-permute-start(bf16[4,32,16,640]{3,2,1,0:T(8,128)(2,1)S(1)} %pad_maximum_fusion.3.mine_ref), channel_id=1, source_target_pairs={{0,1},{1,0},{2,3},{3,2},{4,5},{5,4},{6,7},{7,6},{8,9},{9,8},{10,11... | collective-permute-start | bytes 7864328 | tf_op jit(solution)/shard_map/ppermute | solution.py:600
  233.5 12.6 %copy-start.14 = (bf16[32,16,640]{2,1,0:T(8,128)(2,1)S(1)}, bf16[32,16,640]{2,1,0:T(8,128)(2,1)}, u32[]{:S(2)}) copy-start(bf16[32,16,640]{2,1,0:T(8,128)(2,1)} %copy-done.13) | copy-start | bytes 1966084
  244.5 15.3 %collective-permute-start.26 = (bf16[32,16,640]{2,1,0:T(8,128)(2,1)S(1)}, bf16[32,16,640]{2,1,0:T(8,128)(2,1)S(1)}, u32[]{:S(2)}, u32[]{:S(2)}) collective-permute-start(bf16[32,16,640]{2,1,0:T(8,128)(2,1)S(1)} %get-tuple-element.211), channel_id=1, source_target_pairs={{2,0},{3,1},{4,6},{5,7},{10,8},{11,9},{12,14},{13,15},{18,16},{19,... | collective-permute-start | bytes 1966088 | tf_op jit(solution)/shard_map/ppermute | solution.py:406
  247.4 14.1 %collective-permute-start.28 = (bf16[4,32,16,640]{3,2,1,0:T(8,128)(2,1)S(1)}, bf16[4,32,16,640]{3,2,1,0:T(8,128)(2,1)}, u32[]{:S(2)}, u32[]{:S(2)}) collective-permute-start(bf16[4,32,16,640]{3,2,1,0:T(8,128)(2,1)S(1)} %pad_maximum_fusion.2.mine_ref), channel_id=1, source_target_pairs={{0,1},{1,0},{2,3},{3,2},{4,5},{5,4},{6,7},{7,6},{8,9},{9,8},{10,11... | collective-permute-start | bytes 7864328 | tf_op jit(solution)/shard_map/ppermute | solution.py:592
  249.3 10.5 %copy-start.33 = (bf16[1,32,16,640]{3,2,1,0:T(8,128)(2,1)S(1)}, bf16[1,32,16,640]{3,2,1,0:T(8,128)(2,1)}, u32[]{:S(2)}) copy-start(bf16[1,32,16,640]{3,2,1,0:T(8,128)(2,1)} %fusion.1) | copy-start | bytes 1966084
  249.3 10.5 %copy-start.34 = (bf16[1,32,16,640]{3,2,1,0:T(8,128)(2,1)S(1)}, bf16[1,32,16,640]{3,2,1,0:T(8,128)(2,1)}, u32[]{:S(2)}) copy-start(bf16[1,32,16,640]{3,2,1,0:T(8,128)(2,1)} %select_bitcast_fusion.3) | copy-start | bytes 1966084
  260.2 26.5 %collective-permute-start.27 = (bf16[4,32,16,640]{3,2,1,0:T(8,128)(2,1)S(1)}, bf16[4,32,16,640]{3,2,1,0:T(8,128)(2,1)}, u32[]{:S(2)}, u32[]{:S(2)}) collective-permute-start(bf16[4,32,16,640]{3,2,1,0:T(8,128)(2,1)S(1)} %pad_maximum_fusion.1.mine_ref), channel_id=1, source_target_pairs={{0,1},{1,0},{2,3},{3,2},{4,5},{5,4},{6,7},{7,6},{8,9},{9,8},{10,11... | collective-permute-start | bytes 7864328 | tf_op jit(solution)/shard_map/ppermute | solution.py:600
  267.7 19.0 %collective-permute-start.29 = (bf16[32,80,128]{2,1,0:T(8,128)(2,1)S(1)}, bf16[32,80,128]{2,1,0:T(8,128)(2,1)S(1)}, u32[]{:S(2)}, u32[]{:S(2)}) collective-permute-start(bf16[32,80,128]{2,1,0:T(8,128)(2,1)S(1)} %get-tuple-element.217), channel_id=1, source_target_pairs={{2,0},{3,1},{10,8},{11,9},{18,16},{19,17},{26,24},{27,25}} | collective-permute-start | bytes 1966088 | tf_op jit(solution)/shard_map/ppermute | solution.py:406
  (22 other events, 36.0 us)

commit v3 on v0

v3 whole, which is shorter than its diff:
```python
import functools
import math

import jax
import jax.numpy as jnp
from jax import lax
from jax.experimental import pallas as pl
from jax.experimental.pallas import tpu as pltpu
from jax.sharding import PartitionSpec as P

LANES = 128
VMEM_LIMIT = 48 * 1024 * 1024
MARK = jax.ShapeDtypeStruct((8, LANES), jnp.float32)
MARK_SPEC = pl.BlockSpec((8, LANES), lambda *_: (0, 0))
ANY = pl.BlockSpec(memory_space=pl.ANY)
SMALL = pl.CostEstimate(flops=1000, bytes_accessed=1000, transcendentals=0)


def dot_nt(a, b):
    return lax.dot_general(a, b, (((1,), (1,)), ((), ())), preferred_element_type=jnp.float32)


def params():
    return pltpu.CompilerParams(vmem_limit_bytes=VMEM_LIMIT)


def hi_lo(x):
    hi = x.astype(jnp.bfloat16)
    return hi, (x - hi.astype(jnp.float32)).astype(jnp.bfloat16)


def build_table(start, count, base_ref, step_ref, table_ref):
    for parity in range(2):
        cos0 = base_ref[parity, 0, start : start + count]
        sin0 = base_ref[parity, 1, start : start + count]
        for b in range(step_ref.shape[3]):
            cos1 = step_ref[parity, 0, start : start + count, b : b + 1]
            sin1 = step_ref[parity, 1, start : start + count, b : b + 1]
            both = (cos0 * cos1 - sin0 * sin1, -(sin0 * cos1 + cos0 * sin1))
            for c, table in enumerate(both):
                for part, term in enumerate(hi_lo(table)):
                    at = (2 * part + c) * count
                    table_ref[parity, at : at + count, b * LANES : (b + 1) * LANES] = term


def transform(start, sizes, first_ref, table_ref, folded, out_ref):
    groups = out_ref.shape[0]
    count = groups * sum(sizes)
    found = []
    for parity in range(2):
        main = dot_nt(table_ref[parity], folded[2 * parity])
        found.append(
            main[: 2 * count] + (main[2 * count :] + dot_nt(table_ref[parity, : 2 * count], folded[2 * parity + 1]))
        )
    first = first_ref[start : start + count] > 0.5
    chosen = []
    for left, right in (found, found[::-1]):
        for c in range(2):
            at = slice(c * count, (c + 1) * count)
            chosen.append(jnp.where(first, left[at], right[at]))
    for g in range(groups):
        rows, ahead = [], 0
        for pairs in sizes:
            rows += [values[ahead + g * pairs : ahead + (g + 1) * pairs] for values in chosen]
            ahead += groups * pairs
        out_ref[g] = jnp.concatenate(rows, axis=0).astype(jnp.bfloat16)


def fold_kernel(start, sizes, group, base_ref, step_ref, first_ref, order_ref, *refs):
    fields, refs = refs[:group], refs[-7:]
    out_ref, folded_refs, mark_ref, table_ref = refs[0], refs[1:5], refs[5], refs[6]
    mark_ref[...] = jnp.zeros_like(mark_ref)
    rows, half = order_ref.shape[0], folded_refs[0].shape[1]
    count = out_ref.shape[0] * sum(sizes)

    @pl.when(pl.program_id(0) == 0)
    def _():
        build_table(start, count, base_ref, step_ref, table_ref)

    for f, grid_ref in enumerate(fields):
        near, far = grid_ref[0, :, :half], grid_ref[0, :, half:]
        for parity, folded in enumerate((near + far, near - far)):
            for part, term in enumerate(hi_lo(folded)):
                moved = jnp.dot(order_ref[...], term, preferred_element_type=jnp.float32)
                folded_refs[2 * parity + part][f * rows : (f + 1) * rows] = moved.astype(jnp.bfloat16)
    transform(start, sizes, first_ref, table_ref, [ref[...] for ref in folded_refs], out_ref)


def fold_and_zonal(base, step, first, order, grid, groups, start, sizes, after):
    fields, rows, nlon = grid.shape
    half = nlon // 2
    group = 4 if fields % 4 == 0 and 4 * rows % LANES == 0 else fields
    pairs = sum(sizes)
    count = groups * pairs
    whole = [pl.BlockSpec(a.shape, lambda n, r=a.ndim: (0,) * r) for a in (base, step, first, order)]
    return pl.pallas_call(
        functools.partial(fold_kernel, start, sizes, group),
        grid=(fields // group,),
        in_specs=whole
        + [pl.BlockSpec((1, rows, nlon), lambda n, f=f: (n * group + f, 0, 0)) for f in range(group)]
        + [ANY] * len(after),
        out_specs=(
            pl.BlockSpec((groups, 4 * pairs, group * rows), lambda n: (0, 0, n)),
            *[pl.BlockSpec((group * rows, half), lambda n: (n, 0))] * 4,
            MARK_SPEC,
        ),
        out_shape=(
            jax.ShapeDtypeStruct((groups, 4 * pairs, fields * rows), jnp.bfloat16),
            *[jax.ShapeDtypeStruct((fields * rows, half), jnp.bfloat16)] * 4,
            MARK,
        ),
        scratch_shapes=[pltpu.VMEM((2, 4 * count, half), jnp.bfloat16)],
        compiler_params=params(),
        cost_estimate=SMALL,
        name="fold_and_zonal",
    )(base, step, first, order, *[grid] * group, *after)


def zonal_kernel(start, sizes, base_ref, step_ref, first_ref, *refs):
    folded, (out_ref, mark_ref, table_ref) = refs[:4], refs[-3:]
    count = out_ref.shape[0] * sum(sizes)
    mark_ref[...] = jnp.zeros_like(mark_ref)

    @pl.when(pl.program_id(0) == 0)
    def _():
        build_table(start, count, base_ref, step_ref, table_ref)

    transform(start, sizes, first_ref, table_ref, [ref[...] for ref in folded], out_ref)


def zonal(base, step, first, folded, groups, start, sizes, after):
    columns, half = folded[0].shape
    block = columns // 5 if columns % (5 * LANES) == 0 else columns
    pairs = sum(sizes)
    count = groups * pairs
    whole = [pl.BlockSpec(a.shape, lambda n, r=a.ndim: (0,) * r) for a in (base, step, first)]
    return pl.pallas_call(
        functools.partial(zonal_kernel, start, sizes),
        grid=(columns // block,),
        in_specs=whole + [pl.BlockSpec((block, half), lambda n: (n, 0))] * 4 + [ANY] * len(after),
        out_specs=(pl.BlockSpec((groups, 4 * pairs, block), lambda n: (0, 0, n)), MARK_SPEC),
        out_shape=(jax.ShapeDtypeStruct((groups, 4 * pairs, columns), jnp.bfloat16), MARK),
        scratch_shapes=[pltpu.VMEM((2, 4 * count, half), jnp.bfloat16)],
        compiler_params=params(),
        cost_estimate=SMALL,
        name="zonal",
    )(base, step, first, *folded, *after)


def halves_kernel(fields, wide, in_ref, *refs):
    both_ref, again_ref, low_ref, mark_ref, work_ref = refs[-5:]
    mark_ref[...] = jnp.zeros_like(mark_ref)
    bands = in_ref.shape[0] // 2
    pairs, lines, length = work_ref.shape
    rows = in_ref.shape[2] // fields
    for which in range(2):
        for core in range(2):
            for c in range(2):
                at = slice((2 * which + c) * pairs, (2 * which + c + 1) * pairs)
                parts = [in_ref[2 * b + core].astype(jnp.float32)[at] for b in range(bands)]
                sums = [parts[b] + parts[bands - 1 - b] for b in range(bands // 2)]
                gaps = [parts[b] - parts[bands - 1 - b] for b in range(bands // 2)]
                for f in range(fields):
                    at = slice(f * rows, (f + 1) * rows)
                    even = jnp.concatenate([x[:, at] for x in sums], axis=1)
                    odd = jnp.concatenate([x[:, at] for x in gaps], axis=1)
                    whole = [even[:, :wide], odd[:, :wide], even[:, wide:], odd[:, wide:]]
                    work_ref[:, (2 * core + c) * fields + f, :] = jnp.concatenate(whole, axis=1)
        for b in range(length // LANES):
            found = work_ref[:, :, b * LANES : (b + 1) * LANES].astype(jnp.bfloat16)
            at = slice(b * lines, (b + 1) * lines)
            both_ref[which, :, at] = found
            again_ref[which, :, at] = found
            if which == 0:
                low_ref[:, at] = found


def halves(arrived, fields, wide, ahead, pairs, after):
    groups, _, columns = arrived.shape
    lines, length = 4 * fields, groups * columns // (2 * fields)
    shape = (pairs, lines * length // LANES, LANES)
    shapes = [(2, *shape), (2, *shape), shape]
    return pl.pallas_call(
        functools.partial(halves_kernel, fields, wide),
        grid=(1,),
        out_shape=(*[jax.ShapeDtypeStruct(each, jnp.bfloat16) for each in shapes], MARK),
        in_specs=[pl.BlockSpec((groups, 4 * pairs, columns), lambda _: (0, ahead // pairs, 0))] + [ANY] * len(after),
        out_specs=(*[pl.BlockSpec(each, lambda _, r=len(each): (0,) * r) for each in shapes], MARK_SPEC),
        scratch_shapes=[pltpu.VMEM((pairs, lines, length), jnp.float32)],
        compiler_params=params(),
        cost_estimate=SMALL,
        name="halves",
    )(arrived, *after)


def whole_lines(block, lines, length):
    tiles = length // LANES
    found = []
    for start in range(0, block.shape[0], tiles * lines):
        found.append(
            jnp.concatenate([block[start + b * lines : start + (b + 1) * lines] for b in range(tiles)], axis=1)
        )
    return found


def contract(table, spec, wide):
    half = spec.shape[1] // 2
    count = spec.shape[0]
    even_row = lax.rem(lax.broadcasted_iota(jnp.int32, (table.shape[0], 1), 0), 2) == 0
    main = dot_nt(table[:, :wide], jnp.concatenate([spec[:, :wide], spec[:, wide : 2 * wide]], axis=0))
    total = jnp.where(even_row, main[:, :count], main[:, count:])
    if half > wide:
        rest = table[:, wide:].astype(jnp.float32)
        rest = jnp.concatenate([jnp.where(even_row, rest, 0.0), jnp.where(even_row, 0.0, rest)], axis=1)
        total = total + dot_nt(rest.astype(jnp.bfloat16), spec[:, 2 * wide :])
    return total


def keep_valid(values, lev, wave, modes):
    degrees = values.shape[0] // 2
    row = lax.broadcasted_iota(jnp.int32, (values.shape[0], 1), 0)
    other = lev + 1 - 2 * lax.rem(lev, 2)
    degree = jnp.where(row < degrees, lev * degrees + row, other * degrees + row - degrees)
    return jnp.where(degree < modes - wave, values, 0.0).astype(jnp.bfloat16)


def column_order(sources, fields):
    count = sources.shape[0] * 4 * fields
    row = jnp.arange(count, dtype=jnp.int32)
    chip = jnp.repeat(sources, 4 * fields)
    core = row // (2 * fields) % 2
    c = row // fields % 2
    target = c * (count // 2) + (2 * chip + core) * fields + row % fields
    return (row[None, :] == target[:, None]).astype(jnp.bfloat16)


def in_order(values, order):
    count, degrees, columns = values.shape
    moved = jnp.dot(values.reshape(count * degrees, columns), order, preferred_element_type=jnp.float32)
    return moved.astype(jnp.bfloat16).reshape(count, degrees, columns)


def chip_table(own_ref, other_ref, slot):
    return jnp.concatenate([own_ref[slot], other_ref[slot]], axis=0)


def pair_of(waves_ref, q):
    left, right = waves_ref[2 * q], waves_ref[2 * q + 1]
    return left > right, jnp.minimum(left, right), jnp.maximum(left, right)


def high_kernel(parts, ends, lines, start, modes, wide, info_ref, waves_ref, order_ref, own_ref, other_ref, *refs):
    pieces, (kept_ref, sent_ref, sent_back_ref, mark_ref, work_ref) = refs[:parts], refs[-5:]
    given = refs[parts : parts + len(ends)]
    mark_ref[...] = jnp.zeros_like(mark_ref)
    _, pairs, degrees, _ = kept_ref.shape
    lev = info_ref[0]
    for i in range(pairs):
        swapped, _, wave = pair_of(waves_ref, start + pl.program_id(0) * pairs + i)
        table = chip_table(own_ref, other_ref, 2 * i + jnp.where(swapped, 0, 1))
        block = given[-1][i]
        for ref, end in zip(given[-2::-1], ends[-2::-1]):
            block = jnp.where(pl.program_id(0) < end, ref[i], block)
        both = jnp.concatenate([table, unpacked(block, *table.shape)], axis=0)
        spec = sum([whole_lines(piece[i], lines, 2 * table.shape[1]) for piece in pieces], [])
        values = contract(both, jnp.concatenate(spec, axis=0), wide)
        work_ref[i] = keep_valid(values[: 2 * degrees], lev, wave, modes)
        work_ref[pairs + i] = keep_valid(values[2 * degrees :], lev - 2, wave, modes)
    for which in range(2):
        found = in_order(work_ref[which * pairs : (which + 1) * pairs], order_ref[...])
        kept_ref[which] = found[:, :degrees]
        (sent_ref, sent_back_ref)[which][...] = found[:, degrees:]


def low_kernel(parts, lines, start, modes, wide, info_ref, waves_ref, order_ref, own_ref, other_ref, *refs):
    mine, passed, came = refs[0], refs[1 : 1 + parts], refs[1 + parts : 1 + 2 * parts]
    kept_ref, sent_ref, mark_ref, work_ref = refs[-4:]
    mark_ref[...] = jnp.zeros_like(mark_ref)
    pairs, degrees, _ = kept_ref.shape
    lev = info_ref[0]
    for i in range(pairs):
        swapped, wave, _ = pair_of(waves_ref, start + pl.program_id(0) * pairs + i)
        table = chip_table(own_ref, other_ref, 2 * i + jnp.where(swapped, 1, 0))
        pieces = [mine[i]] + [a[i] + b[i] for a, b in zip(passed, came)]
        spec = sum([whole_lines(piece, lines, 2 * table.shape[1]) for piece in pieces], [])
        work_ref[i] = keep_valid(contract(table, jnp.concatenate(spec, axis=0), wide), lev, wave, modes)
    found = in_order(work_ref[...], order_ref[...])
    kept_ref[...], sent_ref[...] = found[:, :degrees], found[:, degrees:]


def finish_kernel(start, info_ref, waves_ref, *refs):
    out_ref, mark_ref = refs[-2:]
    mark_ref[...] = jnp.zeros_like(mark_ref)
    pairs = refs[0].shape[0]
    core = lax.rem(info_ref[0], 2)
    first = info_ref[0] < 2
    for side, (low, high, back) in enumerate((refs[:3], refs[3:6])):
        half = core if side == 0 else 1 - core
        for i in range(pairs):
            q = start + pl.program_id(0) * pairs + i
            swapped = waves_ref[half, 2 * q] > waves_ref[half, 2 * q + 1]
            out_ref[half, 2 * i + jnp.where(swapped, 1, 0)] = low[i]
            out_ref[half, 2 * i + jnp.where(swapped, 0, 1)] = jnp.where(first, back[i], high[i])


def block_pairs(start, pairs):
    for size in (8, 4, 2):
        if start % size == 0 and pairs % size == 0:
            return size
    return pairs if start % pairs == 0 else 1


def over_pairs(kernel, name, steps, info, waves, operands, in_specs, outs, out_specs, scratch=(), alias=None, after=()):
    operands = [*operands, *after]
    in_specs = [*in_specs, *[ANY] * len(after)]
    return pl.pallas_call(
        kernel,
        grid_spec=pltpu.PrefetchScalarGridSpec(
            num_scalar_prefetch=2,
            grid=(steps,),
            in_specs=in_specs,
            out_specs=(*out_specs, pl.BlockSpec((8, LANES), lambda *_: (0, 0))),
            scratch_shapes=list(scratch),
        ),
        out_shape=(*outs, MARK),
        input_output_aliases={} if alias is None else {2 + alias: 0},
        compiler_params=params(),
        cost_estimate=SMALL,
        name=name,
    )(info, waves, *operands)


def table_specs(start, block, table):
    slots, degrees, half = table.shape
    ahead = slots // 2 // (2 * block)
    offset = start // block
    place = lambda i, info, _: (lax.rem(info[0], 2) * ahead + offset + i, 0, 0)
    return [pl.BlockSpec((2 * block, degrees, half), place)] * 2


class Piece:
    def __init__(self, array, ahead=0, which=None):
        self.array, self.ahead, self.which = array, ahead, which

    def spec(self, block):
        shape = self.array.shape[-2:]
        offset, which = self.ahead // block, self.which
        last = self.array.shape[-3] // block - 1
        if which is None:
            return pl.BlockSpec((block, *shape), lambda i, *_: (jnp.clip(offset + i, 0, last), 0, 0))
        return pl.BlockSpec((None, block, *shape), lambda i, *_: (which, jnp.clip(offset + i, 0, last), 0, 0))


def give_kernel(start, info_ref, waves_ref, own_ref, other_ref, *refs):
    out_ref, mark_ref = refs[-2:]
    pairs, lines, _ = out_ref.shape
    mark_ref[...] = jnp.zeros_like(mark_ref)
    for i in range(pairs):
        swapped, _, _ = pair_of(waves_ref, start + pl.program_id(0) * pairs + i)
        table = chip_table(own_ref, other_ref, 2 * i + jnp.where(swapped, 0, 1))
        rows, half = table.shape
        if not packs(rows, half):
            out_ref[i] = table
            continue
        whole = half // LANES
        for b in range(whole):
            out_ref[i, b * rows : (b + 1) * rows] = table[:, b * LANES : (b + 1) * LANES]
        rest = table[:, whole * LANES :]
        out_ref[i, whole * rows :] = jnp.concatenate([rest[: rows // 2], rest[rows // 2 :]], axis=1)


def packs(rows, half):
    return half % LANES == LANES // 2 and rows % 32 == 0


def unpacked(block, rows, half):
    if not packs(rows, half):
        return block
    whole = half // LANES
    rest = block[whole * rows :]
    rest = jnp.concatenate([rest[:, : LANES // 2], rest[:, LANES // 2 :]], axis=0)
    return jnp.concatenate([block[b * rows : (b + 1) * rows] for b in range(whole)] + [rest], axis=1)


def gate_kernel(*refs):
    pass


def gate(arrays, after):
    count = len(arrays)
    found = pl.pallas_call(
        gate_kernel,
        in_specs=[ANY] * (count + len(after)),
        out_specs=(ANY,) * (count + 1),
        out_shape=(*[jax.ShapeDtypeStruct(a.shape, a.dtype) for a in arrays], MARK),
        input_output_aliases={i: i for i in range(count)},
        compiler_params=params(),
        cost_estimate=SMALL,
        name="gate",
    )(*arrays, *after)
    return found[:count], found[count]


def on_cores(chip_pairs):
    return [(2 * a + core, 2 * b + core) for a, b in chip_pairs for core in range(2)]


def send(block, pairs):
    return lax.ppermute(block, "lev", on_cores(pairs))


class Links:
    def __init__(self):
        self.mark = ()

    def send(self, block, pairs, after=(), meanwhile=()):
        after = tuple(mark for mark in after if mark is not None)
        if self.mark or after:
            (block,), _ = gate([block], (*self.mark, *after))
        (there,), mark = gate([send(block, pairs)], tuple(mark for mark in meanwhile if mark is not None))
        self.mark = (mark,)
        return block, there, mark


INWARD = [(0, 1), (3, 2)]
CENTRE = [(1, 2), (2, 1)]
OUTWARD = [(1, 0), (2, 3)]
GIVE = [(0, 1)]
RETURN = [(1, 0)]
SOURCES = [[0, 1, 2, 3], [1, 0, 2, 3], [2, 3, 1, 0], [3, 2, 1, 0]]


def chunk_sizes(pairs):
    if pairs % 40 == 0:
        return [pairs // 5, 2 * pairs // 5, 2 * pairs // 5]
    return [pairs]


def laid_out(sizes):
    found, start = [], 0
    for size in sizes:
        found.append((start, size))
        start += size
    return found


def given_parts(sizes):
    pairs = sum(sizes)
    if len(sizes) == 3 and pairs % 40 == 0:
        return laid_out([pairs // 5, pairs // 5, 2 * pairs // 5, pairs // 5])
    return laid_out([pairs] + [0] * len(sizes))


def per_device(grid_gradient, legendre, assign):
    fields, rows, nlon = grid_gradient.shape
    modes = nlon // 2
    slots, degrees, half = legendre.shape
    bands = lax.axis_size("lat")
    levels = lax.axis_size("lev")
    chips = levels // 2
    lat_id = lax.axis_index("lat")
    lev_id = lax.axis_index("lev")
    z, core = lev_id // 2, lev_id % 2
    groups = 2 * bands
    pairs = slots // 4
    wide = half // 256 * 256 if half >= 256 else half
    in_line = chips == 4
    sizes = chunk_sizes(pairs) if in_line else [pairs]
    chunks = laid_out(sizes)
    count = len(chunks)
    assign = assign.astype(jnp.int32)

    by_group = assign.reshape(groups, pairs, 2)
    listed = jnp.concatenate([by_group[:, s : s + n].reshape(groups * n, 2) for s, n in chunks])
    swapped = listed[:, 0] % 2 == 1
    even_wave = jnp.where(swapped, listed[:, 1], listed[:, 0])
    odd_wave = jnp.where(swapped, listed[:, 0], listed[:, 1])
    waves_of = jnp.stack([even_wave, odd_wave])
    first = (even_wave < odd_wave).astype(jnp.float32)[:, None]
    weight = jnp.where(waves_of == 0, 1.0, 2.0).astype(jnp.float32)[:, :, None]
    turn = 2.0 * math.pi / nlon

    def cos_sin(places, scale):
        angle = (waves_of[:, :, None] * places % nlon).astype(jnp.float32) * turn
        return jnp.stack([jnp.cos(angle) * scale, jnp.sin(angle) * scale], axis=1)

    base = cos_sin(jnp.arange(LANES, dtype=jnp.int32), weight)
    step = cos_sin(jnp.arange(0, modes, LANES, dtype=jnp.int32), 1.0)

    here = jnp.arange(rows, dtype=jnp.int32)
    wanted = jnp.where(lat_id >= bands // 2, rows - 1 - here, here)
    row_order = (here[None, :] == wanted[:, None]).astype(jnp.bfloat16)

    group_waves = lax.dynamic_slice(assign, (lat_id * slots,), (slots,)).reshape(2, slots // 2)
    waves = lax.dynamic_slice(group_waves, (core, 0), (1, slots // 2))[0]
    info = jnp.stack([lev_id])
    swap = [(i, i ^ 1) for i in range(levels)]
    squares = [[b * levels + 2 * chip + side for b in range(bands) for side in range(2)] for chip in range(chips)]
    other_table = lax.ppermute(legendre, "lev", swap)
    spec = {}
    state = {"mark": (), "out": None}

    def exchange(found):
        return lax.all_to_all(
            found, ("lat", "lev"), split_axis=0, concat_axis=0, axis_index_groups=squares, tiled=True
        )

    def zonal_first():
        found, *state["folded"], mark = fold_and_zonal(
            base, step, first, row_order, grid_gradient, groups, 0, sizes[:1], ()
        )
        state["mark"] = (mark,)
        spec[0] = (exchange(found), 0)

    def zonal_rest():
        found, mark = zonal(
            base, step, first, state["folded"], groups, groups * sizes[0], tuple(sizes[1:]), state["mark"]
        )
        state["mark"] = (mark,)
        arrived = exchange(found)
        for i in range(1, count):
            spec[i] = (arrived, chunks[i][0] - sizes[0])

    def do_halves(i):
        arrived, ahead = spec[i]
        both, again, low, mark = halves(arrived, fields, wide, ahead, sizes[i], state["mark"])
        state["mark"] = (mark,)
        return both, again, low, mark

    columns = chips * 4 * fields
    order_spec = pl.BlockSpec((columns, columns), lambda *_: (0, 0))

    lines = 4 * fields

    def high_slots(i, given, ends, pieces):
        s, n = chunks[i]
        block = block_pairs(s, n)
        shape = jax.ShapeDtypeStruct((n, degrees, columns), jnp.bfloat16)
        result = pl.BlockSpec((block, degrees, columns), lambda j, *_: (j, 0, 0))
        shape2 = jax.ShapeDtypeStruct((2, n, degrees, columns), jnp.bfloat16)
        result2 = pl.BlockSpec((2, block, degrees, columns), lambda j, *_: (0, j, 0, 0))
        parts = [*pieces, *given]
        return over_pairs(
            functools.partial(high_kernel, len(pieces), ends, lines, s, modes, wide), "high_slots", n // block, info,
            waves, [order, legendre, other_table, *[piece.array for piece in parts]],
            [order_spec, *table_specs(s, block, legendre), *[piece.spec(block) for piece in parts]],
            (shape2, shape, shape), (result2, result, result),
            [pltpu.VMEM((2 * block, 2 * degrees, columns), jnp.bfloat16)],
        )

    def low_slots(i, mine, passed, came):
        s, n = chunks[i]
        block = block_pairs(s, n)
        shape = jax.ShapeDtypeStruct((n, degrees, columns), jnp.bfloat16)
        result = pl.BlockSpec((block, degrees, columns), lambda j, *_: (j, 0, 0))
        parts = [mine, *passed, *came]
        return over_pairs(
            functools.partial(low_kernel, len(passed), lines, s, modes, wide), "low_slots", n // block, info, waves,
            [order, legendre, other_table, *[piece.array for piece in parts]],
            [order_spec, *table_specs(s, block, legendre), *[piece.spec(block) for piece in parts]],
            (shape, shape), (result, result),
            [pltpu.VMEM((block, 2 * degrees, columns), jnp.bfloat16)],
        )

    def finish(i, kept, got):
        s, n = chunks[i]
        block = block_pairs(s, n)
        before = () if state["out"] is None else (state["out"],)
        parts = [*kept, *got]
        state["out"], mark = over_pairs(
            functools.partial(finish_kernel, s), "finish", n // block, info, group_waves,
            [*[piece.array for piece in parts], *before],
            [*[piece.spec(block) for piece in parts], *[ANY] * len(before)],
            (jax.ShapeDtypeStruct((2, slots // 2, degrees, columns), jnp.bfloat16),),
            (pl.BlockSpec((2, 2 * block, degrees, columns), lambda j, *_: (0, s // block + j, 0, 0)),),
            alias=6 if before else None,
        )
        return mark

    if not in_line:
        zonal_first()
        both, _, _, _ = do_halves(0)
        sides = [[2 * chip + side for chip in range(chips)] for side in range(2)]
        everyone = lax.all_gather(both, "lev", axis=2, axis_index_groups=sides, tiled=True)
        order = column_order(jnp.arange(chips, dtype=jnp.int32), fields)
        given = Piece(jnp.zeros((pairs, 2 * degrees, half), jnp.bfloat16))
        high, sent, _, _ = high_slots(0, [given], [1], [Piece(everyone, 0, 1)])
        got_high = Piece(lax.ppermute(sent, "lev", swap))
        high = Piece(high, 0, 0)
        low, sent, _ = low_slots(0, Piece(everyone, 0, 0), [], [])
        got_low = Piece(lax.ppermute(sent, "lev", swap))
        finish(0, [Piece(low), high, high], [got_low, got_high, got_high])
        return state["out"].reshape(slots, degrees, columns)

    sources = jnp.array(SOURCES, jnp.int32)[z]
    order = column_order(sources, fields)
    parts = given_parts(sizes)
    gives = len(parts)
    ready, table, give_mark, table_mark = [[None] * gives for _ in range(4)]
    both, again, low, halves_mark = [[None] * count for _ in range(4)]
    high, got_high, high_mark, found_low, got_low, low_mark, back, returned = [[None] * count for _ in range(8)]
    first_in, first_cross, second_cross = [[None] * count for _ in range(3)]
    first_out, second_out, third_out = [[None] * count for _ in range(3)]
    in_mark, out_mark, out2_mark, out3_mark = [[None] * count for _ in range(4)]
    inward, centre, outward = Links(), Links(), Links()
    last = count - 1

    def at(marks, i):
        return marks[i] if 0 <= i < len(marks) else None

    def do_give(i):
        s, n = parts[i] if i < gives else (0, 0)
        if n:
            block = block_pairs(s, n)
            line = (2 * degrees * half // LANES, LANES) if packs(2 * degrees, half) else (2 * degrees, half)
            ready[i], give_mark[i] = over_pairs(
                functools.partial(give_kernel, s), "give", n // block, info, waves, [legendre, other_table],
                table_specs(s, block, legendre), (jax.ShapeDtypeStruct((n, *line), jnp.bfloat16),),
                (pl.BlockSpec((block, *line), lambda j, *_: (j, 0, 0)),), after=state["mark"],
            )
            state["mark"] = (give_mark[i],)

    def send_table(i):
        if ready[i] is not None:
            _, table[i], table_mark[i] = inward.send(ready[i], GIVE)

    def prepare(i):
        both[i], again[i], low[i], halves_mark[i] = do_halves(i)

    def send_in(i):
        again[i], first_in[i], in_mark[i] = inward.send(again[i], INWARD)

    def send_cross(i):
        after = (at(out3_mark, i - 2),)
        meanwhile = (at(high_mark, i - 1), at(give_mark, i + 1), at(halves_mark, i + 1) if i else None)
        both[i], first_cross[i], _ = centre.send(both[i], CENTRE, after, meanwhile)

    def send_cross2(i):
        after = (at(out2_mark, i - 1),)
        meanwhile = (at(halves_mark, 1) if i == 0 else None, at(low_mark, i - 1))
        first_in[i], second_cross[i], _ = centre.send(first_in[i], CENTRE, after, meanwhile)

    def send_out():
        low[0], found, out_mark[0] = outward.send(low[0], OUTWARD)
        first_out[0] = Piece(found)

    def send_out2(i):
        meanwhile = (at(table_mark, i + 1),) if i == last else ()
        blocks = [first_cross[i][0]]
        if i < last:
            blocks.append(low[i + 1])
        if i > 0:
            blocks.append(returned[i - 1])
        _, found, out2_mark[i] = outward.send(jnp.concatenate(blocks), OUTWARD, (), meanwhile)
        second_out[i] = Piece(found)
        ahead = sizes[i]
        if i < last:
            first_out[i + 1] = Piece(found, ahead)
            ahead += sizes[i + 1]
        if i > 0:
            came_back(i - 1, found, ahead)

    def came_back(i, found, ahead):
        found = found.reshape(2 * found.shape[0], degrees, columns)
        back[i] = [Piece(found, 2 * ahead), Piece(found, 2 * ahead + sizes[i])]

    def do_high(i):
        pieces = [Piece(passed[i], 0, 1) for passed in (both, first_in, first_cross, second_cross)]
        s, n = chunks[i]
        block = block_pairs(s, n)
        given, ends = [], []
        for (start, size), array in zip(parts, table):
            if max(s, start) < min(s + n, start + size):
                given.append(Piece(array, s - start))
                ends.append((start + size - s) // block)
        high[i], sent, sent_back, high_mark[i] = high_slots(i, given, ends, pieces)
        got_high[i] = lax.ppermute(sent, "lev", swap)
        got_back = lax.ppermute(sent_back, "lev", swap)
        returned[i] = jnp.concatenate([high[i][1], got_back]).reshape(second_cross[i].shape[1:])

    def send_out3(i):
        _, found, out3_mark[i] = outward.send(second_cross[i][0], OUTWARD)
        third_out[i] = Piece(found)

    def send_back(i):
        _, found, _ = outward.send(returned[i], RETURN)
        came_back(i, found, 0)

    def do_low(i):
        passed = [Piece(array[i], 0, 0) for array in (first_in, first_cross, second_cross)]
        found_low[i], sent, low_mark[i] = low_slots(
            i, Piece(both[i], 0, 0), passed, [first_out[i], second_out[i], third_out[i]]
        )
        got_low[i] = lax.ppermute(sent, "lev", swap)

    def do_finish(i):
        finish(
            i,
            [Piece(found_low[i]), Piece(high[i], 0, 0), back[i][0]],
            [Piece(got_low[i]), Piece(got_high[i]), back[i][1]],
        )

    zonal_first()
    do_give(0)
    send_table(0)
    if count > 1:
        zonal_rest()
    prepare(0)
    send_in(0)
    do_give(1)
    send_cross(0)
    send_out()
    for i in range(count):
        if i == 0 and count > 1:
            prepare(1)
        send_table(i + 1)
        if i < last:
            send_in(i + 1)
        send_out2(i)
        if i > 0:
            do_low(i - 1)
            do_finish(i - 1)
        send_cross2(i)
        do_high(i)
        do_give(i + 2)
        if i + 2 < count:
            prepare(i + 2)
        if i < last:
            send_cross(i + 1)
        send_out3(i)
    send_back(last)
    do_low(last)
    do_finish(last)
    return state["out"].reshape(slots, degrees, columns)


def solution(mesh):
    in_specs = (P("lev", "lat", None), P("lat", "lev", None), P())
    out_specs = P("lat", "lev", None)
    return jax.shard_map(
        per_device, mesh=mesh, in_specs=in_specs, out_specs=out_specs, check_vma=False
    )
```

time: 500 us -> 246 us (0.49); the launches traced: 492 us -> 245 us
  waiting for transfers between devices: 206 us -> 86.7 us
  local copies, waits for them, and re-layouts: 119 us -> 15.7 us
  Pallas kernels: 0 us -> 75.9 us
  blocking collectives: 64.5 us -> 0 us
  matrix products: 62.8 us -> 0 us
  starting transfers between devices: 0.01 us -> 60.8 us
  other arithmetic: 26.8 us -> 4.64 us
  between operations: 13.7 us -> 0.81 us
    all_gather x1 -> x0, waiting for transfers between devices: 206 us -> none  [per_device(): piece = lax.all_gather(arrived, 'lev', axis=1, tiled=True)]
    ppermute x0 -> x31, waiting for transfers between devices: none -> 86.7 us  [the longest x21 85.1 us: send(): return lax.ppermute(block, 'lev', on_cores(pairs))]
    pallas_call x0 -> x57, Pallas kernels: none -> 75.9 us  [the longest x13 43.5 us: over_pairs(): pl.pallas_call(kernel, grid_spec=pltpu.PrefetchScalarGridSpec(num_scalar_...]
    all_to_all x1 -> x0, blocking collectives: 64.5 us -> none  [per_device(): lax.all_to_all(spec, 'lat', split_axis=0, concat_axis=3, tiled=True)]
    dot_general x3 -> x0, matrix products: 62.8 us -> none  [the longest x1 28.2 us: per_device(): jnp.einsum('lcs,frl->sfcr', table, grid_gradient, precision=lax.Precision...]
    ppermute x0 -> x31, starting transfers between devices: none -> 51.8 us  [the longest x21 49.6 us: send(): return lax.ppermute(block, 'lev', on_cores(pairs))]
    unnamed x8 -> x56, local copies, waits for them, and re-layouts: 49.2 us -> 11 us
    slice x2, local copies, waits for them, and re-layouts: 27.3 us -> 0.26 us  [the longest x1 0.25 us: per_device(): swapped = listed[:, 0] % 2 == 1]
  transfers between devices with their start and end apart: 1 -> 33, of which waited for: 1 -> 12; matrix products, arithmetic and copies ran while one was open for 5% -> 4% of each run, Pallas kernels for 0% -> 30%
where the time goes in v3:
time: 246 us; the launch traced here: 245 us
  waiting for transfers between devices  86.7 us (35%)
  Pallas kernels  75.9 us (31%)
  starting transfers between devices  60.8 us (25%)
  local copies, waits for them, and re-layouts  15.7 us (6%)
  other arithmetic  4.64 us (2%)
    ppermute x21, waiting for transfers between devices, send(): return lax.ppermute(block, 'lev', on_cores(pairs))  85.1 us
    ppermute x21, starting transfers between devices, send(): return lax.ppermute(block, 'lev', on_cores(pairs))  49.6 us
    pallas_call x13, Pallas kernels, over_pairs(): pl.pallas_call(kernel, grid_spec=pltpu.PrefetchScalarGridSpec(num_scalar_...  43.5 us
    pallas_call x3, Pallas kernels, halves(): pl.pallas_call(functools.partial(halves_kernel, fields, wide), grid=(1,),...  14.6 us
    unnamed x56, local copies, waits for them, and re-layouts  11 us
    pallas_call x1, Pallas kernels, zonal(): pl.pallas_call(functools.partial(zonal_kernel, start, sizes), grid=(colum...  9.99 us
    all_to_all x2, starting transfers between devices, exchange(): lax.all_to_all(found, ('lat', 'lev'), split_axis=0, concat_axis=0, axis_i...  8.99 us
    pallas_call x1, Pallas kernels, fold_and_zonal(): pl.pallas_call(functools.partial(fold_kernel, start, sizes, group), grid=...  7.7 us
  transfers between devices with their start and end apart: 33, of which 12 were waited for; matrix products, arithmetic and copies ran while one was open for 4% of the time, Pallas kernels for 30%

profile of v3, /device:TPU:0, one launch (start us, length us, event | category | flops | bytes accessed | tf_op | source)
XLA Modules:
  0.0 244.6 jit_solution(13210000235838335096)
XLA Ops:
  2.6 1.4 cosine_multiply_fusion
  4.3 7.7 %fold_and_zonal.1 = (bf16[8,32,1280]{2,1,0:T(8,128)(2,1)}, bf16[1280,640]{1,0:T(8,128)(2,1)S(1)}, bf16[1280,640]{1,0:T(8,128)(2,1)S(1)}, bf16[1280,640]{1,0:T(8,...) custom-call(f32[2,2,320,128]{3,2,1,0:T(8,128)S(1)} %pad_maximum_fusion.3.base_ref, ...), custom_call_target="tpu_custom_call" | custom-call | flops 1000 | bytes 1000 | tf_op jit(solution)/shard_map/fold_and_zonal/pallas_call | solution.py:96
  14.3 4.8 %all-to-all-start.1 = ((bf16[8,32,1280]{2,1,0:T(8,128)(2,1)}), bf16[8,32,1280]{2,1,0:T(8,128)(2,1)S(1)}, u32[]{:S(2)}, u32[]{:S(2)}) async-start(bf16[8,32,1280]{2,1,0:T(8,128)(2,1)} %get-tuple-element.120), calls=%async_computation.1 | async-start | bytes 1310720 | tf_op jit(solution)/shard_map/all_to_all | solution.py:504
  20.0 3.4 %give.4 = (bf16[8,400,128]{2,1,0:T(8,128)(2,1)}, f32[8,128]{1,0:T(8,128)S(1)}) custom-call(s32[1]{0:T(128)} %bitcast.info_ref, s32[80]{0:T(128)S(1)} %dynamic-slice_bitcast_fusion.waves_ref, bf16[160,80,320]{2,1,0:T(8,128)(2,1)} %own_ref.19, bf16[160,80,320]{2,1,0:T(8,128)(2,1)} %collective-permute-done.other_ref, f32[8,128]{1,0:T(8,128)S(1)} %get-tuple-element.117.refs_0_), custom_call_target="tpu_custom_call" | custom-call | flops 1000 | bytes 1000 | tf_op jit(solution)/shard_map/give/pallas_call | solution.py:316
  23.4 3.5 %collective-permute-start.1 = (bf16[8,400,128]{2,1,0:T(8,128)(2,1)}, bf16[8,400,128]{2,1,0:T(8,128)(2,1)S(1)}, u32[]{:S(2)}, u32[]{:S(2)}) collective-permute-start(bf16[8,400,128]{2,1,0:T(8,128)(2,1)} %get-tuple-element.130), channel_id=1, source_target_pairs={{0,2},{1,3},{8,10},{9,11},{16,18},{17,19},{24,26},{25,27}} | collective-permute-start | bytes 2457608 | tf_op jit(solution)/shard_map/ppermute | solution.py:409
  26.9 10.0 %zonal.1 = (bf16[8,128,1280]{2,1,0:T(8,128)(2,1)}, f32[8,128]{1,0:T(8,128)S(1)}) custom-call(f32[2,2,320,128]{3,2,1,0:T(8,128)S(1)} %pad_maximum_fusion.3.base_ref, f32[2,2,320,5]{3,2,1,0:T(8,128)S(1)} %copy.61.step_ref, f32[320,1]{1,0:T(8,128)S(1)} %fusion.7.first_ref, bf16[1280,640]{1,0:T(8,128)(2,1)S(1)} %copy-done.19, bf16[1280,640]{1,0:T(8,128)(2,1)S(1)} %copy-done.21, ...), custom_call_target="tpu_custom_call" | custom-call | flops 1000 | bytes 1000 | tf_op jit(solution)/shard_map/zonal/pallas_call | solution.py:137
  37.8 4.2 %all-to-all-start = ((bf16[8,128,1280]{2,1,0:T(8,128)(2,1)}), bf16[8,128,1280]{2,1,0:T(8,128)(2,1)S(1)}, u32[]{:S(2)}, u32[]{:S(2)}) async-start(bf16[8,128,1280]{2,1,0:T(8,128)(2,1)} %get-tuple-element.119), calls=%async_computation | async-start | bytes 5242880 | tf_op jit(solution)/shard_map/all_to_all | solution.py:504
  43.0 3.0 %halves.3 = (bf16[2,8,160,128]{3,2,1,0:T(8,128)(2,1)S(1)}, bf16[2,8,160,128]{3,2,1,0:T(8,128)(2,1)S(1)}, bf16[8,160,128]{2,1,0:T(8,128)(2,1)}, f32[8,128]{1,0:T(8,128)S(1)}) custom-call(bf16[8,32,1280]{2,1,0:T(8,128)(2,1)S(1)} %copy-done.17, f32[8,128]{1,0:T(8,128)S(1)} %get-tuple-element.121.refs_0_), custom_call_target="tpu_custom_call" | custom-call | flops 1000 | bytes 1000 | tf_op jit(solution)/shard_map/halves/pallas_call | solution.py:183
  47.0 3.6 %collective-permute-start.2 = (bf16[2,8,160,128]{3,2,1,0:T(8,128)(2,1)S(1)}, bf16[2,8,160,128]{3,2,1,0:T(8,128)(2,1)S(1)}, u32[]{:S(2)}, u32[]{:S(2)}) collective-permute-start(bf16[2,8,160,128]{3,2,1,0:T(8,128)(2,1)S(1)} %get-tuple-element.132), channel_id=1, source_target_pairs={{0,2},{1,3},{6,4},{7,5},{8,10},{9,11},{14,12},{15,13},{16,18},{17,... | collective-permute-start | bytes 1966088 | tf_op jit(solution)/shard_map/ppermute | solution.py:409
  51.3 3.1 %give.5 = (bf16[8,400,128]{2,1,0:T(8,128)(2,1)}, f32[8,128]{1,0:T(8,128)S(1)}) custom-call(s32[1]{0:T(128)} %bitcast.info_ref, s32[80]{0:T(128)S(1)} %dynamic-slice_bitcast_fusion.waves_ref, bf16[160,80,320]{2,1,0:T(8,128)(2,1)} %own_ref.19, bf16[160,80,320]{2,1,0:T(8,128)(2,1)} %collective-permute-done.other_ref, f32[8,128]{1,0:T(8,128)S(1)} %get-tuple-element.122.refs_0_), custom_call_target="tpu_custom_call" | custom-call | flops 1000 | bytes 1000 | tf_op jit(solution)/shard_map/give/pallas_call | solution.py:316
  54.4 10.0 %collective-permute-done.2.refs_0_ = bf16[2,8,160,128]{3,2,1,0:T(8,128)(2,1)S(1)} collective-permute-done((bf16[2,8,160,128]{3,2,1,0:T(8,128)(2,1)S(1)}, bf16[2,8,160,128]{3,2,1,0:T(8,128)(2,1)S(1)}, u32[]{:S(2)}, u32[]{:S(2)}) %collective-permute-start.2) | collective-permute-done | bytes 655392 | tf_op jit(solution)/shard_map/ppermute | solution.py:409
  64.4 5.3 %collective-permute-start.3 = (bf16[8,400,128]{2,1,0:T(8,128)(2,1)}, bf16[8,400,128]{2,1,0:T(8,128)(2,1)}, u32[]{:S(2)}, u32[]{:S(2)}) collective-permute-start(bf16[8,400,128]{2,1,0:T(8,128)(2,1)} %get-tuple-element.134), channel_id=1, source_target_pairs={{0,2},{1,3},{8,10},{9,11},{16,18},{17,19},{24,26},{25,27}} | collective-permute-start | bytes 2457608 | tf_op jit(solution)/shard_map/ppermute | solution.py:409
  70.6 1.5 collective-permute-start.6
  72.1 1.3 collective-permute-start.8
  73.4 9.1 %collective-permute-done.8.refs_0_ = bf16[8,160,128]{2,1,0:T(8,128)(2,1)} collective-permute-done((bf16[8,160,128]{2,1,0:T(8,128)(2,1)}, bf16[8,160,128]{2,1,0:T(8,128)(2,1)}, u32[]{:S(2)}, u32[]{:S(2)}) %collective-permute-start.8) | collective-permute-done | bytes 327712 | tf_op jit(solution)/shard_map/ppermute | solution.py:409
  82.5 5.8 %halves.4 = (bf16[2,16,160,128]{3,2,1,0:T(8,128)(2,1)}, bf16[2,16,160,128]{3,2,1,0:T(8,128)(2,1)}, bf16[16,160,128]{2,1,0:T(8,128)(2,1)S(1)}, f32[8,128]{1,0:T(8,128)S(1)}) custom-call(bf16[8,128,1280]{2,1,0:T(8,128)(2,1)S(1)} %all-to-all-done.in_ref, f32[8,128]{1,0:T(8,128)S(1)} %get-tuple-element.123.refs_0_.refs_1_), custom_call_target="tpu_custom_call" | custom-call | flops 1000 | bytes 1000 | tf_op jit(solution)/shard_map/halves/pallas_call | solution.py:183
  88.3 1.9 collective-permute-start.7
  90.2 2.8 %collective-permute-start.4 = (bf16[2,16,160,128]{3,2,1,0:T(8,128)(2,1)}, bf16[2,16,160,128]{3,2,1,0:T(8,128)(2,1)}, u32[]{:S(2)}, u32[]{:S(2)}) collective-permute-start(bf16[2,16,160,128]{3,2,1,0:T(8,128)(2,1)} %get-tuple-element.136), channel_id=1, source_target_pairs={{0,2},{1,3},{6,4},{7,5},{8,10},{9,11},{14,12},{15,13},{16,18},{17,... | collective-permute-start | bytes 3932168 | tf_op jit(solution)/shard_map/ppermute | solution.py:409
  94.0 1.5 collective-permute-start.9
  99.7 3.2 %high_slots.3 = (bf16[2,8,80,128]{3,2,1,0:T(8,128)(2,1)S(1)}, bf16[8,80,128]{2,1,0:T(8,128)(2,1)S(1)}, bf16[8,80,128]{2,1,0:T(8,128)(2,1)S(1)}, f32[8,128]{1,0:T(8,128)S(1)}) custom-call(s32[1]{0:T(128)} %bitcast.info_ref, s32[80]{0:T(128)S(1)} %dynamic-slice_bitcast_fusion.waves_ref, bf16[128,128]{1,0:T(8,128)(2,1)S(1)} %fusion.10.order_ref, ...), custom_call_target="tpu_custom_call" | custom-call | flops 1000 | bytes 1000 | tf_op jit(solution)/shard_map/high_slots/pallas_call | solution.py:316
  103.1 2.8 %give.6 = (bf16[16,400,128]{2,1,0:T(8,128)(2,1)S(1)}, f32[8,128]{1,0:T(8,128)S(1)}) custom-call(s32[1]{0:T(128)} %bitcast.info_ref, s32[80]{0:T(128)S(1)} %dynamic-slice_bitcast_fusion.waves_ref, bf16[160,80,320]{2,1,0:T(8,128)(2,1)} %own_ref.19, bf16[160,80,320]{2,1,0:T(8,128)(2,1)} %collective-permute-done.other_ref, ...), custom_call_target="tpu_custom_call" | custom-call | flops 1000 | bytes 1000 | tf_op jit(solution)/shard_map/give/pallas_call | solution.py:316
  105.9 5.8 %halves.5 = (bf16[2,16,160,128]{3,2,1,0:T(8,128)(2,1)}, bf16[2,16,160,128]{3,2,1,0:T(8,128)(2,1)}, bf16[16,160,128]{2,1,0:T(8,128)(2,1)S(1)}, f32[8,128]{1,0:T(8,128)S(1)}) custom-call(bf16[8,128,1280]{2,1,0:T(8,128)(2,1)S(1)} %all-to-all-done.in_ref, f32[8,128]{1,0:T(8,128)S(1)} %get-tuple-element.125.refs_0_.refs_2_), custom_call_target="tpu_custom_call" | custom-call | flops 1000 | bytes 1000 | tf_op jit(solution)/shard_map/halves/pallas_call | solution.py:183
  112.7 4.5 %collective-permute-done.9.refs_0_ = bf16[24,160,128]{2,1,0:T(8,128)(2,1)} collective-permute-done((bf16[24,160,128]{2,1,0:T(8,128)(2,1)}, bf16[24,160,128]{2,1,0:T(8,128)(2,1)}, u32[]{:S(2)}, u32[]{:S(2)}) %collective-permute-start.9) | collective-permute-done | bytes 983072 | tf_op jit(solution)/shard_map/ppermute | solution.py:409
  117.2 1.3 collective-permute-start.11
  119.4 7.6 %collective-permute-start.12 = (bf16[16,400,128]{2,1,0:T(8,128)(2,1)S(1)}, bf16[16,400,128]{2,1,0:T(8,128)(2,1)S(1)}, u32[]{:S(2)}, u32[]{:S(2)}) collective-permute-start(bf16[16,400,128]{2,1,0:T(8,128)(2,1)S(1)} %get-tuple-element.168), channel_id=1, source_target_pairs={{0,2},{1,3},{8,10},{9,11},{16,18},{17,19},{24,26},{25,27}} | collective-permute-start | bytes 4915208 | tf_op jit(solution)/shard_map/ppermute | solution.py:409
  128.3 1.4 collective-permute-start.16
  129.8 3.2 %low_slots.3 = (bf16[8,80,128]{2,1,0:T(8,128)(2,1)S(1)}, bf16[8,80,128]{2,1,0:T(8,128)(2,1)S(1)}, f32[8,128]{1,0:T(8,128)S(1)}) custom-call(s32[1]{0:T(128)} %bitcast.info_ref, s32[80]{0:T(128)S(1)} %dynamic-slice_bitcast_fusion.waves_ref, bf16[128,128]{1,0:T(8,128)(2,1)S(1)} %fusion.10.order_ref, bf16[160,80,320]{2,1,0:T(8,128)(2,1)} %own_ref.19, ...), custom_call_target="tpu_custom_call" | custom-call | flops 1000 | bytes 1000 | tf_op jit(solution)/shard_map/low_slots/pallas_call | solution.py:316
  134.4 24.5 %collective-permute-done.12.refs_0_ = bf16[16,400,128]{2,1,0:T(8,128)(2,1)S(1)} collective-permute-done((bf16[16,400,128]{2,1,0:T(8,128)(2,1)S(1)}, bf16[16,400,128]{2,1,0:T(8,128)(2,1)S(1)}, u32[]{:S(2)}, u32[]{:S(2)}) %collective-permute-start.12) | collective-permute-done | bytes 1638432 | tf_op jit(solution)/shard_map/ppermute | solution.py:409
  158.9 4.5 %collective-permute-start.13 = (bf16[2,16,160,128]{3,2,1,0:T(8,128)(2,1)}, bf16[2,16,160,128]{3,2,1,0:T(8,128)(2,1)S(1)}, u32[]{:S(2)}, u32[]{:S(2)}) collective-permute-start(bf16[2,16,160,128]{3,2,1,0:T(8,128)(2,1)} %get-tuple-element.170), channel_id=1, source_target_pairs={{0,2},{1,3},{6,4},{7,5},{8,10},{9,11},{14,12},{15,13},{16,18},{17,... | collective-permute-start | bytes 3932168 | tf_op jit(solution)/shard_map/ppermute | solution.py:409
  164.7 1.3 collective-permute-start.18
  165.9 5.3 %high_slots.4 = (bf16[2,16,80,128]{3,2,1,0:T(8,128)(2,1)S(1)}, bf16[16,80,128]{2,1,0:T(8,128)(2,1)S(1)}, bf16[16,80,128]{2,1,0:T(8,128)(2,1)S(1)}, f32[8,128]{1,0:T(8,128)S(1)}) custom-call(s32[1]{0:T(128)} %bitcast.info_ref, s32[80]{0:T(128)S(1)} %dynamic-slice_bitcast_fusion.waves_ref, bf16[128,128]{1,0:T(8,128)(2,1)S(1)} %fusion.10.order_ref, ...), custom_call_target="tpu_custom_call" | custom-call | flops 1000 | bytes 1000 | tf_op jit(solution)/shard_map/high_slots/pallas_call | solution.py:316
  171.4 2.2 give.7
  173.7 5.2 %collective-permute-done.18.refs_0_ = bf16[16,160,128]{2,1,0:T(8,128)(2,1)S(1)} collective-permute-done((bf16[16,160,128]{2,1,0:T(8,128)(2,1)S(1)}, bf16[16,160,128]{2,1,0:T(8,128)(2,1)S(1)}, u32[]{:S(2)}, u32[]{:S(2)}) %collective-permute-start.18) | collective-permute-done | bytes 655392 | tf_op jit(solution)/shard_map/ppermute | solution.py:409
  179.0 1.3 collective-permute-start.20
  180.3 7.4 %collective-permute-done.13.refs_0_ = bf16[2,16,160,128]{3,2,1,0:T(8,128)(2,1)S(1)} collective-permute-done((bf16[2,16,160,128]{3,2,1,0:T(8,128)(2,1)}, bf16[2,16,160,128]{3,2,1,0:T(8,128)(2,1)S(1)}, u32[]{:S(2)}, u32[]{:S(2)}) %collective-permute-start.13) | collective-permute-done | bytes 1310752 | tf_op jit(solution)/shard_map/ppermute | solution.py:409
  188.5 5.5 %collective-permute-start.21 = (bf16[8,400,128]{2,1,0:T(8,128)(2,1)S(1)}, bf16[8,400,128]{2,1,0:T(8,128)(2,1)S(1)}, u32[]{:S(2)}, u32[]{:S(2)}) collective-permute-start(bf16[8,400,128]{2,1,0:T(8,128)(2,1)S(1)} %get-tuple-element.197), channel_id=1, source_target_pairs={{0,2},{1,3},{8,10},{9,11},{16,18},{17,19},{24,26},{25,27}} | collective-permute-start | bytes 2457608 | tf_op jit(solution)/shard_map/ppermute | solution.py:409
  194.0 4.7 %low_slots.4 = (bf16[16,80,128]{2,1,0:T(8,128)(2,1)S(1)}, bf16[16,80,128]{2,1,0:T(8,128)(2,1)S(1)}, f32[8,128]{1,0:T(8,128)S(1)}) custom-call(s32[1]{0:T(128)} %bitcast.info_ref, s32[80]{0:T(128)S(1)} %dynamic-slice_bitcast_fusion.waves_ref, bf16[128,128]{1,0:T(8,128)(2,1)S(1)} %fusion.10.order_ref, bf16[160,80,320]{2,1,0:T(8,128)(2,1)} %own_ref.19, ...), custom_call_target="tpu_custom_call" | custom-call | flops 1000 | bytes 1000 | tf_op jit(solution)/shard_map/low_slots/pallas_call | solution.py:316
  198.8 7.9 %collective-permute-done.21.refs_0_ = bf16[8,400,128]{2,1,0:T(8,128)(2,1)S(1)} collective-permute-done((bf16[8,400,128]{2,1,0:T(8,128)(2,1)S(1)}, bf16[8,400,128]{2,1,0:T(8,128)(2,1)S(1)}, u32[]{:S(2)}, u32[]{:S(2)}) %collective-permute-start.21) | collective-permute-done | bytes 819232 | tf_op jit(solution)/shard_map/ppermute | solution.py:409
  208.3 1.3 collective-permute-start.22
  209.6 5.5 %high_slots.5 = (bf16[2,16,80,128]{3,2,1,0:T(8,128)(2,1)S(1)}, bf16[16,80,128]{2,1,0:T(8,128)(2,1)S(1)}, bf16[16,80,128]{2,1,0:T(8,128)(2,1)S(1)}, f32[8,128]{1,0:T(8,128)}) custom-call(s32[1]{0:T(128)} %bitcast.info_ref, s32[80]{0:T(128)S(1)} %dynamic-slice_bitcast_fusion.waves_ref, bf16[128,128]{1,0:T(8,128)(2,1)S(1)} %fusion.10.order_ref, ...), custom_call_target="tpu_custom_call" | custom-call | flops 1000 | bytes 1000 | tf_op jit(solution)/shard_map/high_slots/pallas_call | solution.py:316
  215.2 1.6 collective-permute-done.23
  216.8 11.3 %collective-permute-done.22.refs_0_ = bf16[16,160,128]{2,1,0:T(8,128)(2,1)S(1)} collective-permute-done((bf16[16,160,128]{2,1,0:T(8,128)(2,1)S(1)}, bf16[16,160,128]{2,1,0:T(8,128)(2,1)S(1)}, u32[]{:S(2)}, u32[]{:S(2)}) %collective-permute-start.22) | collective-permute-done | bytes 655392 | tf_op jit(solution)/shard_map/ppermute | solution.py:409
  228.1 1.3 collective-permute-start.24
  230.5 4.8 %low_slots.5 = (bf16[16,80,128]{2,1,0:T(8,128)(2,1)S(1)}, bf16[16,80,128]{2,1,0:T(8,128)(2,1)S(1)}, f32[8,128]{1,0:T(8,128)}) custom-call(s32[1]{0:T(128)} %bitcast.info_ref, s32[80]{0:T(128)S(1)} %dynamic-slice_bitcast_fusion.waves_ref, bf16[128,128]{1,0:T(8,128)(2,1)S(1)} %fusion.10.order_ref, bf16[160,80,320]{2,1,0:T(8,128)(2,1)} %own_ref.19, ...), custom_call_target="tpu_custom_call" | custom-call | flops 1000 | bytes 1000 | tf_op jit(solution)/shard_map/low_slots/pallas_call | solution.py:316
  235.8 1.5 finish.3
  237.3 1.9 finish.4
  239.3 3.4 %collective-permute-done.24.refs_0_ = bf16[16,160,128]{2,1,0:T(8,128)(2,1)S(1)} collective-permute-done((bf16[16,160,128]{2,1,0:T(8,128)(2,1)S(1)}, bf16[16,160,128]{2,1,0:T(8,128)(2,1)S(1)}, u32[]{:S(2)}, u32[]{:S(2)}) %collective-permute-start.24) | collective-permute-done | bytes 655392 | tf_op jit(solution)/shard_map/ppermute | solution.py:409
  242.7 1.9 finish.5
  (171 shorter events, 26.0 us)
Async XLA Ops:
  0.0 20.0 %collective-permute-start = (bf16[160,80,320]{2,1,0:T(8,128)(2,1)}, bf16[160,80,320]{2,1,0:T(8,128)(2,1)}, u32[]{:S(2)}, u32[]{:S(2)}) collective-permute-start(bf16[160,80,320]{2,1,0:T(8,128)(2,1)} %own_ref.19), channel_id=1, source_target_pairs={{0,1},{1,0},{2,3},{3,2},{4,5},{5,4},{6,7},{7,6},{8,9},{9,8},{10,11... | collective-permute-start | bytes 24576008 | tf_op jit(solution)/shard_map/ppermute | solution.py:499
  14.3 22.6 %all-to-all-start.1 = ((bf16[8,32,1280]{2,1,0:T(8,128)(2,1)}), bf16[8,32,1280]{2,1,0:T(8,128)(2,1)S(1)}, u32[]{:S(2)}, u32[]{:S(2)}) async-start(bf16[8,32,1280]{2,1,0:T(8,128)(2,1)} %get-tuple-element.120), calls=%async_computation.1 | async-start | bytes 1310720 | tf_op jit(solution)/shard_map/all_to_all | solution.py:504
  20.0 6.9 %copy-start.19 = (bf16[1280,640]{1,0:T(8,128)(2,1)S(1)}, bf16[1280,640]{1,0:T(8,128)(2,1)}, u32[]{:S(2)}) copy-start(bf16[1280,640]{1,0:T(8,128)(2,1)} %copy-done.18) | copy-start | bytes 4915204
  20.0 6.9 %copy-start.21 = (bf16[1280,640]{1,0:T(8,128)(2,1)S(1)}, bf16[1280,640]{1,0:T(8,128)(2,1)}, u32[]{:S(2)}) copy-start(bf16[1280,640]{1,0:T(8,128)(2,1)} %copy-done.20) | copy-start | bytes 4915204
  23.4 22.7 %collective-permute-start.1 = (bf16[8,400,128]{2,1,0:T(8,128)(2,1)}, bf16[8,400,128]{2,1,0:T(8,128)(2,1)S(1)}, u32[]{:S(2)}, u32[]{:S(2)}) collective-permute-start(bf16[8,400,128]{2,1,0:T(8,128)(2,1)} %get-tuple-element.130), channel_id=1, source_target_pairs={{0,2},{1,3},{8,10},{9,11},{16,18},{17,19},{24,26},{25,27}} | collective-permute-start | bytes 2457608 | tf_op jit(solution)/shard_map/ppermute | solution.py:409
  37.8 44.7 %all-to-all-start = ((bf16[8,128,1280]{2,1,0:T(8,128)(2,1)}), bf16[8,128,1280]{2,1,0:T(8,128)(2,1)S(1)}, u32[]{:S(2)}, u32[]{:S(2)}) async-start(bf16[8,128,1280]{2,1,0:T(8,128)(2,1)} %get-tuple-element.119), calls=%async_computation | async-start | bytes 5242880 | tf_op jit(solution)/shard_map/all_to_all | solution.py:504
  46.0 8.3 %copy-start.13 = (bf16[2,8,160,128]{3,2,1,0:T(8,128)(2,1)}, bf16[2,8,160,128]{3,2,1,0:T(8,128)(2,1)S(1)}, u32[]{:S(2)}) copy-start(bf16[2,8,160,128]{3,2,1,0:T(8,128)(2,1)S(1)} %get-tuple-element.140.refs_0_) | copy-start | bytes 1966084
  47.0 17.4 %collective-permute-start.2 = (bf16[2,8,160,128]{3,2,1,0:T(8,128)(2,1)S(1)}, bf16[2,8,160,128]{3,2,1,0:T(8,128)(2,1)S(1)}, u32[]{:S(2)}, u32[]{:S(2)}) collective-permute-start(bf16[2,8,160,128]{3,2,1,0:T(8,128)(2,1)S(1)} %get-tuple-element.132), channel_id=1, source_target_pairs={{0,2},{1,3},{6,4},{7,5},{8,10},{9,11},{14,12},{15,13},{16,18},{17,... | collective-permute-start | bytes 1966088 | tf_op jit(solution)/shard_map/ppermute | solution.py:409
  50.6 19.1 %collective-permute-start.5 = (bf16[2,8,160,128]{3,2,1,0:T(8,128)(2,1)S(1)}, bf16[2,8,160,128]{3,2,1,0:T(8,128)(2,1)S(1)}, u32[]{:S(2)}, u32[]{:S(2)}) collective-permute-start(bf16[2,8,160,128]{3,2,1,0:T(8,128)(2,1)S(1)} %get-tuple-element.140.refs_0_), channel_id=1, source_target_pairs={{2,4},{3,5},{4,2},{5,3},{10,12},{11,13},{12,10},{13,11},{18,20},{1... | collective-permute-start | bytes 1966088 | tf_op jit(solution)/shard_map/ppermute | solution.py:409
  64.4 25.8 %collective-permute-start.3 = (bf16[8,400,128]{2,1,0:T(8,128)(2,1)}, bf16[8,400,128]{2,1,0:T(8,128)(2,1)}, u32[]{:S(2)}, u32[]{:S(2)}) collective-permute-start(bf16[8,400,128]{2,1,0:T(8,128)(2,1)} %get-tuple-element.134), channel_id=1, source_target_pairs={{0,2},{1,3},{8,10},{9,11},{16,18},{17,19},{24,26},{25,27}} | collective-permute-start | bytes 2457608 | tf_op jit(solution)/shard_map/ppermute | solution.py:409
  70.6 17.7 %collective-permute-start.6 = (bf16[2,8,160,128]{3,2,1,0:T(8,128)(2,1)S(1)}, bf16[2,8,160,128]{3,2,1,0:T(8,128)(2,1)}, u32[]{:S(2)}, u32[]{:S(2)}) collective-permute-start(bf16[2,8,160,128]{3,2,1,0:T(8,128)(2,1)S(1)} %get-tuple-element.142.refs_1_), channel_id=1, source_target_pairs={{2,4},{3,5},{4,2},{5,3},{10,12},{11,13},{12,10},{13,11},{18,20},{1... | collective-permute-start | bytes 1966088 | tf_op jit(solution)/shard_map/ppermute | solution.py:409
  72.1 10.4 %collective-permute-start.8 = (bf16[8,160,128]{2,1,0:T(8,128)(2,1)}, bf16[8,160,128]{2,1,0:T(8,128)(2,1)}, u32[]{:S(2)}, u32[]{:S(2)}) collective-permute-start(bf16[8,160,128]{2,1,0:T(8,128)(2,1)} %get-tuple-element.152), channel_id=1, source_target_pairs={{2,0},{3,1},{4,6},{5,7},{10,8},{11,9},{12,14},{13,15},{18,16},{19,... | collective-permute-start | bytes 983048 | tf_op jit(solution)/shard_map/ppermute | solution.py:409
  88.3 4.6 %copy-start.8 = (bf16[2,8,160,128]{3,2,1,0:T(8,128)(2,1)S(1)}, bf16[2,8,160,128]{3,2,1,0:T(8,128)(2,1)}, u32[]{:S(2)}) copy-start(bf16[2,8,160,128]{3,2,1,0:T(8,128)(2,1)} %copy-done.7) | copy-start | bytes 1966084
  88.3 30.3 %collective-permute-start.7 = (bf16[2,16,160,128]{3,2,1,0:T(8,128)(2,1)}, bf16[2,16,160,128]{3,2,1,0:T(8,128)(2,1)}, u32[]{:S(2)}, u32[]{:S(2)}) collective-permute-start(bf16[2,16,160,128]{3,2,1,0:T(8,128)(2,1)} %get-tuple-element.144.refs_0_), channel_id=1, source_target_pairs={{2,4},{3,5},{4,2},{5,3},{10,12},{11,13},{12,10},{13,11},{18,20},{1... | collective-permute-start | bytes 3932168 | tf_op jit(solution)/shard_map/ppermute | solution.py:409
  90.2 28.4 %collective-permute-start.4 = (bf16[2,16,160,128]{3,2,1,0:T(8,128)(2,1)}, bf16[2,16,160,128]{3,2,1,0:T(8,128)(2,1)}, u32[]{:S(2)}, u32[]{:S(2)}) collective-permute-start(bf16[2,16,160,128]{3,2,1,0:T(8,128)(2,1)} %get-tuple-element.136), channel_id=1, source_target_pairs={{0,2},{1,3},{6,4},{7,5},{8,10},{9,11},{14,12},{15,13},{16,18},{17,... | collective-permute-start | bytes 3932168 | tf_op jit(solution)/shard_map/ppermute | solution.py:409
  94.0 23.2 %collective-permute-start.9 = (bf16[24,160,128]{2,1,0:T(8,128)(2,1)}, bf16[24,160,128]{2,1,0:T(8,128)(2,1)}, u32[]{:S(2)}, u32[]{:S(2)}) collective-permute-start(bf16[24,160,128]{2,1,0:T(8,128)(2,1)} %get-tuple-element.154), channel_id=1, source_target_pairs={{2,0},{3,1},{4,6},{5,7},{10,8},{11,9},{12,14},{13,15},{18,16},{19,... | collective-permute-start | bytes 2949128 | tf_op jit(solution)/shard_map/ppermute | solution.py:409
  103.0 2.9 %copy-start.24 = (bf16[8,80,128]{2,1,0:T(8,128)(2,1)}, bf16[8,80,128]{2,1,0:T(8,128)(2,1)S(1)}, u32[]{:S(2)}) copy-start(bf16[8,80,128]{2,1,0:T(8,128)(2,1)S(1)} %get-tuple-element.217) | copy-start | bytes 491524
  103.0 9.7 %copy-start.22 = (bf16[2,8,80,128]{3,2,1,0:T(8,128)(2,1)}, bf16[2,8,80,128]{3,2,1,0:T(8,128)(2,1)S(1)}, u32[]{:S(2)}) copy-start(bf16[2,8,80,128]{3,2,1,0:T(8,128)(2,1)S(1)} %get-tuple-element.180.refs_1_) | copy-start | bytes 983044
  103.0 15.5 %collective-permute-start.15 = (bf16[8,80,128]{2,1,0:T(8,128)(2,1)S(1)}, bf16[8,80,128]{2,1,0:T(8,128)(2,1)S(1)}, u32[]{:S(2)}, u32[]{:S(2)}) collective-permute-start(bf16[8,80,128]{2,1,0:T(8,128)(2,1)S(1)} %get-tuple-element.181), channel_id=1, source_target_pairs={{0,1},{1,0},{2,3},{3,2},{4,5},{5,4},{6,7},{7,6},{8,9},{9,8},{10,11... | collective-permute-start | bytes 491528 | tf_op jit(solution)/shard_map/ppermute | solution.py:678
  117.2 10.9 %collective-permute-start.11 = (bf16[8,160,128]{2,1,0:T(8,128)(2,1)S(1)}, bf16[8,160,128]{2,1,0:T(8,128)(2,1)S(1)}, u32[]{:S(2)}, u32[]{:S(2)}) collective-permute-start(bf16[8,160,128]{2,1,0:T(8,128)(2,1)S(1)} %get-tuple-element.159), channel_id=1, source_target_pairs={{2,0},{3,1},{4,6},{5,7},{10,8},{11,9},{12,14},{13,15},{18,16},{19,... | collective-permute-start | bytes 983048 | tf_op jit(solution)/shard_map/ppermute | solution.py:409
  118.6 14.4 %collective-permute-start.10 = (bf16[2,16,160,128]{3,2,1,0:T(8,128)(2,1)}, bf16[2,16,160,128]{3,2,1,0:T(8,128)(2,1)S(1)}, u32[]{:S(2)}, u32[]{:S(2)}) collective-permute-start(bf16[2,16,160,128]{3,2,1,0:T(8,128)(2,1)} %get-tuple-element.156.refs_1_), channel_id=1, source_target_pairs={{2,4},{3,5},{4,2},{5,3},{10,12},{11,13},{12,10},{13,11},{18,20},{1... | collective-permute-start | bytes 3932168 | tf_op jit(solution)/shard_map/ppermute | solution.py:409
  119.4 39.5 %collective-permute-start.12 = (bf16[16,400,128]{2,1,0:T(8,128)(2,1)S(1)}, bf16[16,400,128]{2,1,0:T(8,128)(2,1)S(1)}, u32[]{:S(2)}, u32[]{:S(2)}) collective-permute-start(bf16[16,400,128]{2,1,0:T(8,128)(2,1)S(1)} %get-tuple-element.168), channel_id=1, source_target_pairs={{0,2},{1,3},{8,10},{9,11},{16,18},{17,19},{24,26},{25,27}} | collective-permute-start | bytes 4915208 | tf_op jit(solution)/shard_map/ppermute | solution.py:409
  128.3 36.3 %collective-permute-start.16 = (bf16[40,160,128]{2,1,0:T(8,128)(2,1)S(1)}, bf16[40,160,128]{2,1,0:T(8,128)(2,1)S(1)}, u32[]{:S(2)}, u32[]{:S(2)}) collective-permute-start(bf16[40,160,128]{2,1,0:T(8,128)(2,1)S(1)} %get-tuple-element.182), channel_id=1, source_target_pairs={{2,0},{3,1},{4,6},{5,7},{10,8},{11,9},{12,14},{13,15},{18,16},{19,... | collective-permute-start | bytes 4915208 | tf_op jit(solution)/shard_map/ppermute | solution.py:409
  133.0 30.4 %copy-start.4 = (bf16[2,16,160,128]{3,2,1,0:T(8,128)(2,1)}, bf16[2,16,160,128]{3,2,1,0:T(8,128)(2,1)S(1)}, u32[]{:S(2)}) copy-start(bf16[2,16,160,128]{3,2,1,0:T(8,128)(2,1)S(1)} %get-tuple-element.173.refs_3_) | copy-start | bytes 3932164
  133.6 45.2 %collective-permute-start.14 = (bf16[2,16,160,128]{3,2,1,0:T(8,128)(2,1)}, bf16[2,16,160,128]{3,2,1,0:T(8,128)(2,1)S(1)}, u32[]{:S(2)}, u32[]{:S(2)}) collective-permute-start(bf16[2,16,160,128]{3,2,1,0:T(8,128)(2,1)} %get-tuple-element.164.refs_0_), channel_id=1, source_target_pairs={{2,4},{3,5},{4,2},{5,3},{10,12},{11,13},{12,10},{13,11},{18,20},{1... | collective-permute-start | bytes 3932168 | tf_op jit(solution)/shard_map/ppermute | solution.py:409
  158.9 4.5 %copy-start.6 = (bf16[16,400,128]{2,1,0:T(8,128)(2,1)}, bf16[16,400,128]{2,1,0:T(8,128)(2,1)S(1)}, u32[]{:S(2)}) copy-start(bf16[16,400,128]{2,1,0:T(8,128)(2,1)S(1)} %get-tuple-element.175.refs_5_.refs_4_) | copy-start | bytes 4915204
  158.9 28.8 %collective-permute-start.13 = (bf16[2,16,160,128]{3,2,1,0:T(8,128)(2,1)}, bf16[2,16,160,128]{3,2,1,0:T(8,128)(2,1)S(1)}, u32[]{:S(2)}, u32[]{:S(2)}) collective-permute-start(bf16[2,16,160,128]{3,2,1,0:T(8,128)(2,1)} %get-tuple-element.170), channel_id=1, source_target_pairs={{0,2},{1,3},{6,4},{7,5},{8,10},{9,11},{14,12},{15,13},{16,18},{17,... | collective-permute-start | bytes 3932168 | tf_op jit(solution)/shard_map/ppermute | solution.py:409
  164.7 6.6 %copy-start = (bf16[40,160,128]{2,1,0:T(8,128)(2,1)}, bf16[40,160,128]{2,1,0:T(8,128)(2,1)S(1)}, u32[]{:S(2)}) copy-start(bf16[40,160,128]{2,1,0:T(8,128)(2,1)S(1)} %get-tuple-element.186.refs_5_.refs_4_) | copy-start | bytes 4915204
  164.7 14.2 %collective-permute-start.18 = (bf16[16,160,128]{2,1,0:T(8,128)(2,1)S(1)}, bf16[16,160,128]{2,1,0:T(8,128)(2,1)S(1)}, u32[]{:S(2)}, u32[]{:S(2)}) collective-permute-start(bf16[16,160,128]{2,1,0:T(8,128)(2,1)S(1)} %get-tuple-element.187), channel_id=1, source_target_pairs={{2,0},{3,1},{4,6},{5,7},{10,8},{11,9},{12,14},{13,15},{18,16},{19,... | collective-permute-start | bytes 1966088 | tf_op jit(solution)/shard_map/ppermute | solution.py:409
  171.3 2.3 collective-permute-start.19
  179.0 28.2 %collective-permute-start.20 = (bf16[32,160,128]{2,1,0:T(8,128)(2,1)S(1)}, bf16[32,160,128]{2,1,0:T(8,128)(2,1)S(1)}, u32[]{:S(2)}, u32[]{:S(2)}) collective-permute-start(bf16[32,160,128]{2,1,0:T(8,128)(2,1)S(1)} %get-tuple-element.194), channel_id=1, source_target_pairs={{2,0},{3,1},{4,6},{5,7},{10,8},{11,9},{12,14},{13,15},{18,16},{19,... | collective-permute-start | bytes 3932168 | tf_op jit(solution)/shard_map/ppermute | solution.py:409
  187.8 19.5 %collective-permute-start.17 = (bf16[2,16,160,128]{3,2,1,0:T(8,128)(2,1)S(1)}, bf16[2,16,160,128]{3,2,1,0:T(8,128)(2,1)S(1)}, u32[]{:S(2)}, u32[]{:S(2)}) collective-permute-start(bf16[2,16,160,128]{3,2,1,0:T(8,128)(2,1)S(1)} %get-tuple-element.184.refs_1_), channel_id=1, source_target_pairs={{2,4},{3,5},{4,2},{5,3},{10,12},{11,13},{12,10},{13,11},{18,20},{1... | collective-permute-start | bytes 3932168 | tf_op jit(solution)/shard_map/ppermute | solution.py:409
  188.5 18.1 %collective-permute-start.21 = (bf16[8,400,128]{2,1,0:T(8,128)(2,1)S(1)}, bf16[8,400,128]{2,1,0:T(8,128)(2,1)S(1)}, u32[]{:S(2)}, u32[]{:S(2)}) collective-permute-start(bf16[8,400,128]{2,1,0:T(8,128)(2,1)S(1)} %get-tuple-element.197), channel_id=1, source_target_pairs={{0,2},{1,3},{8,10},{9,11},{16,18},{17,19},{24,26},{25,27}} | collective-permute-start | bytes 2457608 | tf_op jit(solution)/shard_map/ppermute | solution.py:409
  207.3 2.3 copy-start.5
  208.3 19.7 %collective-permute-start.22 = (bf16[16,160,128]{2,1,0:T(8,128)(2,1)S(1)}, bf16[16,160,128]{2,1,0:T(8,128)(2,1)S(1)}, u32[]{:S(2)}, u32[]{:S(2)}) collective-permute-start(bf16[16,160,128]{2,1,0:T(8,128)(2,1)S(1)} %get-tuple-element.201), channel_id=1, source_target_pairs={{2,0},{3,1},{4,6},{5,7},{10,8},{11,9},{12,14},{13,15},{18,16},{19,... | collective-permute-start | bytes 1966088 | tf_op jit(solution)/shard_map/ppermute | solution.py:409
  215.1 1.6 collective-permute-start.23
  215.2 14.2 %copy-start.25 = (bf16[8,80,128]{2,1,0:T(8,128)(2,1)S(1)}, bf16[8,80,128]{2,1,0:T(8,128)(2,1)}, u32[]{:S(2)}) copy-start(bf16[8,80,128]{2,1,0:T(8,128)(2,1)} %copy-done.24) | copy-start | bytes 491524
  215.2 14.3 %copy-start.27 = (bf16[8,80,128]{2,1,0:T(8,128)(2,1)S(1)}, bf16[8,80,128]{2,1,0:T(8,128)(2,1)}, u32[]{:S(2)}) copy-start(bf16[8,80,128]{2,1,0:T(8,128)(2,1)} %copy-done.26) | copy-start | bytes 491524
  228.1 14.6 %collective-permute-start.24 = (bf16[16,160,128]{2,1,0:T(8,128)(2,1)S(1)}, bf16[16,160,128]{2,1,0:T(8,128)(2,1)S(1)}, u32[]{:S(2)}, u32[]{:S(2)}) collective-permute-start(bf16[16,160,128]{2,1,0:T(8,128)(2,1)S(1)} %get-tuple-element.208), channel_id=1, source_target_pairs={{2,0},{3,1},{10,8},{11,9},{18,16},{19,17},{26,24},{27,25}} | collective-permute-start | bytes 1966088 | tf_op jit(solution)/shard_map/ppermute | solution.py:409
  229.4 5.9 %collective-permute-start.30 = (bf16[8,80,128]{2,1,0:T(8,128)(2,1)S(1)}, bf16[8,80,128]{2,1,0:T(8,128)(2,1)S(1)}, u32[]{:S(2)}, u32[]{:S(2)}) collective-permute-start(bf16[8,80,128]{2,1,0:T(8,128)(2,1)S(1)} %copy-done.25), channel_id=1, source_target_pairs={{0,1},{1,0},{2,3},{3,2},{4,5},{5,4},{6,7},{7,6},{8,9},{9,8},{10,11... | collective-permute-start | bytes 491528 | tf_op jit(solution)/shard_map/ppermute | solution.py:677
  229.5 5.9 %collective-permute-start.29 = (bf16[8,80,128]{2,1,0:T(8,128)(2,1)S(1)}, bf16[8,80,128]{2,1,0:T(8,128)(2,1)S(1)}, u32[]{:S(2)}, u32[]{:S(2)}) collective-permute-start(bf16[8,80,128]{2,1,0:T(8,128)(2,1)S(1)} %copy-done.27), channel_id=1, source_target_pairs={{0,1},{1,0},{2,3},{3,2},{4,5},{5,4},{6,7},{7,6},{8,9},{9,8},{10,11... | collective-permute-start | bytes 491528 | tf_op jit(solution)/shard_map/ppermute | solution.py:694
  230.0 7.4 %collective-permute-start.28 = (bf16[16,80,128]{2,1,0:T(8,128)(2,1)S(1)}, bf16[16,80,128]{2,1,0:T(8,128)(2,1)S(1)}, u32[]{:S(2)}, u32[]{:S(2)}) collective-permute-start(bf16[16,80,128]{2,1,0:T(8,128)(2,1)S(1)} %get-tuple-element.214), channel_id=1, source_target_pairs={{0,1},{1,0},{2,3},{3,2},{4,5},{5,4},{6,7},{7,6},{8,9},{9,8},{10,11... | collective-permute-start | bytes 983048 | tf_op jit(solution)/shard_map/ppermute | solution.py:677
  230.0 7.3 %collective-permute-start.27 = (bf16[16,80,128]{2,1,0:T(8,128)(2,1)S(1)}, bf16[16,80,128]{2,1,0:T(8,128)(2,1)S(1)}, u32[]{:S(2)}, u32[]{:S(2)}) collective-permute-start(bf16[16,80,128]{2,1,0:T(8,128)(2,1)S(1)} %get-tuple-element.213), channel_id=1, source_target_pairs={{0,1},{1,0},{2,3},{3,2},{4,5},{5,4},{6,7},{7,6},{8,9},{9,8},{10,11... | collective-permute-start | bytes 983048 | tf_op jit(solution)/shard_map/ppermute | solution.py:694
  230.5 5.3 %copy-start.1 = (bf16[40,160,128]{2,1,0:T(8,128)(2,1)S(1)}, bf16[40,160,128]{2,1,0:T(8,128)(2,1)}, u32[]{:S(2)}) copy-start(bf16[40,160,128]{2,1,0:T(8,128)(2,1)} %copy-done) | copy-start | bytes 4915204
  230.5 5.3 %copy-start.23 = (bf16[2,8,80,128]{3,2,1,0:T(8,128)(2,1)S(1)}, bf16[2,8,80,128]{3,2,1,0:T(8,128)(2,1)}, u32[]{:S(2)}) copy-start(bf16[2,8,80,128]{3,2,1,0:T(8,128)(2,1)} %copy-done.22) | copy-start | bytes 983044
  235.3 7.4 %collective-permute-start.26 = (bf16[16,80,128]{2,1,0:T(8,128)(2,1)S(1)}, bf16[16,80,128]{2,1,0:T(8,128)(2,1)S(1)}, u32[]{:S(2)}, u32[]{:S(2)}) collective-permute-start(bf16[16,80,128]{2,1,0:T(8,128)(2,1)S(1)} %get-tuple-element.211), channel_id=1, source_target_pairs={{0,1},{1,0},{2,3},{3,2},{4,5},{5,4},{6,7},{7,6},{8,9},{9,8},{10,11... | collective-permute-start | bytes 983048 | tf_op jit(solution)/shard_map/ppermute | solution.py:677
  235.4 7.3 %collective-permute-start.25 = (bf16[16,80,128]{2,1,0:T(8,128)(2,1)S(1)}, bf16[16,80,128]{2,1,0:T(8,128)(2,1)S(1)}, u32[]{:S(2)}, u32[]{:S(2)}) collective-permute-start(bf16[16,80,128]{2,1,0:T(8,128)(2,1)S(1)} %get-tuple-element.210), channel_id=1, source_target_pairs={{0,1},{1,0},{2,3},{3,2},{4,5},{5,4},{6,7},{7,6},{8,9},{9,8},{10,11... | collective-permute-start | bytes 983048 | tf_op jit(solution)/shard_map/ppermute | solution.py:694
  235.8 1.5 copy-start.3
  (13 other events, 14.0 us)

commit v4 on v3

--- a/solution.py
+++ b/solution.py
@@ -447,7 +447,7 @@
 def given_parts(sizes):
     pairs = sum(sizes)
     if len(sizes) == 3 and pairs % 40 == 0:
-        return laid_out([pairs // 5, pairs // 5, 2 * pairs // 5, pairs // 5])
+        return laid_out([pairs // 5, pairs // 5, 3 * pairs // 10, 3 * pairs // 10])
     return laid_out([pairs] + [0] * len(sizes))
 
 
@@ -532,9 +532,8 @@
 
     lines = 4 * fields
 
-    def high_slots(i, given, ends, pieces):
+    def high_slots(i, block, given, ends, pieces):
         s, n = chunks[i]
-        block = block_pairs(s, n)
         shape = jax.ShapeDtypeStruct((n, degrees, columns), jnp.bfloat16)
         result = pl.BlockSpec((block, degrees, columns), lambda j, *_: (j, 0, 0))
         shape2 = jax.ShapeDtypeStruct((2, n, degrees, columns), jnp.bfloat16)
@@ -584,7 +583,7 @@
         everyone = lax.all_gather(both, "lev", axis=2, axis_index_groups=sides, tiled=True)
         order = column_order(jnp.arange(chips, dtype=jnp.int32), fields)
         given = Piece(jnp.zeros((pairs, 2 * degrees, half), jnp.bfloat16))
-        high, sent, _, _ = high_slots(0, [given], [1], [Piece(everyone, 0, 1)])
+        high, sent, _, _ = high_slots(0, pairs, [given], [1], [Piece(everyone, 0, 1)])
         got_high = Piece(lax.ppermute(sent, "lev", swap))
         high = Piece(high, 0, 0)
         low, sent, _ = low_slots(0, Piece(everyone, 0, 0), [], [])
@@ -602,6 +601,7 @@
     first_in, first_cross, second_cross = [[None] * count for _ in range(3)]
     first_out, second_out, third_out = [[None] * count for _ in range(3)]
     in_mark, out_mark, out2_mark, out3_mark = [[None] * count for _ in range(4)]
+    finish_mark = [None] * count
     inward, centre, outward = Links(), Links(), Links()
     last = count - 1
 
@@ -641,11 +641,11 @@
         first_in[i], second_cross[i], _ = centre.send(first_in[i], CENTRE, after, meanwhile)
 
     def send_out():
-        low[0], found, out_mark[0] = outward.send(low[0], OUTWARD)
+        low[0], found, out_mark[0] = outward.send(low[0], OUTWARD, (), (halves_mark[1],))
         first_out[0] = Piece(found)
 
     def send_out2(i):
-        meanwhile = (at(table_mark, i + 1),) if i == last else ()
+        meanwhile = ()
         blocks = [first_cross[i][0]]
         if i < last:
             blocks.append(low[i + 1])
@@ -667,23 +667,24 @@
     def do_high(i):
         pieces = [Piece(passed[i], 0, 1) for passed in (both, first_in, first_cross, second_cross)]
         s, n = chunks[i]
-        block = block_pairs(s, n)
+        block = math.gcd(block_pairs(s, n), *[start for start, _ in parts if s < start < s + n])
         given, ends = [], []
         for (start, size), array in zip(parts, table):
             if max(s, start) < min(s + n, start + size):
                 given.append(Piece(array, s - start))
                 ends.append((start + size - s) // block)
-        high[i], sent, sent_back, high_mark[i] = high_slots(i, given, ends, pieces)
+        high[i], sent, sent_back, high_mark[i] = high_slots(i, block, given, ends, pieces)
         got_high[i] = lax.ppermute(sent, "lev", swap)
         got_back = lax.ppermute(sent_back, "lev", swap)
         returned[i] = jnp.concatenate([high[i][1], got_back]).reshape(second_cross[i].shape[1:])
 
     def send_out3(i):
-        _, found, out3_mark[i] = outward.send(second_cross[i][0], OUTWARD)
+        meanwhile = (at(table_mark, i + 1),) if i == last else ()
+        _, found, out3_mark[i] = outward.send(second_cross[i][0], OUTWARD, (), meanwhile)
         third_out[i] = Piece(found)
 
     def send_back(i):
-        _, found, _ = outward.send(returned[i], RETURN)
+        _, found, _ = outward.send(returned[i], RETURN, (), (at(finish_mark, i - 1), at(low_mark, i)))
         came_back(i, found, 0)
 
     def do_low(i):
@@ -694,7 +695,7 @@
         got_low[i] = lax.ppermute(sent, "lev", swap)
 
     def do_finish(i):
-        finish(
+        finish_mark[i] = finish(
             i,
             [Piece(found_low[i]), Piece(high[i], 0, 0), back[i][0]],
             [Piece(got_low[i]), Piece(got_high[i]), back[i][1]],
@@ -709,10 +710,9 @@
     send_in(0)
     do_give(1)
     send_cross(0)
+    prepare(1)
     send_out()
     for i in range(count):
-        if i == 0 and count > 1:
-            prepare(1)
         send_table(i + 1)
         if i < last:
             send_in(i + 1)
@@ -728,8 +728,8 @@
         if i < last:
             send_cross(i + 1)
         send_out3(i)
+    do_low(last)
     send_back(last)
-    do_low(last)
     do_finish(last)
     return state["out"].reshape(slots, degrees, columns)
 

time: 246 us -> 242 us (0.984)
  waiting for transfers between devices: 86.7 us -> 76.4 us
  Pallas kernels: 75.9 us -> 79.6 us
    ppermute x21, waiting for transfers between devices: 85.1 us -> 73.9 us  [send(): return lax.ppermute(block, 'lev', on_cores(pairs))]
    pallas_call x13, Pallas kernels: 43.5 us -> 47.6 us  [over_pairs(): pl.pallas_call(kernel, grid_spec=pltpu.PrefetchScalarGridSpec(num_scalar_...]
    unnamed x56 -> x58, local copies, waits for them, and re-layouts: 11 us -> 11.7 us
  transfers between devices with their start and end apart: 33 -> 33, of which waited for: 12 -> 13; matrix products, arithmetic and copies ran while one was open for 4% -> 4% of each run, Pallas kernels for 30% -> 32%
where the time goes in v4:
time: 242 us; the launch traced here: 241 us
  Pallas kernels  79.6 us (33%)
  waiting for transfers between devices  76.4 us (32%)
  starting transfers between devices  63.1 us (26%)
  local copies, waits for them, and re-layouts  16.4 us (7%)
  other arithmetic  4.63 us (2%)
    ppermute x21, waiting for transfers between devices, send(): return lax.ppermute(block, 'lev', on_cores(pairs))  73.9 us
    ppermute x21, starting transfers between devices, send(): return lax.ppermute(block, 'lev', on_cores(pairs))  51.8 us
    pallas_call x13, Pallas kernels, over_pairs(): pl.pallas_call(kernel, grid_spec=pltpu.PrefetchScalarGridSpec(num_scalar_...  47.6 us
    pallas_call x3, Pallas kernels, halves(): pl.pallas_call(functools.partial(halves_kernel, fields, wide), grid=(1,),...  14.2 us
    unnamed x58, local copies, waits for them, and re-layouts  11.7 us
    pallas_call x1, Pallas kernels, zonal(): pl.pallas_call(functools.partial(zonal_kernel, start, sizes), grid=(colum...  9.99 us
    all_to_all x2, starting transfers between devices, exchange(): lax.all_to_all(found, ('lat', 'lev'), split_axis=0, concat_axis=0, axis_i...  9.04 us
    pallas_call x1, Pallas kernels, fold_and_zonal(): pl.pallas_call(functools.partial(fold_kernel, start, sizes, group), grid=...  7.69 us
  transfers between devices with their start and end apart: 33, of which 13 were waited for; matrix products, arithmetic and copies ran while one was open for 4% of the time, Pallas kernels for 32%

profile of v4, /device:TPU:0, one launch (start us, length us, event | category | flops | bytes accessed | tf_op | source)
XLA Modules:
  0.0 240.9 jit_solution(14081816304529875608)
XLA Ops:
  2.6 1.4 cosine_multiply_fusion
  4.3 7.7 %fold_and_zonal.1 = (bf16[8,32,1280]{2,1,0:T(8,128)(2,1)}, bf16[1280,640]{1,0:T(8,128)(2,1)S(1)}, bf16[1280,640]{1,0:T(8,128)(2,1)S(1)}, bf16[1280,640]{1,0:T(8,...) custom-call(f32[2,2,320,128]{3,2,1,0:T(8,128)S(1)} %pad_maximum_fusion.3.base_ref, ...), custom_call_target="tpu_custom_call" | custom-call | flops 1000 | bytes 1000 | tf_op jit(solution)/shard_map/fold_and_zonal/pallas_call | solution.py:96
  14.3 4.8 %all-to-all-start.1 = ((bf16[8,32,1280]{2,1,0:T(8,128)(2,1)}), bf16[8,32,1280]{2,1,0:T(8,128)(2,1)S(1)}, u32[]{:S(2)}, u32[]{:S(2)}) async-start(bf16[8,32,1280]{2,1,0:T(8,128)(2,1)} %get-tuple-element.122), calls=%async_computation.1 | async-start | bytes 1310720 | tf_op jit(solution)/shard_map/all_to_all | solution.py:504
  20.0 3.4 %give.4 = (bf16[8,400,128]{2,1,0:T(8,128)(2,1)}, f32[8,128]{1,0:T(8,128)S(1)}) custom-call(s32[1]{0:T(128)} %bitcast.info_ref, s32[80]{0:T(128)S(1)} %dynamic-slice_bitcast_fusion.waves_ref, bf16[160,80,320]{2,1,0:T(8,128)(2,1)} %own_ref.19, bf16[160,80,320]{2,1,0:T(8,128)(2,1)} %collective-permute-done.other_ref, f32[8,128]{1,0:T(8,128)S(1)} %get-tuple-element.119.refs_0_), custom_call_target="tpu_custom_call" | custom-call | flops 1000 | bytes 1000 | tf_op jit(solution)/shard_map/give/pallas_call | solution.py:316
  23.4 3.5 %collective-permute-start.1 = (bf16[8,400,128]{2,1,0:T(8,128)(2,1)}, bf16[8,400,128]{2,1,0:T(8,128)(2,1)S(1)}, u32[]{:S(2)}, u32[]{:S(2)}) collective-permute-start(bf16[8,400,128]{2,1,0:T(8,128)(2,1)} %get-tuple-element.132), channel_id=1, source_target_pairs={{0,2},{1,3},{8,10},{9,11},{16,18},{17,19},{24,26},{25,27}} | collective-permute-start | bytes 2457608 | tf_op jit(solution)/shard_map/ppermute | solution.py:409
  26.9 10.0 %zonal.1 = (bf16[8,128,1280]{2,1,0:T(8,128)(2,1)}, f32[8,128]{1,0:T(8,128)S(1)}) custom-call(f32[2,2,320,128]{3,2,1,0:T(8,128)S(1)} %pad_maximum_fusion.3.base_ref, f32[2,2,320,5]{3,2,1,0:T(8,128)S(1)} %copy.61.step_ref, f32[320,1]{1,0:T(8,128)S(1)} %fusion.7.first_ref, bf16[1280,640]{1,0:T(8,128)(2,1)S(1)} %copy-done.22, bf16[1280,640]{1,0:T(8,128)(2,1)S(1)} %copy-done.24, ...), custom_call_target="tpu_custom_call" | custom-call | flops 1000 | bytes 1000 | tf_op jit(solution)/shard_map/zonal/pallas_call | solution.py:137
  37.8 4.2 %all-to-all-start = ((bf16[8,128,1280]{2,1,0:T(8,128)(2,1)}), bf16[8,128,1280]{2,1,0:T(8,128)(2,1)S(1)}, u32[]{:S(2)}, u32[]{:S(2)}) async-start(bf16[8,128,1280]{2,1,0:T(8,128)(2,1)} %get-tuple-element.121), calls=%async_computation | async-start | bytes 5242880 | tf_op jit(solution)/shard_map/all_to_all | solution.py:504
  43.1 3.0 %halves.3 = (bf16[2,8,160,128]{3,2,1,0:T(8,128)(2,1)S(1)}, bf16[2,8,160,128]{3,2,1,0:T(8,128)(2,1)S(1)}, bf16[8,160,128]{2,1,0:T(8,128)(2,1)}, f32[8,128]{1,0:T(8,128)S(1)}) custom-call(bf16[8,32,1280]{2,1,0:T(8,128)(2,1)S(1)} %copy-done.20, f32[8,128]{1,0:T(8,128)S(1)} %get-tuple-element.123.refs_0_), custom_call_target="tpu_custom_call" | custom-call | flops 1000 | bytes 1000 | tf_op jit(solution)/shard_map/halves/pallas_call | solution.py:183
  47.0 3.5 %collective-permute-start.2 = (bf16[2,8,160,128]{3,2,1,0:T(8,128)(2,1)S(1)}, bf16[2,8,160,128]{3,2,1,0:T(8,128)(2,1)S(1)}, u32[]{:S(2)}, u32[]{:S(2)}) collective-permute-start(bf16[2,8,160,128]{3,2,1,0:T(8,128)(2,1)S(1)} %get-tuple-element.134), channel_id=1, source_target_pairs={{0,2},{1,3},{6,4},{7,5},{8,10},{9,11},{14,12},{15,13},{16,18},{17,... | collective-permute-start | bytes 1966088 | tf_op jit(solution)/shard_map/ppermute | solution.py:409
  51.3 3.1 %give.5 = (bf16[8,400,128]{2,1,0:T(8,128)(2,1)}, f32[8,128]{1,0:T(8,128)S(1)}) custom-call(s32[1]{0:T(128)} %bitcast.info_ref, s32[80]{0:T(128)S(1)} %dynamic-slice_bitcast_fusion.waves_ref, bf16[160,80,320]{2,1,0:T(8,128)(2,1)} %own_ref.19, bf16[160,80,320]{2,1,0:T(8,128)(2,1)} %collective-permute-done.other_ref, f32[8,128]{1,0:T(8,128)S(1)} %get-tuple-element.124.refs_0_), custom_call_target="tpu_custom_call" | custom-call | flops 1000 | bytes 1000 | tf_op jit(solution)/shard_map/give/pallas_call | solution.py:316
  54.4 10.0 %collective-permute-done.2.refs_0_ = bf16[2,8,160,128]{3,2,1,0:T(8,128)(2,1)S(1)} collective-permute-done((bf16[2,8,160,128]{3,2,1,0:T(8,128)(2,1)S(1)}, bf16[2,8,160,128]{3,2,1,0:T(8,128)(2,1)S(1)}, u32[]{:S(2)}, u32[]{:S(2)}) %collective-permute-start.2) | collective-permute-done | bytes 655392 | tf_op jit(solution)/shard_map/ppermute | solution.py:409
  64.4 5.3 %collective-permute-start.3 = (bf16[8,400,128]{2,1,0:T(8,128)(2,1)}, bf16[8,400,128]{2,1,0:T(8,128)(2,1)}, u32[]{:S(2)}, u32[]{:S(2)}) collective-permute-start(bf16[8,400,128]{2,1,0:T(8,128)(2,1)} %get-tuple-element.136), channel_id=1, source_target_pairs={{0,2},{1,3},{8,10},{9,11},{16,18},{17,19},{24,26},{25,27}} | collective-permute-start | bytes 2457608 | tf_op jit(solution)/shard_map/ppermute | solution.py:409
  70.5 1.5 collective-permute-start.6
  72.0 1.3 collective-permute-start.8
  74.3 5.9 %halves.4 = (bf16[2,16,160,128]{3,2,1,0:T(8,128)(2,1)}, bf16[2,16,160,128]{3,2,1,0:T(8,128)(2,1)}, bf16[16,160,128]{2,1,0:T(8,128)(2,1)S(1)}, f32[8,128]{1,0:T(8,128)S(1)}) custom-call(bf16[8,128,1280]{2,1,0:T(8,128)(2,1)S(1)} %all-to-all-done.in_ref, f32[8,128]{1,0:T(8,128)S(1)} %get-tuple-element.125.refs_0_.refs_1_), custom_call_target="tpu_custom_call" | custom-call | flops 1000 | bytes 1000 | tf_op jit(solution)/shard_map/halves/pallas_call | solution.py:183
  80.1 5.5 %collective-permute-done.3.refs_0_ = bf16[8,400,128]{2,1,0:T(8,128)(2,1)} collective-permute-done((bf16[8,400,128]{2,1,0:T(8,128)(2,1)}, bf16[8,400,128]{2,1,0:T(8,128)(2,1)}, u32[]{:S(2)}, u32[]{:S(2)}) %collective-permute-start.3) | collective-permute-done | bytes 819232 | tf_op jit(solution)/shard_map/ppermute | solution.py:409
  85.6 5.6 %collective-permute-start.4 = (bf16[2,16,160,128]{3,2,1,0:T(8,128)(2,1)}, bf16[2,16,160,128]{3,2,1,0:T(8,128)(2,1)}, u32[]{:S(2)}, u32[]{:S(2)}) collective-permute-start(bf16[2,16,160,128]{3,2,1,0:T(8,128)(2,1)} %get-tuple-element.138), channel_id=1, source_target_pairs={{0,2},{1,3},{6,4},{7,5},{8,10},{9,11},{14,12},{15,13},{16,18},{17,... | collective-permute-start | bytes 3932168 | tf_op jit(solution)/shard_map/ppermute | solution.py:409
  91.2 1.7 collective-permute-start.7
  94.0 1.5 collective-permute-start.9
  99.7 3.2 %high_slots.3 = (bf16[2,8,80,128]{3,2,1,0:T(8,128)(2,1)S(1)}, bf16[8,80,128]{2,1,0:T(8,128)(2,1)S(1)}, bf16[8,80,128]{2,1,0:T(8,128)(2,1)S(1)}, f32[8,128]{1,0:T(8,128)S(1)}) custom-call(s32[1]{0:T(128)} %bitcast.info_ref, s32[80]{0:T(128)S(1)} %dynamic-slice_bitcast_fusion.waves_ref, bf16[128,128]{1,0:T(8,128)(2,1)S(1)} %fusion.10.order_ref, ...), custom_call_target="tpu_custom_call" | custom-call | flops 1000 | bytes 1000 | tf_op jit(solution)/shard_map/high_slots/pallas_call | solution.py:316
  103.0 4.3 %give.6 = (bf16[12,400,128]{2,1,0:T(8,128)(2,1)}, f32[8,128]{1,0:T(8,128)S(1)}) custom-call(s32[1]{0:T(128)} %bitcast.info_ref, s32[80]{0:T(128)S(1)} %dynamic-slice_bitcast_fusion.waves_ref, bf16[160,80,320]{2,1,0:T(8,128)(2,1)} %own_ref.19, bf16[160,80,320]{2,1,0:T(8,128)(2,1)} %collective-permute-done.other_ref, ...), custom_call_target="tpu_custom_call" | custom-call | flops 1000 | bytes 1000 | tf_op jit(solution)/shard_map/give/pallas_call | solution.py:316
  107.3 5.4 %halves.5 = (bf16[2,16,160,128]{3,2,1,0:T(8,128)(2,1)S(1)}, bf16[2,16,160,128]{3,2,1,0:T(8,128)(2,1)}, bf16[16,160,128]{2,1,0:T(8,128)(2,1)S(1)}, f32[8,128]{1,0:T(8,128)S(1)}) custom-call(bf16[8,128,1280]{2,1,0:T(8,128)(2,1)S(1)} %all-to-all-done.in_ref, f32[8,128]{1,0:T(8,128)S(1)} %get-tuple-element.127.refs_0_.refs_2_), custom_call_target="tpu_custom_call" | custom-call | flops 1000 | bytes 1000 | tf_op jit(solution)/shard_map/halves/pallas_call | solution.py:183
  113.7 3.8 %collective-permute-done.9.refs_0_ = bf16[24,160,128]{2,1,0:T(8,128)(2,1)} collective-permute-done((bf16[24,160,128]{2,1,0:T(8,128)(2,1)}, bf16[24,160,128]{2,1,0:T(8,128)(2,1)}, u32[]{:S(2)}, u32[]{:S(2)}) %collective-permute-start.9) | collective-permute-done | bytes 983072 | tf_op jit(solution)/shard_map/ppermute | solution.py:409
  117.5 1.3 collective-permute-start.11
  119.6 5.8 %collective-permute-start.12 = (bf16[12,400,128]{2,1,0:T(8,128)(2,1)}, bf16[12,400,128]{2,1,0:T(8,128)(2,1)S(1)}, u32[]{:S(2)}, u32[]{:S(2)}) collective-permute-start(bf16[12,400,128]{2,1,0:T(8,128)(2,1)} %get-tuple-element.170), channel_id=1, source_target_pairs={{0,2},{1,3},{8,10},{9,11},{16,18},{17,19},{24,26},{25,27}} | collective-permute-start | bytes 3686408 | tf_op jit(solution)/shard_map/ppermute | solution.py:409
  127.0 1.4 collective-permute-start.16
  128.5 3.8 %low_slots.3 = (bf16[8,80,128]{2,1,0:T(8,128)(2,1)S(1)}, bf16[8,80,128]{2,1,0:T(8,128)(2,1)}, f32[8,128]{1,0:T(8,128)S(1)}) custom-call(s32[1]{0:T(128)} %bitcast.info_ref, s32[80]{0:T(128)S(1)} %dynamic-slice_bitcast_fusion.waves_ref, bf16[128,128]{1,0:T(8,128)(2,1)S(1)} %fusion.10.order_ref, bf16[160,80,320]{2,1,0:T(8,128)(2,1)} %own_ref.19, ...), custom_call_target="tpu_custom_call" | custom-call | flops 1000 | bytes 1000 | tf_op jit(solution)/shard_map/low_slots/pallas_call | solution.py:316
  132.3 17.4 %collective-permute-done.12.refs_0_ = bf16[12,400,128]{2,1,0:T(8,128)(2,1)S(1)} collective-permute-done((bf16[12,400,128]{2,1,0:T(8,128)(2,1)}, bf16[12,400,128]{2,1,0:T(8,128)(2,1)S(1)}, u32[]{:S(2)}, u32[]{:S(2)}) %collective-permute-start.12) | collective-permute-done | bytes 1228832 | tf_op jit(solution)/shard_map/ppermute | solution.py:409
  149.7 4.4 %collective-permute-start.13 = (bf16[2,16,160,128]{3,2,1,0:T(8,128)(2,1)}, bf16[2,16,160,128]{3,2,1,0:T(8,128)(2,1)S(1)}, u32[]{:S(2)}, u32[]{:S(2)}) collective-permute-start(bf16[2,16,160,128]{3,2,1,0:T(8,128)(2,1)} %get-tuple-element.172), channel_id=1, source_target_pairs={{0,2},{1,3},{6,4},{7,5},{8,10},{9,11},{14,12},{15,13},{16,18},{17,... | collective-permute-start | bytes 3932168 | tf_op jit(solution)/shard_map/ppermute | solution.py:409
  155.2 8.7 %collective-permute-done.16.refs_0_ = bf16[40,160,128]{2,1,0:T(8,128)(2,1)S(1)} collective-permute-done((bf16[40,160,128]{2,1,0:T(8,128)(2,1)S(1)}, bf16[40,160,128]{2,1,0:T(8,128)(2,1)S(1)}, u32[]{:S(2)}, u32[]{:S(2)}) %collective-permute-start.16) | collective-permute-done | bytes 1638432 | tf_op jit(solution)/shard_map/ppermute | solution.py:409
  163.8 1.3 collective-permute-start.18
  165.1 5.1 %high_slots.4 = (bf16[2,16,80,128]{3,2,1,0:T(8,128)(2,1)S(1)}, bf16[16,80,128]{2,1,0:T(8,128)(2,1)S(1)}, bf16[16,80,128]{2,1,0:T(8,128)(2,1)S(1)}, f32[8,128]{1,0:T(8,128)S(1)}) custom-call(s32[1]{0:T(128)} %bitcast.info_ref, s32[80]{0:T(128)S(1)} %dynamic-slice_bitcast_fusion.waves_ref, bf16[128,128]{1,0:T(8,128)(2,1)S(1)} %fusion.10.order_ref, ...), custom_call_target="tpu_custom_call" | custom-call | flops 1000 | bytes 1000 | tf_op jit(solution)/shard_map/high_slots/pallas_call | solution.py:316
  170.3 4.3 %give.7 = (bf16[12,400,128]{2,1,0:T(8,128)(2,1)}, f32[8,128]{1,0:T(8,128)S(1)}) custom-call(s32[1]{0:T(128)} %bitcast.info_ref, s32[80]{0:T(128)S(1)} %dynamic-slice_bitcast_fusion.waves_ref, bf16[160,80,320]{2,1,0:T(8,128)(2,1)} %own_ref.19, bf16[160,80,320]{2,1,0:T(8,128)(2,1)} %collective-permute-done.other_ref, ...), custom_call_target="tpu_custom_call" | custom-call | flops 1000 | bytes 1000 | tf_op jit(solution)/shard_map/give/pallas_call | solution.py:316
  174.7 3.8 %collective-permute-done.18.refs_0_ = bf16[16,160,128]{2,1,0:T(8,128)(2,1)S(1)} collective-permute-done((bf16[16,160,128]{2,1,0:T(8,128)(2,1)S(1)}, bf16[16,160,128]{2,1,0:T(8,128)(2,1)S(1)}, u32[]{:S(2)}, u32[]{:S(2)}) %collective-permute-start.18) | collective-permute-done | bytes 655392 | tf_op jit(solution)/shard_map/ppermute | solution.py:409
  180.2 1.3 collective-permute-start.20
  182.2 7.0 %collective-permute-start.22 = (bf16[12,400,128]{2,1,0:T(8,128)(2,1)}, bf16[12,400,128]{2,1,0:T(8,128)(2,1)S(1)}, u32[]{:S(2)}, u32[]{:S(2)}) collective-permute-start(bf16[12,400,128]{2,1,0:T(8,128)(2,1)} %get-tuple-element.202), channel_id=1, source_target_pairs={{0,2},{1,3},{8,10},{9,11},{16,18},{17,19},{24,26},{25,27}} | collective-permute-start | bytes 3686408 | tf_op jit(solution)/shard_map/ppermute | solution.py:409
  189.3 4.7 %low_slots.4 = (bf16[16,80,128]{2,1,0:T(8,128)(2,1)S(1)}, bf16[16,80,128]{2,1,0:T(8,128)(2,1)S(1)}, f32[8,128]{1,0:T(8,128)S(1)}) custom-call(s32[1]{0:T(128)} %bitcast.info_ref, s32[80]{0:T(128)S(1)} %dynamic-slice_bitcast_fusion.waves_ref, bf16[128,128]{1,0:T(8,128)(2,1)S(1)} %fusion.10.order_ref, bf16[160,80,320]{2,1,0:T(8,128)(2,1)} %own_ref.19, ...), custom_call_target="tpu_custom_call" | custom-call | flops 1000 | bytes 1000 | tf_op jit(solution)/shard_map/low_slots/pallas_call | solution.py:316
  194.0 15.5 %collective-permute-done.20.refs_0_ = bf16[32,160,128]{2,1,0:T(8,128)(2,1)S(1)} collective-permute-done((bf16[32,160,128]{2,1,0:T(8,128)(2,1)S(1)}, bf16[32,160,128]{2,1,0:T(8,128)(2,1)S(1)}, u32[]{:S(2)}, u32[]{:S(2)}) %collective-permute-start.20) | collective-permute-done | bytes 1310752 | tf_op jit(solution)/shard_map/ppermute | solution.py:409
  210.6 1.3 collective-permute-start.21
  212.0 6.2 %high_slots.5 = (bf16[2,16,80,128]{3,2,1,0:T(8,128)(2,1)S(1)}, bf16[16,80,128]{2,1,0:T(8,128)(2,1)S(1)}, bf16[16,80,128]{2,1,0:T(8,128)(2,1)S(1)}, f32[8,128]{1,0:T(8,128)}) custom-call(s32[1]{0:T(128)} %bitcast.info_ref, s32[80]{0:T(128)S(1)} %dynamic-slice_bitcast_fusion.waves_ref, bf16[128,128]{1,0:T(8,128)(2,1)S(1)} %fusion.10.order_ref, ...), custom_call_target="tpu_custom_call" | custom-call | flops 1000 | bytes 1000 | tf_op jit(solution)/shard_map/high_slots/pallas_call | solution.py:316
  218.2 1.6 collective-permute-done.23
  219.9 4.5 %collective-permute-done.21.refs_0_ = bf16[16,160,128]{2,1,0:T(8,128)(2,1)S(1)} collective-permute-done((bf16[16,160,128]{2,1,0:T(8,128)(2,1)S(1)}, bf16[16,160,128]{2,1,0:T(8,128)(2,1)S(1)}, u32[]{:S(2)}, u32[]{:S(2)}) %collective-permute-start.21) | collective-permute-done | bytes 655392 | tf_op jit(solution)/shard_map/ppermute | solution.py:409
  224.4 1.3 collective-permute-start.24
  226.8 4.2 %low_slots.5 = (bf16[16,80,128]{2,1,0:T(8,128)(2,1)S(1)}, bf16[16,80,128]{2,1,0:T(8,128)(2,1)S(1)}, f32[8,128]{1,0:T(8,128)S(1)}) custom-call(s32[1]{0:T(128)} %bitcast.info_ref, s32[80]{0:T(128)S(1)} %dynamic-slice_bitcast_fusion.waves_ref, bf16[128,128]{1,0:T(8,128)(2,1)S(1)} %fusion.10.order_ref, bf16[160,80,320]{2,1,0:T(8,128)(2,1)} %own_ref.19, ...), custom_call_target="tpu_custom_call" | custom-call | flops 1000 | bytes 1000 | tf_op jit(solution)/shard_map/low_slots/pallas_call | solution.py:316
  231.6 1.5 finish.3
  233.1 1.9 finish.4
  235.1 3.9 %collective-permute-done.24.refs_0_ = bf16[16,160,128]{2,1,0:T(8,128)(2,1)S(1)} collective-permute-done((bf16[16,160,128]{2,1,0:T(8,128)(2,1)S(1)}, bf16[16,160,128]{2,1,0:T(8,128)(2,1)S(1)}, u32[]{:S(2)}, u32[]{:S(2)}) %collective-permute-start.24) | collective-permute-done | bytes 655392 | tf_op jit(solution)/shard_map/ppermute | solution.py:409
  239.0 1.9 finish.5
  (173 shorter events, 26.6 us)
Async XLA Ops:
  0.0 20.0 %collective-permute-start = (bf16[160,80,320]{2,1,0:T(8,128)(2,1)}, bf16[160,80,320]{2,1,0:T(8,128)(2,1)}, u32[]{:S(2)}, u32[]{:S(2)}) collective-permute-start(bf16[160,80,320]{2,1,0:T(8,128)(2,1)} %own_ref.19), channel_id=1, source_target_pairs={{0,1},{1,0},{2,3},{3,2},{4,5},{5,4},{6,7},{7,6},{8,9},{9,8},{10,11... | collective-permute-start | bytes 24576008 | tf_op jit(solution)/shard_map/ppermute | solution.py:499
  14.3 22.6 %all-to-all-start.1 = ((bf16[8,32,1280]{2,1,0:T(8,128)(2,1)}), bf16[8,32,1280]{2,1,0:T(8,128)(2,1)S(1)}, u32[]{:S(2)}, u32[]{:S(2)}) async-start(bf16[8,32,1280]{2,1,0:T(8,128)(2,1)} %get-tuple-element.122), calls=%async_computation.1 | async-start | bytes 1310720 | tf_op jit(solution)/shard_map/all_to_all | solution.py:504
  20.0 6.9 %copy-start.22 = (bf16[1280,640]{1,0:T(8,128)(2,1)S(1)}, bf16[1280,640]{1,0:T(8,128)(2,1)}, u32[]{:S(2)}) copy-start(bf16[1280,640]{1,0:T(8,128)(2,1)} %copy-done.21) | copy-start | bytes 4915204
  20.0 6.9 %copy-start.24 = (bf16[1280,640]{1,0:T(8,128)(2,1)S(1)}, bf16[1280,640]{1,0:T(8,128)(2,1)}, u32[]{:S(2)}) copy-start(bf16[1280,640]{1,0:T(8,128)(2,1)} %copy-done.23) | copy-start | bytes 4915204
  23.4 22.7 %collective-permute-start.1 = (bf16[8,400,128]{2,1,0:T(8,128)(2,1)}, bf16[8,400,128]{2,1,0:T(8,128)(2,1)S(1)}, u32[]{:S(2)}, u32[]{:S(2)}) collective-permute-start(bf16[8,400,128]{2,1,0:T(8,128)(2,1)} %get-tuple-element.132), channel_id=1, source_target_pairs={{0,2},{1,3},{8,10},{9,11},{16,18},{17,19},{24,26},{25,27}} | collective-permute-start | bytes 2457608 | tf_op jit(solution)/shard_map/ppermute | solution.py:409
  37.8 36.5 %all-to-all-start = ((bf16[8,128,1280]{2,1,0:T(8,128)(2,1)}), bf16[8,128,1280]{2,1,0:T(8,128)(2,1)S(1)}, u32[]{:S(2)}, u32[]{:S(2)}) async-start(bf16[8,128,1280]{2,1,0:T(8,128)(2,1)} %get-tuple-element.121), calls=%async_computation | async-start | bytes 5242880 | tf_op jit(solution)/shard_map/all_to_all | solution.py:504
  46.1 8.3 %copy-start.16 = (bf16[2,8,160,128]{3,2,1,0:T(8,128)(2,1)}, bf16[2,8,160,128]{3,2,1,0:T(8,128)(2,1)S(1)}, u32[]{:S(2)}) copy-start(bf16[2,8,160,128]{3,2,1,0:T(8,128)(2,1)S(1)} %get-tuple-element.142.refs_0_) | copy-start | bytes 1966084
  47.0 17.4 %collective-permute-start.2 = (bf16[2,8,160,128]{3,2,1,0:T(8,128)(2,1)S(1)}, bf16[2,8,160,128]{3,2,1,0:T(8,128)(2,1)S(1)}, u32[]{:S(2)}, u32[]{:S(2)}) collective-permute-start(bf16[2,8,160,128]{3,2,1,0:T(8,128)(2,1)S(1)} %get-tuple-element.134), channel_id=1, source_target_pairs={{0,2},{1,3},{6,4},{7,5},{8,10},{9,11},{14,12},{15,13},{16,18},{17,... | collective-permute-start | bytes 1966088 | tf_op jit(solution)/shard_map/ppermute | solution.py:409
  50.6 19.1 %collective-permute-start.5 = (bf16[2,8,160,128]{3,2,1,0:T(8,128)(2,1)S(1)}, bf16[2,8,160,128]{3,2,1,0:T(8,128)(2,1)S(1)}, u32[]{:S(2)}, u32[]{:S(2)}) collective-permute-start(bf16[2,8,160,128]{3,2,1,0:T(8,128)(2,1)S(1)} %get-tuple-element.142.refs_0_), channel_id=1, source_target_pairs={{2,4},{3,5},{4,2},{5,3},{10,12},{11,13},{12,10},{13,11},{18,20},{1... | collective-permute-start | bytes 1966088 | tf_op jit(solution)/shard_map/ppermute | solution.py:409
  64.4 21.2 %collective-permute-start.3 = (bf16[8,400,128]{2,1,0:T(8,128)(2,1)}, bf16[8,400,128]{2,1,0:T(8,128)(2,1)}, u32[]{:S(2)}, u32[]{:S(2)}) collective-permute-start(bf16[8,400,128]{2,1,0:T(8,128)(2,1)} %get-tuple-element.136), channel_id=1, source_target_pairs={{0,2},{1,3},{8,10},{9,11},{16,18},{17,19},{24,26},{25,27}} | collective-permute-start | bytes 2457608 | tf_op jit(solution)/shard_map/ppermute | solution.py:409
  70.5 20.7 %collective-permute-start.6 = (bf16[2,8,160,128]{3,2,1,0:T(8,128)(2,1)S(1)}, bf16[2,8,160,128]{3,2,1,0:T(8,128)(2,1)}, u32[]{:S(2)}, u32[]{:S(2)}) collective-permute-start(bf16[2,8,160,128]{3,2,1,0:T(8,128)(2,1)S(1)} %get-tuple-element.144.refs_1_), channel_id=1, source_target_pairs={{2,4},{3,5},{4,2},{5,3},{10,12},{11,13},{12,10},{13,11},{18,20},{1... | collective-permute-start | bytes 1966088 | tf_op jit(solution)/shard_map/ppermute | solution.py:409
  72.0 20.9 %collective-permute-start.8 = (bf16[8,160,128]{2,1,0:T(8,128)(2,1)}, bf16[8,160,128]{2,1,0:T(8,128)(2,1)}, u32[]{:S(2)}, u32[]{:S(2)}) collective-permute-start(bf16[8,160,128]{2,1,0:T(8,128)(2,1)} %get-tuple-element.154), channel_id=1, source_target_pairs={{2,0},{3,1},{4,6},{5,7},{10,8},{11,9},{12,14},{13,15},{18,16},{19,... | collective-permute-start | bytes 983048 | tf_op jit(solution)/shard_map/ppermute | solution.py:409
  85.6 7.3 %copy-start.11 = (bf16[2,8,160,128]{3,2,1,0:T(8,128)(2,1)S(1)}, bf16[2,8,160,128]{3,2,1,0:T(8,128)(2,1)}, u32[]{:S(2)}) copy-start(bf16[2,8,160,128]{3,2,1,0:T(8,128)(2,1)} %copy-done.10) | copy-start | bytes 1966084
  85.6 33.2 %collective-permute-start.4 = (bf16[2,16,160,128]{3,2,1,0:T(8,128)(2,1)}, bf16[2,16,160,128]{3,2,1,0:T(8,128)(2,1)}, u32[]{:S(2)}, u32[]{:S(2)}) collective-permute-start(bf16[2,16,160,128]{3,2,1,0:T(8,128)(2,1)} %get-tuple-element.138), channel_id=1, source_target_pairs={{0,2},{1,3},{6,4},{7,5},{8,10},{9,11},{14,12},{15,13},{16,18},{17,... | collective-permute-start | bytes 3932168 | tf_op jit(solution)/shard_map/ppermute | solution.py:409
  91.2 27.7 %collective-permute-start.7 = (bf16[2,16,160,128]{3,2,1,0:T(8,128)(2,1)}, bf16[2,16,160,128]{3,2,1,0:T(8,128)(2,1)}, u32[]{:S(2)}, u32[]{:S(2)}) collective-permute-start(bf16[2,16,160,128]{3,2,1,0:T(8,128)(2,1)} %get-tuple-element.146.refs_0_), channel_id=1, source_target_pairs={{2,4},{3,5},{4,2},{5,3},{10,12},{11,13},{12,10},{13,11},{18,20},{1... | collective-permute-start | bytes 3932168 | tf_op jit(solution)/shard_map/ppermute | solution.py:409
  94.0 23.5 %collective-permute-start.9 = (bf16[24,160,128]{2,1,0:T(8,128)(2,1)}, bf16[24,160,128]{2,1,0:T(8,128)(2,1)}, u32[]{:S(2)}, u32[]{:S(2)}) collective-permute-start(bf16[24,160,128]{2,1,0:T(8,128)(2,1)} %get-tuple-element.156), channel_id=1, source_target_pairs={{2,0},{3,1},{4,6},{5,7},{10,8},{11,9},{12,14},{13,15},{18,16},{19,... | collective-permute-start | bytes 2949128 | tf_op jit(solution)/shard_map/ppermute | solution.py:409
  102.9 4.4 %copy-start.27 = (bf16[8,80,128]{2,1,0:T(8,128)(2,1)}, bf16[8,80,128]{2,1,0:T(8,128)(2,1)S(1)}, u32[]{:S(2)}) copy-start(bf16[8,80,128]{2,1,0:T(8,128)(2,1)S(1)} %get-tuple-element.216) | copy-start | bytes 491524
  102.9 10.7 %copy-start.25 = (bf16[2,8,80,128]{3,2,1,0:T(8,128)(2,1)}, bf16[2,8,80,128]{3,2,1,0:T(8,128)(2,1)S(1)}, u32[]{:S(2)}) copy-start(bf16[2,8,80,128]{3,2,1,0:T(8,128)(2,1)S(1)} %get-tuple-element.182.refs_1_) | copy-start | bytes 983044
  103.0 15.8 %collective-permute-start.15 = (bf16[8,80,128]{2,1,0:T(8,128)(2,1)S(1)}, bf16[8,80,128]{2,1,0:T(8,128)(2,1)S(1)}, u32[]{:S(2)}, u32[]{:S(2)}) collective-permute-start(bf16[8,80,128]{2,1,0:T(8,128)(2,1)S(1)} %get-tuple-element.183), channel_id=1, source_target_pairs={{0,1},{1,0},{2,3},{3,2},{4,5},{5,4},{6,7},{7,6},{8,9},{9,8},{10,11... | collective-permute-start | bytes 491528 | tf_op jit(solution)/shard_map/ppermute | solution.py:678
  117.5 9.3 %collective-permute-start.11 = (bf16[8,160,128]{2,1,0:T(8,128)(2,1)S(1)}, bf16[8,160,128]{2,1,0:T(8,128)(2,1)S(1)}, u32[]{:S(2)}, u32[]{:S(2)}) collective-permute-start(bf16[8,160,128]{2,1,0:T(8,128)(2,1)S(1)} %get-tuple-element.161), channel_id=1, source_target_pairs={{2,0},{3,1},{4,6},{5,7},{10,8},{11,9},{12,14},{13,15},{18,16},{19,... | collective-permute-start | bytes 983048 | tf_op jit(solution)/shard_map/ppermute | solution.py:409
  118.9 35.2 %collective-permute-start.10 = (bf16[2,16,160,128]{3,2,1,0:T(8,128)(2,1)}, bf16[2,16,160,128]{3,2,1,0:T(8,128)(2,1)S(1)}, u32[]{:S(2)}, u32[]{:S(2)}) collective-permute-start(bf16[2,16,160,128]{3,2,1,0:T(8,128)(2,1)} %get-tuple-element.158.refs_1_), channel_id=1, source_target_pairs={{2,4},{3,5},{4,2},{5,3},{10,12},{11,13},{12,10},{13,11},{18,20},{1... | collective-permute-start | bytes 3932168 | tf_op jit(solution)/shard_map/ppermute | solution.py:409
  119.6 30.0 %collective-permute-start.12 = (bf16[12,400,128]{2,1,0:T(8,128)(2,1)}, bf16[12,400,128]{2,1,0:T(8,128)(2,1)S(1)}, u32[]{:S(2)}, u32[]{:S(2)}) collective-permute-start(bf16[12,400,128]{2,1,0:T(8,128)(2,1)} %get-tuple-element.170), channel_id=1, source_target_pairs={{0,2},{1,3},{8,10},{9,11},{16,18},{17,19},{24,26},{25,27}} | collective-permute-start | bytes 3686408 | tf_op jit(solution)/shard_map/ppermute | solution.py:409
  127.0 36.8 %collective-permute-start.16 = (bf16[40,160,128]{2,1,0:T(8,128)(2,1)S(1)}, bf16[40,160,128]{2,1,0:T(8,128)(2,1)S(1)}, u32[]{:S(2)}, u32[]{:S(2)}) collective-permute-start(bf16[40,160,128]{2,1,0:T(8,128)(2,1)S(1)} %get-tuple-element.184), channel_id=1, source_target_pairs={{2,0},{3,1},{4,6},{5,7},{10,8},{11,9},{12,14},{13,15},{18,16},{19,... | collective-permute-start | bytes 4915208 | tf_op jit(solution)/shard_map/ppermute | solution.py:409
  149.7 29.4 %collective-permute-start.13 = (bf16[2,16,160,128]{3,2,1,0:T(8,128)(2,1)}, bf16[2,16,160,128]{3,2,1,0:T(8,128)(2,1)S(1)}, u32[]{:S(2)}, u32[]{:S(2)}) collective-permute-start(bf16[2,16,160,128]{3,2,1,0:T(8,128)(2,1)} %get-tuple-element.172), channel_id=1, source_target_pairs={{0,2},{1,3},{6,4},{7,5},{8,10},{9,11},{14,12},{15,13},{16,18},{17,... | collective-permute-start | bytes 3932168 | tf_op jit(solution)/shard_map/ppermute | solution.py:409
  154.1 25.0 %collective-permute-start.14 = (bf16[2,16,160,128]{3,2,1,0:T(8,128)(2,1)S(1)}, bf16[2,16,160,128]{3,2,1,0:T(8,128)(2,1)S(1)}, u32[]{:S(2)}, u32[]{:S(2)}) collective-permute-start(bf16[2,16,160,128]{3,2,1,0:T(8,128)(2,1)S(1)} %get-tuple-element.166.refs_0_), channel_id=1, source_target_pairs={{2,4},{3,5},{4,2},{5,3},{10,12},{11,13},{12,10},{13,11},{18,20},{1... | collective-permute-start | bytes 3932168 | tf_op jit(solution)/shard_map/ppermute | solution.py:409
  163.8 6.4 %copy-start = (bf16[40,160,128]{2,1,0:T(8,128)(2,1)}, bf16[40,160,128]{2,1,0:T(8,128)(2,1)S(1)}, u32[]{:S(2)}) copy-start(bf16[40,160,128]{2,1,0:T(8,128)(2,1)S(1)} %get-tuple-element.188.refs_5_.refs_4_) | copy-start | bytes 4915204
  163.8 14.7 %collective-permute-start.18 = (bf16[16,160,128]{2,1,0:T(8,128)(2,1)S(1)}, bf16[16,160,128]{2,1,0:T(8,128)(2,1)S(1)}, u32[]{:S(2)}, u32[]{:S(2)}) collective-permute-start(bf16[16,160,128]{2,1,0:T(8,128)(2,1)S(1)} %get-tuple-element.189), channel_id=1, source_target_pairs={{2,0},{3,1},{4,6},{5,7},{10,8},{11,9},{12,14},{13,15},{18,16},{19,... | collective-permute-start | bytes 1966088 | tf_op jit(solution)/shard_map/ppermute | solution.py:409
  170.2 4.4 %collective-permute-start.19 = (bf16[16,80,128]{2,1,0:T(8,128)(2,1)S(1)}, bf16[16,80,128]{2,1,0:T(8,128)(2,1)S(1)}, u32[]{:S(2)}, u32[]{:S(2)}) collective-permute-start(bf16[16,80,128]{2,1,0:T(8,128)(2,1)S(1)} %get-tuple-element.194), channel_id=1, source_target_pairs={{0,1},{1,0},{2,3},{3,2},{4,5},{5,4},{6,7},{7,6},{8,9},{9,8},{10,11... | collective-permute-start | bytes 983048 | tf_op jit(solution)/shard_map/ppermute | solution.py:678
  180.2 29.4 %collective-permute-start.20 = (bf16[32,160,128]{2,1,0:T(8,128)(2,1)S(1)}, bf16[32,160,128]{2,1,0:T(8,128)(2,1)S(1)}, u32[]{:S(2)}, u32[]{:S(2)}) collective-permute-start(bf16[32,160,128]{2,1,0:T(8,128)(2,1)S(1)} %get-tuple-element.196), channel_id=1, source_target_pairs={{2,0},{3,1},{4,6},{5,7},{10,8},{11,9},{12,14},{13,15},{18,16},{19,... | collective-permute-start | bytes 3932168 | tf_op jit(solution)/shard_map/ppermute | solution.py:409
  181.5 12.6 %copy-start.4 = (bf16[2,16,160,128]{3,2,1,0:T(8,128)(2,1)}, bf16[2,16,160,128]{3,2,1,0:T(8,128)(2,1)S(1)}, u32[]{:S(2)}) copy-start(bf16[2,16,160,128]{3,2,1,0:T(8,128)(2,1)S(1)} %get-tuple-element.186.refs_1_) | copy-start | bytes 3932164
  181.5 28.1 %collective-permute-start.17 = (bf16[2,16,160,128]{3,2,1,0:T(8,128)(2,1)S(1)}, bf16[2,16,160,128]{3,2,1,0:T(8,128)(2,1)S(1)}, u32[]{:S(2)}, u32[]{:S(2)}) collective-permute-start(bf16[2,16,160,128]{3,2,1,0:T(8,128)(2,1)S(1)} %get-tuple-element.186.refs_1_), channel_id=1, source_target_pairs={{2,4},{3,5},{4,2},{5,3},{10,12},{11,13},{12,10},{13,11},{18,20},{1... | collective-permute-start | bytes 3932168 | tf_op jit(solution)/shard_map/ppermute | solution.py:409
  182.2 29.7 %collective-permute-start.22 = (bf16[12,400,128]{2,1,0:T(8,128)(2,1)}, bf16[12,400,128]{2,1,0:T(8,128)(2,1)S(1)}, u32[]{:S(2)}, u32[]{:S(2)}) collective-permute-start(bf16[12,400,128]{2,1,0:T(8,128)(2,1)} %get-tuple-element.202), channel_id=1, source_target_pairs={{0,2},{1,3},{8,10},{9,11},{16,18},{17,19},{24,26},{25,27}} | collective-permute-start | bytes 3686408 | tf_op jit(solution)/shard_map/ppermute | solution.py:409
  209.6 2.4 copy-start.9
  210.6 13.7 %collective-permute-start.21 = (bf16[16,160,128]{2,1,0:T(8,128)(2,1)S(1)}, bf16[16,160,128]{2,1,0:T(8,128)(2,1)S(1)}, u32[]{:S(2)}, u32[]{:S(2)}) collective-permute-start(bf16[16,160,128]{2,1,0:T(8,128)(2,1)S(1)} %get-tuple-element.199), channel_id=1, source_target_pairs={{2,0},{3,1},{4,6},{5,7},{10,8},{11,9},{12,14},{13,15},{18,16},{19,... | collective-permute-start | bytes 1966088 | tf_op jit(solution)/shard_map/ppermute | solution.py:409
  218.2 1.6 collective-permute-start.23
  218.2 7.5 %copy-start.28 = (bf16[8,80,128]{2,1,0:T(8,128)(2,1)S(1)}, bf16[8,80,128]{2,1,0:T(8,128)(2,1)}, u32[]{:S(2)}) copy-start(bf16[8,80,128]{2,1,0:T(8,128)(2,1)} %copy-done.27) | copy-start | bytes 491524
  218.2 8.5 %copy-start.5 = (bf16[2,16,160,128]{3,2,1,0:T(8,128)(2,1)S(1)}, bf16[2,16,160,128]{3,2,1,0:T(8,128)(2,1)}, u32[]{:S(2)}) copy-start(bf16[2,16,160,128]{3,2,1,0:T(8,128)(2,1)} %copy-done.4) | copy-start | bytes 3932164
  218.2 8.5 %copy-start.8 = (bf16[2,16,160,128]{3,2,1,0:T(8,128)(2,1)S(1)}, bf16[2,16,160,128]{3,2,1,0:T(8,128)(2,1)}, u32[]{:S(2)}) copy-start(bf16[2,16,160,128]{3,2,1,0:T(8,128)(2,1)} %copy-done.7) | copy-start | bytes 3932164
  224.4 14.7 %collective-permute-start.24 = (bf16[16,160,128]{2,1,0:T(8,128)(2,1)S(1)}, bf16[16,160,128]{2,1,0:T(8,128)(2,1)S(1)}, u32[]{:S(2)}, u32[]{:S(2)}) collective-permute-start(bf16[16,160,128]{2,1,0:T(8,128)(2,1)S(1)} %get-tuple-element.210), channel_id=1, source_target_pairs={{2,0},{3,1},{10,8},{11,9},{18,16},{19,17},{26,24},{27,25}} | collective-permute-start | bytes 1966088 | tf_op jit(solution)/shard_map/ppermute | solution.py:409
  225.7 5.4 %collective-permute-start.28 = (bf16[8,80,128]{2,1,0:T(8,128)(2,1)S(1)}, bf16[8,80,128]{2,1,0:T(8,128)(2,1)S(1)}, u32[]{:S(2)}, u32[]{:S(2)}) collective-permute-start(bf16[8,80,128]{2,1,0:T(8,128)(2,1)S(1)} %copy-done.28), channel_id=1, source_target_pairs={{0,1},{1,0},{2,3},{3,2},{4,5},{5,4},{6,7},{7,6},{8,9},{9,8},{10,11... | collective-permute-start | bytes 491528 | tf_op jit(solution)/shard_map/ppermute | solution.py:677
  225.7 5.4 %collective-permute-start.27 = (bf16[8,80,128]{2,1,0:T(8,128)(2,1)}, bf16[8,80,128]{2,1,0:T(8,128)(2,1)S(1)}, u32[]{:S(2)}, u32[]{:S(2)}) collective-permute-start(bf16[8,80,128]{2,1,0:T(8,128)(2,1)} %get-tuple-element.215), channel_id=1, source_target_pairs={{0,1},{1,0},{2,3},{3,2},{4,5},{5,4},{6,7},{7,6},{8,9},{9,8},{10,11... | collective-permute-start | bytes 491528 | tf_op jit(solution)/shard_map/ppermute | solution.py:695
  226.2 6.9 %collective-permute-start.26 = (bf16[16,80,128]{2,1,0:T(8,128)(2,1)S(1)}, bf16[16,80,128]{2,1,0:T(8,128)(2,1)S(1)}, u32[]{:S(2)}, u32[]{:S(2)}) collective-permute-start(bf16[16,80,128]{2,1,0:T(8,128)(2,1)S(1)} %get-tuple-element.213), channel_id=1, source_target_pairs={{0,1},{1,0},{2,3},{3,2},{4,5},{5,4},{6,7},{7,6},{8,9},{9,8},{10,11... | collective-permute-start | bytes 983048 | tf_op jit(solution)/shard_map/ppermute | solution.py:677
  226.3 6.8 %collective-permute-start.25 = (bf16[16,80,128]{2,1,0:T(8,128)(2,1)S(1)}, bf16[16,80,128]{2,1,0:T(8,128)(2,1)S(1)}, u32[]{:S(2)}, u32[]{:S(2)}) collective-permute-start(bf16[16,80,128]{2,1,0:T(8,128)(2,1)S(1)} %get-tuple-element.212), channel_id=1, source_target_pairs={{0,1},{1,0},{2,3},{3,2},{4,5},{5,4},{6,7},{7,6},{8,9},{9,8},{10,11... | collective-permute-start | bytes 983048 | tf_op jit(solution)/shard_map/ppermute | solution.py:695
  226.7 4.9 %copy-start.1 = (bf16[40,160,128]{2,1,0:T(8,128)(2,1)S(1)}, bf16[40,160,128]{2,1,0:T(8,128)(2,1)}, u32[]{:S(2)}) copy-start(bf16[40,160,128]{2,1,0:T(8,128)(2,1)} %copy-done) | copy-start | bytes 4915204
  226.7 4.9 %copy-start.26 = (bf16[2,8,80,128]{3,2,1,0:T(8,128)(2,1)S(1)}, bf16[2,8,80,128]{3,2,1,0:T(8,128)(2,1)}, u32[]{:S(2)}) copy-start(bf16[2,8,80,128]{3,2,1,0:T(8,128)(2,1)} %copy-done.25) | copy-start | bytes 983044
  231.0 8.0 %collective-permute-start.30 = (bf16[16,80,128]{2,1,0:T(8,128)(2,1)S(1)}, bf16[16,80,128]{2,1,0:T(8,128)(2,1)S(1)}, u32[]{:S(2)}, u32[]{:S(2)}) collective-permute-start(bf16[16,80,128]{2,1,0:T(8,128)(2,1)S(1)} %get-tuple-element.222), channel_id=1, source_target_pairs={{0,1},{1,0},{2,3},{3,2},{4,5},{5,4},{6,7},{7,6},{8,9},{9,8},{10,11... | collective-permute-start | bytes 983048 | tf_op jit(solution)/shard_map/ppermute | solution.py:677
  231.2 7.9 %collective-permute-start.29 = (bf16[16,80,128]{2,1,0:T(8,128)(2,1)S(1)}, bf16[16,80,128]{2,1,0:T(8,128)(2,1)S(1)}, u32[]{:S(2)}, u32[]{:S(2)}) collective-permute-start(bf16[16,80,128]{2,1,0:T(8,128)(2,1)S(1)} %get-tuple-element.221), channel_id=1, source_target_pairs={{0,1},{1,0},{2,3},{3,2},{4,5},{5,4},{6,7},{7,6},{8,9},{9,8},{10,11... | collective-permute-start | bytes 983048 | tf_op jit(solution)/shard_map/ppermute | solution.py:695
  231.6 1.5 copy-start.3
  (14 other events, 15.6 us)

commit v5 on v4

--- a/solution.py
+++ b/solution.py
@@ -601,7 +601,6 @@
     first_in, first_cross, second_cross = [[None] * count for _ in range(3)]
     first_out, second_out, third_out = [[None] * count for _ in range(3)]
     in_mark, out_mark, out2_mark, out3_mark = [[None] * count for _ in range(4)]
-    finish_mark = [None] * count
     inward, centre, outward = Links(), Links(), Links()
     last = count - 1
 
@@ -636,7 +635,7 @@
         both[i], first_cross[i], _ = centre.send(both[i], CENTRE, after, meanwhile)
 
     def send_cross2(i):
-        after = (at(out2_mark, i - 1),)
+        after = ()
         meanwhile = (at(halves_mark, 1) if i == 0 else None, at(low_mark, i - 1))
         first_in[i], second_cross[i], _ = centre.send(first_in[i], CENTRE, after, meanwhile)
 
@@ -684,7 +683,7 @@
         third_out[i] = Piece(found)
 
     def send_back(i):
-        _, found, _ = outward.send(returned[i], RETURN, (), (at(finish_mark, i - 1), at(low_mark, i)))
+        _, found, _ = outward.send(returned[i], RETURN)
         came_back(i, found, 0)
 
     def do_low(i):
@@ -695,7 +694,7 @@
         got_low[i] = lax.ppermute(sent, "lev", swap)
 
     def do_finish(i):
-        finish_mark[i] = finish(
+        finish(
             i,
             [Piece(found_low[i]), Piece(high[i], 0, 0), back[i][0]],
             [Piece(got_low[i]), Piece(got_high[i]), back[i][1]],
@@ -728,8 +727,8 @@
         if i < last:
             send_cross(i + 1)
         send_out3(i)
+    send_back(last)
     do_low(last)
-    send_back(last)
     do_finish(last)
     return state["out"].reshape(slots, degrees, columns)
 

time: 242 us -> 242 us (level)
  no operation moved by 1% of the time
where the time goes in v5:
time: 242 us; the launch traced here: 241 us
  Pallas kernels  80.1 us (33%)
  waiting for transfers between devices  76 us (31%)
  starting transfers between devices  63 us (26%)
  local copies, waits for them, and re-layouts  16.4 us (7%)
  other arithmetic  4.63 us (2%)
    ppermute x21, waiting for transfers between devices, send(): return lax.ppermute(block, 'lev', on_cores(pairs))  73.4 us
    ppermute x21, starting transfers between devices, send(): return lax.ppermute(block, 'lev', on_cores(pairs))  51.8 us
    pallas_call x13, Pallas kernels, over_pairs(): pl.pallas_call(kernel, grid_spec=pltpu.PrefetchScalarGridSpec(num_scalar_...  48.1 us
    pallas_call x3, Pallas kernels, halves(): pl.pallas_call(functools.partial(halves_kernel, fields, wide), grid=(1,),...  14.2 us
    unnamed x58, local copies, waits for them, and re-layouts  11.7 us
    pallas_call x1, Pallas kernels, zonal(): pl.pallas_call(functools.partial(zonal_kernel, start, sizes), grid=(colum...  9.98 us
    all_to_all x2, starting transfers between devices, exchange(): lax.all_to_all(found, ('lat', 'lev'), split_axis=0, concat_axis=0, axis_i...  9.01 us
    pallas_call x1, Pallas kernels, fold_and_zonal(): pl.pallas_call(functools.partial(fold_kernel, start, sizes, group), grid=...  7.73 us
  transfers between devices with their start and end apart: 33, of which 13 were waited for; matrix products, arithmetic and copies ran while one was open for 4% of the time, Pallas kernels for 32%

profile of v5, /device:TPU:0, one launch (start us, length us, event | category | flops | bytes accessed | tf_op | source)
XLA Modules:
  0.0 240.9 jit_solution(549268403342127060)
XLA Ops:
  2.6 1.4 cosine_multiply_fusion
  4.3 7.7 %fold_and_zonal.1 = (bf16[8,32,1280]{2,1,0:T(8,128)(2,1)}, bf16[1280,640]{1,0:T(8,128)(2,1)S(1)}, bf16[1280,640]{1,0:T(8,128)(2,1)S(1)}, bf16[1280,640]{1,0:T(8,...) custom-call(f32[2,2,320,128]{3,2,1,0:T(8,128)S(1)} %pad_maximum_fusion.3.base_ref, ...), custom_call_target="tpu_custom_call" | custom-call | flops 1000 | bytes 1000 | tf_op jit(solution)/shard_map/fold_and_zonal/pallas_call | solution.py:96
  14.3 4.8 %all-to-all-start.1 = ((bf16[8,32,1280]{2,1,0:T(8,128)(2,1)}), bf16[8,32,1280]{2,1,0:T(8,128)(2,1)S(1)}, u32[]{:S(2)}, u32[]{:S(2)}) async-start(bf16[8,32,1280]{2,1,0:T(8,128)(2,1)} %get-tuple-element.120), calls=%async_computation.1 | async-start | bytes 1310720 | tf_op jit(solution)/shard_map/all_to_all | solution.py:504
  20.0 3.4 %give.4 = (bf16[8,400,128]{2,1,0:T(8,128)(2,1)}, f32[8,128]{1,0:T(8,128)S(1)}) custom-call(s32[1]{0:T(128)} %bitcast.info_ref, s32[80]{0:T(128)S(1)} %dynamic-slice_bitcast_fusion.waves_ref, bf16[160,80,320]{2,1,0:T(8,128)(2,1)} %own_ref.19, bf16[160,80,320]{2,1,0:T(8,128)(2,1)} %collective-permute-done.other_ref, f32[8,128]{1,0:T(8,128)S(1)} %get-tuple-element.117.refs_0_), custom_call_target="tpu_custom_call" | custom-call | flops 1000 | bytes 1000 | tf_op jit(solution)/shard_map/give/pallas_call | solution.py:316
  23.4 3.5 %collective-permute-start.1 = (bf16[8,400,128]{2,1,0:T(8,128)(2,1)}, bf16[8,400,128]{2,1,0:T(8,128)(2,1)S(1)}, u32[]{:S(2)}, u32[]{:S(2)}) collective-permute-start(bf16[8,400,128]{2,1,0:T(8,128)(2,1)} %get-tuple-element.130), channel_id=1, source_target_pairs={{0,2},{1,3},{8,10},{9,11},{16,18},{17,19},{24,26},{25,27}} | collective-permute-start | bytes 2457608 | tf_op jit(solution)/shard_map/ppermute | solution.py:409
  27.0 10.0 %zonal.1 = (bf16[8,128,1280]{2,1,0:T(8,128)(2,1)}, f32[8,128]{1,0:T(8,128)S(1)}) custom-call(f32[2,2,320,128]{3,2,1,0:T(8,128)S(1)} %pad_maximum_fusion.3.base_ref, f32[2,2,320,5]{3,2,1,0:T(8,128)S(1)} %copy.61.step_ref, f32[320,1]{1,0:T(8,128)S(1)} %fusion.7.first_ref, bf16[1280,640]{1,0:T(8,128)(2,1)S(1)} %copy-done.22, bf16[1280,640]{1,0:T(8,128)(2,1)S(1)} %copy-done.24, ...), custom_call_target="tpu_custom_call" | custom-call | flops 1000 | bytes 1000 | tf_op jit(solution)/shard_map/zonal/pallas_call | solution.py:137
  37.8 4.2 %all-to-all-start = ((bf16[8,128,1280]{2,1,0:T(8,128)(2,1)}), bf16[8,128,1280]{2,1,0:T(8,128)(2,1)S(1)}, u32[]{:S(2)}, u32[]{:S(2)}) async-start(bf16[8,128,1280]{2,1,0:T(8,128)(2,1)} %get-tuple-element.119), calls=%async_computation | async-start | bytes 5242880 | tf_op jit(solution)/shard_map/all_to_all | solution.py:504
  43.1 3.0 %halves.3 = (bf16[2,8,160,128]{3,2,1,0:T(8,128)(2,1)S(1)}, bf16[2,8,160,128]{3,2,1,0:T(8,128)(2,1)S(1)}, bf16[8,160,128]{2,1,0:T(8,128)(2,1)}, f32[8,128]{1,0:T(8,128)S(1)}) custom-call(bf16[8,32,1280]{2,1,0:T(8,128)(2,1)S(1)} %copy-done.20, f32[8,128]{1,0:T(8,128)S(1)} %get-tuple-element.121.refs_0_), custom_call_target="tpu_custom_call" | custom-call | flops 1000 | bytes 1000 | tf_op jit(solution)/shard_map/halves/pallas_call | solution.py:183
  47.1 3.5 %collective-permute-start.2 = (bf16[2,8,160,128]{3,2,1,0:T(8,128)(2,1)S(1)}, bf16[2,8,160,128]{3,2,1,0:T(8,128)(2,1)S(1)}, u32[]{:S(2)}, u32[]{:S(2)}) collective-permute-start(bf16[2,8,160,128]{3,2,1,0:T(8,128)(2,1)S(1)} %get-tuple-element.132), channel_id=1, source_target_pairs={{0,2},{1,3},{6,4},{7,5},{8,10},{9,11},{14,12},{15,13},{16,18},{17,... | collective-permute-start | bytes 1966088 | tf_op jit(solution)/shard_map/ppermute | solution.py:409
  51.3 3.1 %give.5 = (bf16[8,400,128]{2,1,0:T(8,128)(2,1)}, f32[8,128]{1,0:T(8,128)S(1)}) custom-call(s32[1]{0:T(128)} %bitcast.info_ref, s32[80]{0:T(128)S(1)} %dynamic-slice_bitcast_fusion.waves_ref, bf16[160,80,320]{2,1,0:T(8,128)(2,1)} %own_ref.19, bf16[160,80,320]{2,1,0:T(8,128)(2,1)} %collective-permute-done.other_ref, f32[8,128]{1,0:T(8,128)S(1)} %get-tuple-element.122.refs_0_), custom_call_target="tpu_custom_call" | custom-call | flops 1000 | bytes 1000 | tf_op jit(solution)/shard_map/give/pallas_call | solution.py:316
  54.4 10.0 %collective-permute-done.2.refs_0_ = bf16[2,8,160,128]{3,2,1,0:T(8,128)(2,1)S(1)} collective-permute-done((bf16[2,8,160,128]{3,2,1,0:T(8,128)(2,1)S(1)}, bf16[2,8,160,128]{3,2,1,0:T(8,128)(2,1)S(1)}, u32[]{:S(2)}, u32[]{:S(2)}) %collective-permute-start.2) | collective-permute-done | bytes 655392 | tf_op jit(solution)/shard_map/ppermute | solution.py:409
  64.4 5.3 %collective-permute-start.3 = (bf16[8,400,128]{2,1,0:T(8,128)(2,1)}, bf16[8,400,128]{2,1,0:T(8,128)(2,1)}, u32[]{:S(2)}, u32[]{:S(2)}) collective-permute-start(bf16[8,400,128]{2,1,0:T(8,128)(2,1)} %get-tuple-element.134), channel_id=1, source_target_pairs={{0,2},{1,3},{8,10},{9,11},{16,18},{17,19},{24,26},{25,27}} | collective-permute-start | bytes 2457608 | tf_op jit(solution)/shard_map/ppermute | solution.py:409
  70.6 1.5 collective-permute-start.6
  72.1 1.3 collective-permute-start.9
  74.3 5.9 %halves.4 = (bf16[2,16,160,128]{3,2,1,0:T(8,128)(2,1)}, bf16[2,16,160,128]{3,2,1,0:T(8,128)(2,1)}, bf16[16,160,128]{2,1,0:T(8,128)(2,1)S(1)}, f32[8,128]{1,0:T(8,128)S(1)}) custom-call(bf16[8,128,1280]{2,1,0:T(8,128)(2,1)S(1)} %all-to-all-done.in_ref, f32[8,128]{1,0:T(8,128)S(1)} %get-tuple-element.123.refs_0_.refs_1_), custom_call_target="tpu_custom_call" | custom-call | flops 1000 | bytes 1000 | tf_op jit(solution)/shard_map/halves/pallas_call | solution.py:183
  80.2 5.5 %collective-permute-done.3.refs_0_ = bf16[8,400,128]{2,1,0:T(8,128)(2,1)} collective-permute-done((bf16[8,400,128]{2,1,0:T(8,128)(2,1)}, bf16[8,400,128]{2,1,0:T(8,128)(2,1)}, u32[]{:S(2)}, u32[]{:S(2)}) %collective-permute-start.3) | collective-permute-done | bytes 819232 | tf_op jit(solution)/shard_map/ppermute | solution.py:409
  85.6 5.6 %collective-permute-start.4 = (bf16[2,16,160,128]{3,2,1,0:T(8,128)(2,1)}, bf16[2,16,160,128]{3,2,1,0:T(8,128)(2,1)}, u32[]{:S(2)}, u32[]{:S(2)}) collective-permute-start(bf16[2,16,160,128]{3,2,1,0:T(8,128)(2,1)} %get-tuple-element.136), channel_id=1, source_target_pairs={{0,2},{1,3},{6,4},{7,5},{8,10},{9,11},{14,12},{15,13},{16,18},{17,... | collective-permute-start | bytes 3932168 | tf_op jit(solution)/shard_map/ppermute | solution.py:409
  91.2 1.7 collective-permute-start.7
  94.0 1.5 collective-permute-start.10
  99.8 3.2 %high_slots.3 = (bf16[2,8,80,128]{3,2,1,0:T(8,128)(2,1)S(1)}, bf16[8,80,128]{2,1,0:T(8,128)(2,1)S(1)}, bf16[8,80,128]{2,1,0:T(8,128)(2,1)S(1)}, f32[8,128]{1,0:T(8,128)S(1)}) custom-call(s32[1]{0:T(128)} %bitcast.info_ref, s32[80]{0:T(128)S(1)} %dynamic-slice_bitcast_fusion.waves_ref, bf16[128,128]{1,0:T(8,128)(2,1)S(1)} %fusion.10.order_ref, ...), custom_call_target="tpu_custom_call" | custom-call | flops 1000 | bytes 1000 | tf_op jit(solution)/shard_map/high_slots/pallas_call | solution.py:316
  103.1 4.3 %give.6 = (bf16[12,400,128]{2,1,0:T(8,128)(2,1)}, f32[8,128]{1,0:T(8,128)S(1)}) custom-call(s32[1]{0:T(128)} %bitcast.info_ref, s32[80]{0:T(128)S(1)} %dynamic-slice_bitcast_fusion.waves_ref, bf16[160,80,320]{2,1,0:T(8,128)(2,1)} %own_ref.19, bf16[160,80,320]{2,1,0:T(8,128)(2,1)} %collective-permute-done.other_ref, ...), custom_call_target="tpu_custom_call" | custom-call | flops 1000 | bytes 1000 | tf_op jit(solution)/shard_map/give/pallas_call | solution.py:316
  107.3 5.4 %halves.5 = (bf16[2,16,160,128]{3,2,1,0:T(8,128)(2,1)S(1)}, bf16[2,16,160,128]{3,2,1,0:T(8,128)(2,1)}, bf16[16,160,128]{2,1,0:T(8,128)(2,1)S(1)}, f32[8,128]{1,0:T(8,128)S(1)}) custom-call(bf16[8,128,1280]{2,1,0:T(8,128)(2,1)S(1)} %all-to-all-done.in_ref, f32[8,128]{1,0:T(8,128)S(1)} %get-tuple-element.125.refs_0_.refs_2_), custom_call_target="tpu_custom_call" | custom-call | flops 1000 | bytes 1000 | tf_op jit(solution)/shard_map/halves/pallas_call | solution.py:183
  113.7 3.8 %collective-permute-done.10.refs_0_ = bf16[24,160,128]{2,1,0:T(8,128)(2,1)} collective-permute-done((bf16[24,160,128]{2,1,0:T(8,128)(2,1)}, bf16[24,160,128]{2,1,0:T(8,128)(2,1)}, u32[]{:S(2)}, u32[]{:S(2)}) %collective-permute-start.10) | collective-permute-done | bytes 983072 | tf_op jit(solution)/shard_map/ppermute | solution.py:409
  117.5 1.3 collective-permute-start.11
  119.7 5.8 %collective-permute-start.12 = (bf16[12,400,128]{2,1,0:T(8,128)(2,1)}, bf16[12,400,128]{2,1,0:T(8,128)(2,1)S(1)}, u32[]{:S(2)}, u32[]{:S(2)}) collective-permute-start(bf16[12,400,128]{2,1,0:T(8,128)(2,1)} %get-tuple-element.168), channel_id=1, source_target_pairs={{0,2},{1,3},{8,10},{9,11},{16,18},{17,19},{24,26},{25,27}} | collective-permute-start | bytes 3686408 | tf_op jit(solution)/shard_map/ppermute | solution.py:409
  127.1 1.4 collective-permute-start.17
  128.5 3.8 %low_slots.3 = (bf16[8,80,128]{2,1,0:T(8,128)(2,1)S(1)}, bf16[8,80,128]{2,1,0:T(8,128)(2,1)}, f32[8,128]{1,0:T(8,128)S(1)}) custom-call(s32[1]{0:T(128)} %bitcast.info_ref, s32[80]{0:T(128)S(1)} %dynamic-slice_bitcast_fusion.waves_ref, bf16[128,128]{1,0:T(8,128)(2,1)S(1)} %fusion.10.order_ref, bf16[160,80,320]{2,1,0:T(8,128)(2,1)} %own_ref.19, ...), custom_call_target="tpu_custom_call" | custom-call | flops 1000 | bytes 1000 | tf_op jit(solution)/shard_map/low_slots/pallas_call | solution.py:316
  132.3 17.4 %collective-permute-done.12.refs_0_ = bf16[12,400,128]{2,1,0:T(8,128)(2,1)S(1)} collective-permute-done((bf16[12,400,128]{2,1,0:T(8,128)(2,1)}, bf16[12,400,128]{2,1,0:T(8,128)(2,1)S(1)}, u32[]{:S(2)}, u32[]{:S(2)}) %collective-permute-start.12) | collective-permute-done | bytes 1228832 | tf_op jit(solution)/shard_map/ppermute | solution.py:409
  149.7 4.4 %collective-permute-start.13 = (bf16[2,16,160,128]{3,2,1,0:T(8,128)(2,1)}, bf16[2,16,160,128]{3,2,1,0:T(8,128)(2,1)S(1)}, u32[]{:S(2)}, u32[]{:S(2)}) collective-permute-start(bf16[2,16,160,128]{3,2,1,0:T(8,128)(2,1)} %get-tuple-element.170), channel_id=1, source_target_pairs={{0,2},{1,3},{6,4},{7,5},{8,10},{9,11},{14,12},{15,13},{16,18},{17,... | collective-permute-start | bytes 3932168 | tf_op jit(solution)/shard_map/ppermute | solution.py:409
  155.2 8.7 %collective-permute-done.17.refs_0_ = bf16[40,160,128]{2,1,0:T(8,128)(2,1)S(1)} collective-permute-done((bf16[40,160,128]{2,1,0:T(8,128)(2,1)S(1)}, bf16[40,160,128]{2,1,0:T(8,128)(2,1)S(1)}, u32[]{:S(2)}, u32[]{:S(2)}) %collective-permute-start.17) | collective-permute-done | bytes 1638432 | tf_op jit(solution)/shard_map/ppermute | solution.py:409
  163.9 1.3 collective-permute-start.18
  165.2 5.1 %high_slots.4 = (bf16[2,16,80,128]{3,2,1,0:T(8,128)(2,1)S(1)}, bf16[16,80,128]{2,1,0:T(8,128)(2,1)S(1)}, bf16[16,80,128]{2,1,0:T(8,128)(2,1)S(1)}, f32[8,128]{1,0:T(8,128)S(1)}) custom-call(s32[1]{0:T(128)} %bitcast.info_ref, s32[80]{0:T(128)S(1)} %dynamic-slice_bitcast_fusion.waves_ref, bf16[128,128]{1,0:T(8,128)(2,1)S(1)} %fusion.10.order_ref, ...), custom_call_target="tpu_custom_call" | custom-call | flops 1000 | bytes 1000 | tf_op jit(solution)/shard_map/high_slots/pallas_call | solution.py:316
  170.4 4.3 %give.7 = (bf16[12,400,128]{2,1,0:T(8,128)(2,1)}, f32[8,128]{1,0:T(8,128)S(1)}) custom-call(s32[1]{0:T(128)} %bitcast.info_ref, s32[80]{0:T(128)S(1)} %dynamic-slice_bitcast_fusion.waves_ref, bf16[160,80,320]{2,1,0:T(8,128)(2,1)} %own_ref.19, bf16[160,80,320]{2,1,0:T(8,128)(2,1)} %collective-permute-done.other_ref, ...), custom_call_target="tpu_custom_call" | custom-call | flops 1000 | bytes 1000 | tf_op jit(solution)/shard_map/give/pallas_call | solution.py:316
  174.7 3.8 %collective-permute-done.18.refs_0_ = bf16[16,160,128]{2,1,0:T(8,128)(2,1)S(1)} collective-permute-done((bf16[16,160,128]{2,1,0:T(8,128)(2,1)S(1)}, bf16[16,160,128]{2,1,0:T(8,128)(2,1)S(1)}, u32[]{:S(2)}, u32[]{:S(2)}) %collective-permute-start.18) | collective-permute-done | bytes 655392 | tf_op jit(solution)/shard_map/ppermute | solution.py:409
  180.2 1.3 collective-permute-start.20
  182.3 7.0 %collective-permute-start.22 = (bf16[12,400,128]{2,1,0:T(8,128)(2,1)}, bf16[12,400,128]{2,1,0:T(8,128)(2,1)S(1)}, u32[]{:S(2)}, u32[]{:S(2)}) collective-permute-start(bf16[12,400,128]{2,1,0:T(8,128)(2,1)} %get-tuple-element.200), channel_id=1, source_target_pairs={{0,2},{1,3},{8,10},{9,11},{16,18},{17,19},{24,26},{25,27}} | collective-permute-start | bytes 3686408 | tf_op jit(solution)/shard_map/ppermute | solution.py:409
  189.3 4.7 %low_slots.4 = (bf16[16,80,128]{2,1,0:T(8,128)(2,1)S(1)}, bf16[16,80,128]{2,1,0:T(8,128)(2,1)S(1)}, f32[8,128]{1,0:T(8,128)S(1)}) custom-call(s32[1]{0:T(128)} %bitcast.info_ref, s32[80]{0:T(128)S(1)} %dynamic-slice_bitcast_fusion.waves_ref, bf16[128,128]{1,0:T(8,128)(2,1)S(1)} %fusion.10.order_ref, bf16[160,80,320]{2,1,0:T(8,128)(2,1)} %own_ref.19, ...), custom_call_target="tpu_custom_call" | custom-call | flops 1000 | bytes 1000 | tf_op jit(solution)/shard_map/low_slots/pallas_call | solution.py:316
  194.1 15.5 %collective-permute-done.20.refs_0_ = bf16[32,160,128]{2,1,0:T(8,128)(2,1)S(1)} collective-permute-done((bf16[32,160,128]{2,1,0:T(8,128)(2,1)S(1)}, bf16[32,160,128]{2,1,0:T(8,128)(2,1)S(1)}, u32[]{:S(2)}, u32[]{:S(2)}) %collective-permute-start.20) | collective-permute-done | bytes 1310752 | tf_op jit(solution)/shard_map/ppermute | solution.py:409
  210.7 1.3 collective-permute-start.21
  212.1 6.2 %high_slots.5 = (bf16[2,16,80,128]{3,2,1,0:T(8,128)(2,1)S(1)}, bf16[16,80,128]{2,1,0:T(8,128)(2,1)S(1)}, bf16[16,80,128]{2,1,0:T(8,128)(2,1)S(1)}, f32[8,128]{1,0:T(8,128)}) custom-call(s32[1]{0:T(128)} %bitcast.info_ref, s32[80]{0:T(128)S(1)} %dynamic-slice_bitcast_fusion.waves_ref, bf16[128,128]{1,0:T(8,128)(2,1)S(1)} %fusion.10.order_ref, ...), custom_call_target="tpu_custom_call" | custom-call | flops 1000 | bytes 1000 | tf_op jit(solution)/shard_map/high_slots/pallas_call | solution.py:316
  218.3 1.6 collective-permute-done.23
  219.9 4.5 %collective-permute-done.21.refs_0_ = bf16[16,160,128]{2,1,0:T(8,128)(2,1)S(1)} collective-permute-done((bf16[16,160,128]{2,1,0:T(8,128)(2,1)S(1)}, bf16[16,160,128]{2,1,0:T(8,128)(2,1)S(1)}, u32[]{:S(2)}, u32[]{:S(2)}) %collective-permute-start.21) | collective-permute-done | bytes 655392 | tf_op jit(solution)/shard_map/ppermute | solution.py:409
  224.4 1.3 collective-permute-start.24
  226.8 4.7 %low_slots.5 = (bf16[16,80,128]{2,1,0:T(8,128)(2,1)S(1)}, bf16[16,80,128]{2,1,0:T(8,128)(2,1)S(1)}, f32[8,128]{1,0:T(8,128)}) custom-call(s32[1]{0:T(128)} %bitcast.info_ref, s32[80]{0:T(128)S(1)} %dynamic-slice_bitcast_fusion.waves_ref, bf16[128,128]{1,0:T(8,128)(2,1)S(1)} %fusion.10.order_ref, bf16[160,80,320]{2,1,0:T(8,128)(2,1)} %own_ref.19, ...), custom_call_target="tpu_custom_call" | custom-call | flops 1000 | bytes 1000 | tf_op jit(solution)/shard_map/low_slots/pallas_call | solution.py:316
  232.0 1.5 finish.3
  233.6 1.9 finish.4
  235.5 3.5 %collective-permute-done.24.refs_0_ = bf16[16,160,128]{2,1,0:T(8,128)(2,1)S(1)} collective-permute-done((bf16[16,160,128]{2,1,0:T(8,128)(2,1)S(1)}, bf16[16,160,128]{2,1,0:T(8,128)(2,1)S(1)}, u32[]{:S(2)}, u32[]{:S(2)}) %collective-permute-start.24) | collective-permute-done | bytes 655392 | tf_op jit(solution)/shard_map/ppermute | solution.py:409
  239.1 1.9 finish.5
  (173 shorter events, 26.5 us)
Async XLA Ops:
  0.0 20.0 %collective-permute-start = (bf16[160,80,320]{2,1,0:T(8,128)(2,1)}, bf16[160,80,320]{2,1,0:T(8,128)(2,1)}, u32[]{:S(2)}, u32[]{:S(2)}) collective-permute-start(bf16[160,80,320]{2,1,0:T(8,128)(2,1)} %own_ref.19), channel_id=1, source_target_pairs={{0,1},{1,0},{2,3},{3,2},{4,5},{5,4},{6,7},{7,6},{8,9},{9,8},{10,11... | collective-permute-start | bytes 24576008 | tf_op jit(solution)/shard_map/ppermute | solution.py:499
  14.3 22.6 %all-to-all-start.1 = ((bf16[8,32,1280]{2,1,0:T(8,128)(2,1)}), bf16[8,32,1280]{2,1,0:T(8,128)(2,1)S(1)}, u32[]{:S(2)}, u32[]{:S(2)}) async-start(bf16[8,32,1280]{2,1,0:T(8,128)(2,1)} %get-tuple-element.120), calls=%async_computation.1 | async-start | bytes 1310720 | tf_op jit(solution)/shard_map/all_to_all | solution.py:504
  20.0 7.0 %copy-start.22 = (bf16[1280,640]{1,0:T(8,128)(2,1)S(1)}, bf16[1280,640]{1,0:T(8,128)(2,1)}, u32[]{:S(2)}) copy-start(bf16[1280,640]{1,0:T(8,128)(2,1)} %copy-done.21) | copy-start | bytes 4915204
  20.0 7.0 %copy-start.24 = (bf16[1280,640]{1,0:T(8,128)(2,1)S(1)}, bf16[1280,640]{1,0:T(8,128)(2,1)}, u32[]{:S(2)}) copy-start(bf16[1280,640]{1,0:T(8,128)(2,1)} %copy-done.23) | copy-start | bytes 4915204
  23.4 22.7 %collective-permute-start.1 = (bf16[8,400,128]{2,1,0:T(8,128)(2,1)}, bf16[8,400,128]{2,1,0:T(8,128)(2,1)S(1)}, u32[]{:S(2)}, u32[]{:S(2)}) collective-permute-start(bf16[8,400,128]{2,1,0:T(8,128)(2,1)} %get-tuple-element.130), channel_id=1, source_target_pairs={{0,2},{1,3},{8,10},{9,11},{16,18},{17,19},{24,26},{25,27}} | collective-permute-start | bytes 2457608 | tf_op jit(solution)/shard_map/ppermute | solution.py:409
  37.8 36.5 %all-to-all-start = ((bf16[8,128,1280]{2,1,0:T(8,128)(2,1)}), bf16[8,128,1280]{2,1,0:T(8,128)(2,1)S(1)}, u32[]{:S(2)}, u32[]{:S(2)}) async-start(bf16[8,128,1280]{2,1,0:T(8,128)(2,1)} %get-tuple-element.119), calls=%async_computation | async-start | bytes 5242880 | tf_op jit(solution)/shard_map/all_to_all | solution.py:504
  46.1 8.3 %copy-start.16 = (bf16[2,8,160,128]{3,2,1,0:T(8,128)(2,1)}, bf16[2,8,160,128]{3,2,1,0:T(8,128)(2,1)S(1)}, u32[]{:S(2)}) copy-start(bf16[2,8,160,128]{3,2,1,0:T(8,128)(2,1)S(1)} %get-tuple-element.140.refs_0_) | copy-start | bytes 1966084
  47.1 17.3 %collective-permute-start.2 = (bf16[2,8,160,128]{3,2,1,0:T(8,128)(2,1)S(1)}, bf16[2,8,160,128]{3,2,1,0:T(8,128)(2,1)S(1)}, u32[]{:S(2)}, u32[]{:S(2)}) collective-permute-start(bf16[2,8,160,128]{3,2,1,0:T(8,128)(2,1)S(1)} %get-tuple-element.132), channel_id=1, source_target_pairs={{0,2},{1,3},{6,4},{7,5},{8,10},{9,11},{14,12},{15,13},{16,18},{17,... | collective-permute-start | bytes 1966088 | tf_op jit(solution)/shard_map/ppermute | solution.py:409
  50.6 19.1 %collective-permute-start.5 = (bf16[2,8,160,128]{3,2,1,0:T(8,128)(2,1)S(1)}, bf16[2,8,160,128]{3,2,1,0:T(8,128)(2,1)S(1)}, u32[]{:S(2)}, u32[]{:S(2)}) collective-permute-start(bf16[2,8,160,128]{3,2,1,0:T(8,128)(2,1)S(1)} %get-tuple-element.140.refs_0_), channel_id=1, source_target_pairs={{2,4},{3,5},{4,2},{5,3},{10,12},{11,13},{12,10},{13,11},{18,20},{1... | collective-permute-start | bytes 1966088 | tf_op jit(solution)/shard_map/ppermute | solution.py:409
  64.4 21.2 %collective-permute-start.3 = (bf16[8,400,128]{2,1,0:T(8,128)(2,1)}, bf16[8,400,128]{2,1,0:T(8,128)(2,1)}, u32[]{:S(2)}, u32[]{:S(2)}) collective-permute-start(bf16[8,400,128]{2,1,0:T(8,128)(2,1)} %get-tuple-element.134), channel_id=1, source_target_pairs={{0,2},{1,3},{8,10},{9,11},{16,18},{17,19},{24,26},{25,27}} | collective-permute-start | bytes 2457608 | tf_op jit(solution)/shard_map/ppermute | solution.py:409
  70.6 20.6 %collective-permute-start.6 = (bf16[2,8,160,128]{3,2,1,0:T(8,128)(2,1)S(1)}, bf16[2,8,160,128]{3,2,1,0:T(8,128)(2,1)}, u32[]{:S(2)}, u32[]{:S(2)}) collective-permute-start(bf16[2,8,160,128]{3,2,1,0:T(8,128)(2,1)S(1)} %get-tuple-element.142.refs_1_), channel_id=1, source_target_pairs={{2,4},{3,5},{4,2},{5,3},{10,12},{11,13},{12,10},{13,11},{18,20},{1... | collective-permute-start | bytes 1966088 | tf_op jit(solution)/shard_map/ppermute | solution.py:409
  72.1 20.9 %collective-permute-start.9 = (bf16[8,160,128]{2,1,0:T(8,128)(2,1)}, bf16[8,160,128]{2,1,0:T(8,128)(2,1)}, u32[]{:S(2)}, u32[]{:S(2)}) collective-permute-start(bf16[8,160,128]{2,1,0:T(8,128)(2,1)} %get-tuple-element.152), channel_id=1, source_target_pairs={{2,0},{3,1},{4,6},{5,7},{10,8},{11,9},{12,14},{13,15},{18,16},{19,... | collective-permute-start | bytes 983048 | tf_op jit(solution)/shard_map/ppermute | solution.py:409
  85.6 7.3 %copy-start.11 = (bf16[2,8,160,128]{3,2,1,0:T(8,128)(2,1)S(1)}, bf16[2,8,160,128]{3,2,1,0:T(8,128)(2,1)}, u32[]{:S(2)}) copy-start(bf16[2,8,160,128]{3,2,1,0:T(8,128)(2,1)} %copy-done.10) | copy-start | bytes 1966084
  85.6 33.2 %collective-permute-start.4 = (bf16[2,16,160,128]{3,2,1,0:T(8,128)(2,1)}, bf16[2,16,160,128]{3,2,1,0:T(8,128)(2,1)}, u32[]{:S(2)}, u32[]{:S(2)}) collective-permute-start(bf16[2,16,160,128]{3,2,1,0:T(8,128)(2,1)} %get-tuple-element.136), channel_id=1, source_target_pairs={{0,2},{1,3},{6,4},{7,5},{8,10},{9,11},{14,12},{15,13},{16,18},{17,... | collective-permute-start | bytes 3932168 | tf_op jit(solution)/shard_map/ppermute | solution.py:409
  91.2 27.7 %collective-permute-start.7 = (bf16[2,16,160,128]{3,2,1,0:T(8,128)(2,1)}, bf16[2,16,160,128]{3,2,1,0:T(8,128)(2,1)}, u32[]{:S(2)}, u32[]{:S(2)}) collective-permute-start(bf16[2,16,160,128]{3,2,1,0:T(8,128)(2,1)} %get-tuple-element.144.refs_0_), channel_id=1, source_target_pairs={{2,4},{3,5},{4,2},{5,3},{10,12},{11,13},{12,10},{13,11},{18,20},{1... | collective-permute-start | bytes 3932168 | tf_op jit(solution)/shard_map/ppermute | solution.py:409
  94.0 23.5 %collective-permute-start.10 = (bf16[24,160,128]{2,1,0:T(8,128)(2,1)}, bf16[24,160,128]{2,1,0:T(8,128)(2,1)}, u32[]{:S(2)}, u32[]{:S(2)}) collective-permute-start(bf16[24,160,128]{2,1,0:T(8,128)(2,1)} %get-tuple-element.156), channel_id=1, source_target_pairs={{2,0},{3,1},{4,6},{5,7},{10,8},{11,9},{12,14},{13,15},{18,16},{19,... | collective-permute-start | bytes 2949128 | tf_op jit(solution)/shard_map/ppermute | solution.py:409
  103.0 4.4 %copy-start.27 = (bf16[8,80,128]{2,1,0:T(8,128)(2,1)}, bf16[8,80,128]{2,1,0:T(8,128)(2,1)S(1)}, u32[]{:S(2)}) copy-start(bf16[8,80,128]{2,1,0:T(8,128)(2,1)S(1)} %get-tuple-element.217) | copy-start | bytes 491524
  103.0 10.7 %copy-start.25 = (bf16[2,8,80,128]{3,2,1,0:T(8,128)(2,1)}, bf16[2,8,80,128]{3,2,1,0:T(8,128)(2,1)S(1)}, u32[]{:S(2)}) copy-start(bf16[2,8,80,128]{3,2,1,0:T(8,128)(2,1)S(1)} %get-tuple-element.182.refs_1_) | copy-start | bytes 983044
  103.0 15.8 %collective-permute-start.16 = (bf16[8,80,128]{2,1,0:T(8,128)(2,1)S(1)}, bf16[8,80,128]{2,1,0:T(8,128)(2,1)S(1)}, u32[]{:S(2)}, u32[]{:S(2)}) collective-permute-start(bf16[8,80,128]{2,1,0:T(8,128)(2,1)S(1)} %get-tuple-element.183), channel_id=1, source_target_pairs={{0,1},{1,0},{2,3},{3,2},{4,5},{5,4},{6,7},{7,6},{8,9},{9,8},{10,11... | collective-permute-start | bytes 491528 | tf_op jit(solution)/shard_map/ppermute | solution.py:677
  117.5 9.3 %collective-permute-start.11 = (bf16[8,160,128]{2,1,0:T(8,128)(2,1)S(1)}, bf16[8,160,128]{2,1,0:T(8,128)(2,1)S(1)}, u32[]{:S(2)}, u32[]{:S(2)}) collective-permute-start(bf16[8,160,128]{2,1,0:T(8,128)(2,1)S(1)} %get-tuple-element.159), channel_id=1, source_target_pairs={{2,0},{3,1},{4,6},{5,7},{10,8},{11,9},{12,14},{13,15},{18,16},{19,... | collective-permute-start | bytes 983048 | tf_op jit(solution)/shard_map/ppermute | solution.py:409
  118.9 35.2 %collective-permute-start.8 = (bf16[2,16,160,128]{3,2,1,0:T(8,128)(2,1)}, bf16[2,16,160,128]{3,2,1,0:T(8,128)(2,1)S(1)}, u32[]{:S(2)}, u32[]{:S(2)}) collective-permute-start(bf16[2,16,160,128]{3,2,1,0:T(8,128)(2,1)} %get-tuple-element.151.refs_1_), channel_id=1, source_target_pairs={{2,4},{3,5},{4,2},{5,3},{10,12},{11,13},{12,10},{13,11},{18,20},{1... | collective-permute-start | bytes 3932168 | tf_op jit(solution)/shard_map/ppermute | solution.py:409
  119.7 30.0 %collective-permute-start.12 = (bf16[12,400,128]{2,1,0:T(8,128)(2,1)}, bf16[12,400,128]{2,1,0:T(8,128)(2,1)S(1)}, u32[]{:S(2)}, u32[]{:S(2)}) collective-permute-start(bf16[12,400,128]{2,1,0:T(8,128)(2,1)} %get-tuple-element.168), channel_id=1, source_target_pairs={{0,2},{1,3},{8,10},{9,11},{16,18},{17,19},{24,26},{25,27}} | collective-permute-start | bytes 3686408 | tf_op jit(solution)/shard_map/ppermute | solution.py:409
  127.1 36.8 %collective-permute-start.17 = (bf16[40,160,128]{2,1,0:T(8,128)(2,1)S(1)}, bf16[40,160,128]{2,1,0:T(8,128)(2,1)S(1)}, u32[]{:S(2)}, u32[]{:S(2)}) collective-permute-start(bf16[40,160,128]{2,1,0:T(8,128)(2,1)S(1)} %get-tuple-element.184), channel_id=1, source_target_pairs={{2,0},{3,1},{4,6},{5,7},{10,8},{11,9},{12,14},{13,15},{18,16},{19,... | collective-permute-start | bytes 4915208 | tf_op jit(solution)/shard_map/ppermute | solution.py:409
  149.7 29.4 %collective-permute-start.13 = (bf16[2,16,160,128]{3,2,1,0:T(8,128)(2,1)}, bf16[2,16,160,128]{3,2,1,0:T(8,128)(2,1)S(1)}, u32[]{:S(2)}, u32[]{:S(2)}) collective-permute-start(bf16[2,16,160,128]{3,2,1,0:T(8,128)(2,1)} %get-tuple-element.170), channel_id=1, source_target_pairs={{0,2},{1,3},{6,4},{7,5},{8,10},{9,11},{14,12},{15,13},{16,18},{17,... | collective-permute-start | bytes 3932168 | tf_op jit(solution)/shard_map/ppermute | solution.py:409
  154.1 25.0 %collective-permute-start.14 = (bf16[2,16,160,128]{3,2,1,0:T(8,128)(2,1)S(1)}, bf16[2,16,160,128]{3,2,1,0:T(8,128)(2,1)S(1)}, u32[]{:S(2)}, u32[]{:S(2)}) collective-permute-start(bf16[2,16,160,128]{3,2,1,0:T(8,128)(2,1)S(1)} %get-tuple-element.164.refs_0_), channel_id=1, source_target_pairs={{2,4},{3,5},{4,2},{5,3},{10,12},{11,13},{12,10},{13,11},{18,20},{1... | collective-permute-start | bytes 3932168 | tf_op jit(solution)/shard_map/ppermute | solution.py:409
  163.9 6.4 %copy-start = (bf16[40,160,128]{2,1,0:T(8,128)(2,1)}, bf16[40,160,128]{2,1,0:T(8,128)(2,1)S(1)}, u32[]{:S(2)}) copy-start(bf16[40,160,128]{2,1,0:T(8,128)(2,1)S(1)} %get-tuple-element.185.refs_5_.refs_4_) | copy-start | bytes 4915204
  163.9 14.7 %collective-permute-start.18 = (bf16[16,160,128]{2,1,0:T(8,128)(2,1)S(1)}, bf16[16,160,128]{2,1,0:T(8,128)(2,1)S(1)}, u32[]{:S(2)}, u32[]{:S(2)}) collective-permute-start(bf16[16,160,128]{2,1,0:T(8,128)(2,1)S(1)} %get-tuple-element.187), channel_id=1, source_target_pairs={{2,0},{3,1},{4,6},{5,7},{10,8},{11,9},{12,14},{13,15},{18,16},{19,... | collective-permute-start | bytes 1966088 | tf_op jit(solution)/shard_map/ppermute | solution.py:409
  170.3 4.4 %collective-permute-start.19 = (bf16[16,80,128]{2,1,0:T(8,128)(2,1)S(1)}, bf16[16,80,128]{2,1,0:T(8,128)(2,1)S(1)}, u32[]{:S(2)}, u32[]{:S(2)}) collective-permute-start(bf16[16,80,128]{2,1,0:T(8,128)(2,1)S(1)} %get-tuple-element.192), channel_id=1, source_target_pairs={{0,1},{1,0},{2,3},{3,2},{4,5},{5,4},{6,7},{7,6},{8,9},{9,8},{10,11... | collective-permute-start | bytes 983048 | tf_op jit(solution)/shard_map/ppermute | solution.py:677
  180.2 29.4 %collective-permute-start.20 = (bf16[32,160,128]{2,1,0:T(8,128)(2,1)S(1)}, bf16[32,160,128]{2,1,0:T(8,128)(2,1)S(1)}, u32[]{:S(2)}, u32[]{:S(2)}) collective-permute-start(bf16[32,160,128]{2,1,0:T(8,128)(2,1)S(1)} %get-tuple-element.194), channel_id=1, source_target_pairs={{2,0},{3,1},{4,6},{5,7},{10,8},{11,9},{12,14},{13,15},{18,16},{19,... | collective-permute-start | bytes 3932168 | tf_op jit(solution)/shard_map/ppermute | solution.py:409
  181.5 12.6 %copy-start.4 = (bf16[2,16,160,128]{3,2,1,0:T(8,128)(2,1)}, bf16[2,16,160,128]{3,2,1,0:T(8,128)(2,1)S(1)}, u32[]{:S(2)}) copy-start(bf16[2,16,160,128]{3,2,1,0:T(8,128)(2,1)S(1)} %get-tuple-element.179.refs_1_) | copy-start | bytes 3932164
  181.5 28.1 %collective-permute-start.15 = (bf16[2,16,160,128]{3,2,1,0:T(8,128)(2,1)S(1)}, bf16[2,16,160,128]{3,2,1,0:T(8,128)(2,1)S(1)}, u32[]{:S(2)}, u32[]{:S(2)}) collective-permute-start(bf16[2,16,160,128]{3,2,1,0:T(8,128)(2,1)S(1)} %get-tuple-element.179.refs_1_), channel_id=1, source_target_pairs={{2,4},{3,5},{4,2},{5,3},{10,12},{11,13},{12,10},{13,11},{18,20},{1... | collective-permute-start | bytes 3932168 | tf_op jit(solution)/shard_map/ppermute | solution.py:409
  182.3 29.7 %collective-permute-start.22 = (bf16[12,400,128]{2,1,0:T(8,128)(2,1)}, bf16[12,400,128]{2,1,0:T(8,128)(2,1)S(1)}, u32[]{:S(2)}, u32[]{:S(2)}) collective-permute-start(bf16[12,400,128]{2,1,0:T(8,128)(2,1)} %get-tuple-element.200), channel_id=1, source_target_pairs={{0,2},{1,3},{8,10},{9,11},{16,18},{17,19},{24,26},{25,27}} | collective-permute-start | bytes 3686408 | tf_op jit(solution)/shard_map/ppermute | solution.py:409
  209.6 2.4 %copy-start.9 = (bf16[2,16,160,128]{3,2,1,0:T(8,128)(2,1)}, bf16[2,16,160,128]{3,2,1,0:T(8,128)(2,1)S(1)}, u32[]{:S(2)}) copy-start(bf16[2,16,160,128]{3,2,1,0:T(8,128)(2,1)S(1)} %get-tuple-element.190.refs_3_) | copy-start | bytes 3932164
  210.7 13.7 %collective-permute-start.21 = (bf16[16,160,128]{2,1,0:T(8,128)(2,1)S(1)}, bf16[16,160,128]{2,1,0:T(8,128)(2,1)S(1)}, u32[]{:S(2)}, u32[]{:S(2)}) collective-permute-start(bf16[16,160,128]{2,1,0:T(8,128)(2,1)S(1)} %get-tuple-element.197), channel_id=1, source_target_pairs={{2,0},{3,1},{4,6},{5,7},{10,8},{11,9},{12,14},{13,15},{18,16},{19,... | collective-permute-start | bytes 1966088 | tf_op jit(solution)/shard_map/ppermute | solution.py:409
  218.2 1.6 collective-permute-start.23
  218.3 7.4 %copy-start.28 = (bf16[8,80,128]{2,1,0:T(8,128)(2,1)S(1)}, bf16[8,80,128]{2,1,0:T(8,128)(2,1)}, u32[]{:S(2)}) copy-start(bf16[8,80,128]{2,1,0:T(8,128)(2,1)} %copy-done.27) | copy-start | bytes 491524
  218.3 8.5 %copy-start.5 = (bf16[2,16,160,128]{3,2,1,0:T(8,128)(2,1)S(1)}, bf16[2,16,160,128]{3,2,1,0:T(8,128)(2,1)}, u32[]{:S(2)}) copy-start(bf16[2,16,160,128]{3,2,1,0:T(8,128)(2,1)} %copy-done.4) | copy-start | bytes 3932164
  218.3 8.5 %copy-start.8 = (bf16[2,16,160,128]{3,2,1,0:T(8,128)(2,1)S(1)}, bf16[2,16,160,128]{3,2,1,0:T(8,128)(2,1)}, u32[]{:S(2)}) copy-start(bf16[2,16,160,128]{3,2,1,0:T(8,128)(2,1)} %copy-done.7) | copy-start | bytes 3932164
  224.4 14.6 %collective-permute-start.24 = (bf16[16,160,128]{2,1,0:T(8,128)(2,1)S(1)}, bf16[16,160,128]{2,1,0:T(8,128)(2,1)S(1)}, u32[]{:S(2)}, u32[]{:S(2)}) collective-permute-start(bf16[16,160,128]{2,1,0:T(8,128)(2,1)S(1)} %get-tuple-element.208), channel_id=1, source_target_pairs={{2,0},{3,1},{10,8},{11,9},{18,16},{19,17},{26,24},{27,25}} | collective-permute-start | bytes 1966088 | tf_op jit(solution)/shard_map/ppermute | solution.py:409
  225.7 5.8 %collective-permute-start.30 = (bf16[8,80,128]{2,1,0:T(8,128)(2,1)S(1)}, bf16[8,80,128]{2,1,0:T(8,128)(2,1)S(1)}, u32[]{:S(2)}, u32[]{:S(2)}) collective-permute-start(bf16[8,80,128]{2,1,0:T(8,128)(2,1)S(1)} %copy-done.28), channel_id=1, source_target_pairs={{0,1},{1,0},{2,3},{3,2},{4,5},{5,4},{6,7},{7,6},{8,9},{9,8},{10,11... | collective-permute-start | bytes 491528 | tf_op jit(solution)/shard_map/ppermute | solution.py:676
  225.8 5.8 %collective-permute-start.29 = (bf16[8,80,128]{2,1,0:T(8,128)(2,1)}, bf16[8,80,128]{2,1,0:T(8,128)(2,1)S(1)}, u32[]{:S(2)}, u32[]{:S(2)}) collective-permute-start(bf16[8,80,128]{2,1,0:T(8,128)(2,1)} %get-tuple-element.216), channel_id=1, source_target_pairs={{0,1},{1,0},{2,3},{3,2},{4,5},{5,4},{6,7},{7,6},{8,9},{9,8},{10,11... | collective-permute-start | bytes 491528 | tf_op jit(solution)/shard_map/ppermute | solution.py:694
  226.3 7.3 %collective-permute-start.28 = (bf16[16,80,128]{2,1,0:T(8,128)(2,1)S(1)}, bf16[16,80,128]{2,1,0:T(8,128)(2,1)S(1)}, u32[]{:S(2)}, u32[]{:S(2)}) collective-permute-start(bf16[16,80,128]{2,1,0:T(8,128)(2,1)S(1)} %get-tuple-element.214), channel_id=1, source_target_pairs={{0,1},{1,0},{2,3},{3,2},{4,5},{5,4},{6,7},{7,6},{8,9},{9,8},{10,11... | collective-permute-start | bytes 983048 | tf_op jit(solution)/shard_map/ppermute | solution.py:676
  226.4 7.2 %collective-permute-start.27 = (bf16[16,80,128]{2,1,0:T(8,128)(2,1)S(1)}, bf16[16,80,128]{2,1,0:T(8,128)(2,1)S(1)}, u32[]{:S(2)}, u32[]{:S(2)}) collective-permute-start(bf16[16,80,128]{2,1,0:T(8,128)(2,1)S(1)} %get-tuple-element.213), channel_id=1, source_target_pairs={{0,1},{1,0},{2,3},{3,2},{4,5},{5,4},{6,7},{7,6},{8,9},{9,8},{10,11... | collective-permute-start | bytes 983048 | tf_op jit(solution)/shard_map/ppermute | solution.py:694
  226.8 5.2 %copy-start.1 = (bf16[40,160,128]{2,1,0:T(8,128)(2,1)S(1)}, bf16[40,160,128]{2,1,0:T(8,128)(2,1)}, u32[]{:S(2)}) copy-start(bf16[40,160,128]{2,1,0:T(8,128)(2,1)} %copy-done) | copy-start | bytes 4915204
  226.8 5.2 %copy-start.26 = (bf16[2,8,80,128]{3,2,1,0:T(8,128)(2,1)S(1)}, bf16[2,8,80,128]{3,2,1,0:T(8,128)(2,1)}, u32[]{:S(2)}) copy-start(bf16[2,8,80,128]{3,2,1,0:T(8,128)(2,1)} %copy-done.25) | copy-start | bytes 983044
  231.5 7.5 %collective-permute-start.26 = (bf16[16,80,128]{2,1,0:T(8,128)(2,1)S(1)}, bf16[16,80,128]{2,1,0:T(8,128)(2,1)S(1)}, u32[]{:S(2)}, u32[]{:S(2)}) collective-permute-start(bf16[16,80,128]{2,1,0:T(8,128)(2,1)S(1)} %get-tuple-element.211), channel_id=1, source_target_pairs={{0,1},{1,0},{2,3},{3,2},{4,5},{5,4},{6,7},{7,6},{8,9},{9,8},{10,11... | collective-permute-start | bytes 983048 | tf_op jit(solution)/shard_map/ppermute | solution.py:676
  231.6 7.5 %collective-permute-start.25 = (bf16[16,80,128]{2,1,0:T(8,128)(2,1)S(1)}, bf16[16,80,128]{2,1,0:T(8,128)(2,1)S(1)}, u32[]{:S(2)}, u32[]{:S(2)}) collective-permute-start(bf16[16,80,128]{2,1,0:T(8,128)(2,1)S(1)} %get-tuple-element.210), channel_id=1, source_target_pairs={{0,1},{1,0},{2,3},{3,2},{4,5},{5,4},{6,7},{7,6},{8,9},{9,8},{10,11... | collective-permute-start | bytes 983048 | tf_op jit(solution)/shard_map/ppermute | solution.py:694
  232.0 1.5 copy-start.3
  (14 other events, 15.7 us)
